TPU v7x, 512 devices: a whole 4x4x16 slice. The times are simulated.
512 devices in a mesh: row: 2 (over core), nbr: 16 (over z_lo, y), feat: 16 (over x, z_hi).
Axes of the slice: x: 4, y: 4, z: 16 (z_hi: 4, z_lo: 4; z = z_hi * 4 + z_lo), core: 2. Of those that a mesh axis runs over, the one named last changes fastest.
Arguments:
- features: float32 [1024, 32768], P('feat', 'nbr'), may hold values from -6 to 6
- tile_list: int32 [2, 16, 2, 256], P('row', 'nbr'), may hold values from 0 to 15, as said below
- tile_count: int32 [2, 16], P('row', 'nbr'), may hold values from 96 to 256
- weight: float32 [1024, 1024], P(('row', 'nbr'), 'feat'), may hold values from -0.1875 to 0.1875
- cotangent: float32 [4096, 1024], P(('row', 'nbr'), 'feat'), may hold values from -6 to 6
Outputs:
- activations: float32 [4096, 1024], P(('row', 'nbr'), 'feat')
- feature_grad: float32 [1024, 32768], P('feat', 'nbr')
- weight_grad: float32 [1024, 1024], P(('row', 'nbr'), 'feat')
Inputs may be any that keep to these rules, and one draw needn't show every extreme that they name: `tile_list`: each device's list names every (row block, column block) pair of its block exactly once; only the first tile_count entries are used.
All inputs are finite; a program needn't handle non-finite values.
Results may differ from a plain program's by a relative error of at most 0.0003.
Values sent between devices are 32-bit elements; how exact they have to be, the bound alone decides.
No kernel may reach another device: no remote copies, remote signals or barrier semaphores. Data moves between devices by JAX's collectives and lax.ppermute only.
A program may use at most 64 MiB of HBM per device.

v0:
```python
import jax
import jax.numpy as jnp
from jax import lax
from jax.sharding import PartitionSpec as P

TILE = 128


modulus = 32749
highest = lax.Precision.HIGHEST
tile_batch = 32


def edge_value(row_index, col_index):
    hashed = (
        row_index * row_index % modulus * 3
        + col_index * col_index % modulus * 5
        + row_index * col_index % modulus * 7
        + row_index * 11
        + col_index * 13
    ) % modulus
    return hashed.astype(jnp.float32) / modulus - 0.5


def edge_tiles(row_picks, col_picks, row_base, col_base, tile, edge_scale):
    offsets = jnp.arange(tile, dtype=jnp.int32)
    rows_global = row_base + row_picks[:, None, None] * tile + offsets[None, :, None]
    cols_global = col_base + col_picks[:, None, None] * tile + offsets[None, None, :]
    return edge_value(rows_global, cols_global) * edge_scale


def tile_product(
    pairs, first_slot, end_slot, row_base, col_base, source, target_blocks, transpose, edge_scale
):
    tile = source.shape[1]
    width = source.shape[2]
    slots = pairs.shape[1]
    turns = jnp.maximum(end_slot - first_slot + tile_batch - 1, 0) // tile_batch

    def advance(block_turn, running):
        positions = first_slot + block_turn * tile_batch + jnp.arange(tile_batch, dtype=jnp.int32)
        in_range = positions < end_slot
        positions = jnp.minimum(positions, slots - 1)
        row_picks = pairs[0][positions]
        col_picks = pairs[1][positions]
        values = edge_tiles(row_picks, col_picks, row_base, col_base, tile, edge_scale)
        values = jnp.where(in_range[:, None, None], values, 0.0)
        if transpose:
            product = jnp.einsum("tab,taf->tbf", values, source[row_picks], precision=highest)
            target_picks = col_picks
        else:
            product = jnp.einsum("tab,tbf->taf", values, source[col_picks], precision=highest)
            target_picks = row_picks
        placing = (
            target_picks[None, :] == jnp.arange(target_blocks, dtype=jnp.int32)[:, None]
        ).astype(jnp.float32)
        return running + jnp.dot(
            placing, product.reshape(tile_batch, tile * width), precision=highest
        )

    running = lax.fori_loop(
        0, turns, advance, jnp.zeros((target_blocks, tile * width), jnp.float32)
    )
    return running.reshape(target_blocks * tile, width)


def per_device(features, tile_list, tile_count, weight, cotangent):
    pairs = tile_list[0, 0]
    tile_total = tile_count[0, 0]
    n_nbr = lax.axis_size("nbr")
    row_id = lax.axis_index("row")
    nbr_id = lax.axis_index("nbr")
    width = features.shape[0]
    c_dev = features.shape[1]
    r_dev = cotangent.shape[0] * n_nbr
    edge_scale = (12.0 / (c_dev * n_nbr / 2)) ** 0.5
    col_base = nbr_id * c_dev
    source = features.T.reshape(c_dev // TILE, TILE, width)
    row_blocks = r_dev // TILE
    partial_value = tile_product(
        pairs, 0, tile_total, row_id * r_dev, col_base, source, row_blocks, False, edge_scale
    )
    hidden = lax.psum_scatter(partial_value, "nbr", scatter_dimension=0, tiled=True)
    weight_cols = lax.all_gather(weight, ("row", "nbr"), axis=0, tiled=True)
    hidden_all = lax.all_gather(hidden, "feat", axis=1, tiled=True)
    pre_act = jnp.dot(hidden_all, weight_cols, precision=highest)
    squash = jax.nn.sigmoid(pre_act)
    activations = pre_act * squash
    grad_pre = cotangent * squash * (1.0 + pre_act * (1.0 - squash))
    grad_hidden = lax.psum_scatter(
        jnp.dot(grad_pre, weight_cols.T, precision=highest), "feat", scatter_dimension=1, tiled=True
    )
    weight_terms = jnp.dot(hidden_all.T, grad_pre, precision=highest)
    weight_grad = lax.psum_scatter(weight_terms, ("row", "nbr"), scatter_dimension=0, tiled=True)
    grad_block = lax.all_gather(grad_hidden, "nbr", axis=0, tiled=True)
    column_part = tile_product(
        pairs,
        0,
        tile_total,
        row_id * r_dev,
        col_base,
        grad_block.reshape(row_blocks, TILE, width),
        c_dev // TILE,
        True,
        edge_scale,
    )
    feature_grad = lax.psum(column_part.T, "row")
    return (activations, feature_grad, weight_grad)


def solution(mesh):
    in_specs = (
        P("feat", "nbr"),
        P("row", "nbr", None, None),
        P("row", "nbr"),
        P(("row", "nbr"), "feat"),
        P(("row", "nbr"), "feat"),
    )
    out_specs = (P(("row", "nbr"), "feat"), P("feat", "nbr"), P(("row", "nbr"), "feat"))
    return jax.shard_map(
        per_device, mesh=mesh, in_specs=in_specs, out_specs=out_specs, check_vma=False
    )
```

profile of v0, /device:TPU:1, one launch (start us, length us, event | category | flops | bytes accessed | tf_op | source)
XLA Modules:
  0.0 759.8 jit_solution(294618756036174718)
XLA Ops:
  10.1 43.2 %while.24 = (s32[]{:T(128)}, f32[16,8192]{1,0:T(8,128)}, s32[]{:T(128)}, s32[2,256]{1,0:T(2,128)S(1)}, s32[]{:T(128)}, /*index=5*/s32[]{:T(128)}, s32[]{:T(128)}, f32[16,128,64]{2,1,0:T(8,128)S(1)}, s32[]{:T(128)}, s32[]{:T(128)}) while((s32[]{:T(128)}, f32[16,8192]{1,0:T(8,128)}, s32[]{:T(128)}, s32[2,256]{1,0:T(2,128)S(1)}, s32[]{:T(128)}, ...), condition=%wide.region_1.2_spmd, body=%wide.region_0.1_spmd.sunk | while | flops 465259456 | bytes 12794501 | solution.py:61
  13.1 7.8 %fusion.133 = f32[32,128,64]{2,1,0:T(8,128)} fusion(f32[32,128,64]{2,1,0:T(8,128)S(1)} %gather_fusion.1, s32[32,128]{1,0:T(8,128)S(1)} %get-tuple-element.416, s32[32,128]{1,0:T(8,128)S(1)} %get-tuple-element.418, s32[32,128]{1,0:T(8,128)S(1)} %get-tuple-element.419, s32[32,128]{1,0:T(8,128)S(1)} %get-tuple-element.420, ...), kind=kOutput, calls=%fused_computation.19.clone.1 | convolution fusion | flops 414711808 | bytes 2195488 | tf_op jit(solution)/shard_map/while/body/tab,tbf->taf/dot_general | solution.py:52
  20.9 2.2 reshape.524
  27.5 7.8 %fusion.133 = f32[32,128,64]{2,1,0:T(8,128)} fusion(f32[32,128,64]{2,1,0:T(8,128)S(1)} %gather_fusion.1, s32[32,128]{1,0:T(8,128)S(1)} %get-tuple-element.416, s32[32,128]{1,0:T(8,128)S(1)} %get-tuple-element.418, s32[32,128]{1,0:T(8,128)S(1)} %get-tuple-element.419, s32[32,128]{1,0:T(8,128)S(1)} %get-tuple-element.420, ...), kind=kOutput, calls=%fused_computation.19.clone.1 | convolution fusion | flops 414711808 | bytes 2195488 | tf_op jit(solution)/shard_map/while/body/tab,tbf->taf/dot_general | solution.py:52
  35.3 2.2 reshape.524
  41.9 7.8 %fusion.133 = f32[32,128,64]{2,1,0:T(8,128)} fusion(f32[32,128,64]{2,1,0:T(8,128)S(1)} %gather_fusion.1, s32[32,128]{1,0:T(8,128)S(1)} %get-tuple-element.416, s32[32,128]{1,0:T(8,128)S(1)} %get-tuple-element.418, s32[32,128]{1,0:T(8,128)S(1)} %get-tuple-element.419, s32[32,128]{1,0:T(8,128)S(1)} %get-tuple-element.420, ...), kind=kOutput, calls=%fused_computation.19.clone.1 | convolution fusion | flops 414711808 | bytes 2195488 | tf_op jit(solution)/shard_map/while/body/tab,tbf->taf/dot_general | solution.py:52
  49.7 2.2 reshape.524
  53.3 2.5 reshape.453
  55.9 138.9 %all_gather.10 = f32[1024,64]{1,0:T(8,128)S(1)} all-gather(f32[32,64]{1,0:T(8,128)S(1)} %copy-done.8), channel_id=1, replica_groups=mesh['row'=2,'nbr'=16,'feat'=16] {'row','nbr'}, dimensions={0}, use_global_device_ids=true | all-gather | bytes 270336 | tf_op jit(solution)/shard_map/all_gather | solution.py:84
  194.8 17.9 %reduce-scatter.4.cloned.1.call-done = f32[128,64]{1,0:T(8,128)} async-done(((f32[2048,64]{1,0:T(8,128)}), f32[128,64]{1,0:T(8,128)}) %reduce-scatter.4.cloned.1.call-update) | async-done | bytes 32784 | tf_op jit(solution)/shard_map/reduce_scatter | solution.py:83
  213.5 49.4 %all_gather.9 = f32[128,1024]{0,1:T(8,128)S(1)} all-gather(f32[128,64]{0,1:T(8,128)S(1)} %copy.24), channel_id=1, replica_groups=mesh['row'=2,'nbr'=16,'feat'=16] {'feat'}, dimensions={1}, use_global_device_ids=true | all-gather | bytes 557056 | tf_op jit(solution)/shard_map/all_gather | solution.py:85
  266.8 119.0 %reduce-scatter.6.cloned.1.call-done = f32[128,64]{0,1:T(8,128)} async-done(((f32[128,1024]{0,1:T(8,128)}), f32[128,64]{0,1:T(8,128)}) %reduce-scatter.6.cloned.1.call-update) | async-done | bytes 32784 | tf_op jit(solution)/shard_map/reduce_scatter | solution.py:90
  385.8 35.9 %all_gather.11 = f32[2048,64]{0,1:T(8,128)S(1)} all-gather(f32[128,64]{0,1:T(8,128)} %reduce-scatter.6.cloned.1.call-done), channel_id=1, replica_groups=mesh['row'=2,'nbr'=16,'feat'=16] {'nbr'}, dimensions={0}, use_global_device_ids=true | all-gather | bytes 557056 | tf_op jit(solution)/shard_map/all_gather | solution.py:95
  422.9 47.5 %while.25 = (s32[]{:T(128)}, f32[16,8192]{1,0:T(8,128)}, s32[]{:T(128)}, s32[2,256]{1,0:T(2,128)S(1)}, s32[]{:T(128)}, /*index=5*/s32[]{:T(128)}, s32[]{:T(128)}, f32[16,128,64]{2,1,0:T(8,128)S(1)}, s32[]{:T(128)}, s32[]{:T(128)}) while((s32[]{:T(128)}, f32[16,8192]{1,0:T(8,128)}, s32[]{:T(128)}, s32[2,256]{1,0:T(2,128)S(1)}, s32[]{:T(128)}, ...), condition=%wide.region_5.6_spmd, body=%wide.region_4.5_spmd.sunk | while | flops 465259456 | bytes 12794501 | solution.py:61
  425.9 9.2 %fusion.142 = f32[32,128,64]{2,1,0:T(8,128)} fusion(f32[32,128,64]{2,1,0:T(8,128)S(1)} %gather_fusion.4, s32[32,128]{1,0:T(8,128)S(1)} %get-tuple-element.434, s32[32,128]{1,0:T(8,128)S(1)} %get-tuple-element.436, s32[32,128]{1,0:T(8,128)S(1)} %get-tuple-element.437, s32[32,128]{1,0:T(8,128)S(1)} %get-tuple-element.438, ...), kind=kOutput, calls=%fused_computation.82.clone.1 | convolution fusion | flops 414711808 | bytes 2195488 | tf_op jit(solution)/shard_map/while/body/tab,taf->tbf/dot_general | solution.py:49
  435.1 2.2 reshape.531
  441.7 9.2 %fusion.142 = f32[32,128,64]{2,1,0:T(8,128)} fusion(f32[32,128,64]{2,1,0:T(8,128)S(1)} %gather_fusion.4, s32[32,128]{1,0:T(8,128)S(1)} %get-tuple-element.434, s32[32,128]{1,0:T(8,128)S(1)} %get-tuple-element.436, s32[32,128]{1,0:T(8,128)S(1)} %get-tuple-element.437, s32[32,128]{1,0:T(8,128)S(1)} %get-tuple-element.438, ...), kind=kOutput, calls=%fused_computation.82.clone.1 | convolution fusion | flops 414711808 | bytes 2195488 | tf_op jit(solution)/shard_map/while/body/tab,taf->tbf/dot_general | solution.py:49
  450.9 2.2 reshape.531
  457.6 9.2 %fusion.142 = f32[32,128,64]{2,1,0:T(8,128)} fusion(f32[32,128,64]{2,1,0:T(8,128)S(1)} %gather_fusion.4, s32[32,128]{1,0:T(8,128)S(1)} %get-tuple-element.434, s32[32,128]{1,0:T(8,128)S(1)} %get-tuple-element.436, s32[32,128]{1,0:T(8,128)S(1)} %get-tuple-element.437, s32[32,128]{1,0:T(8,128)S(1)} %get-tuple-element.438, ...), kind=kOutput, calls=%fused_computation.82.clone.1 | convolution fusion | flops 414711808 | bytes 2195488 | tf_op jit(solution)/shard_map/while/body/tab,taf->tbf/dot_general | solution.py:49
  466.8 2.2 reshape.531
  470.4 2.5 reshape.455
  474.4 122.3 %all-reduce.2.cloned.1.call-done = f32[64,2048]{0,1:T(8,128)} async-done(((f32[64,2048]{0,1:T(8,128)}), f32[64,2048]{0,1:T(8,128)}) %all-reduce.2.cloned.1.call-update) | async-done | bytes 524304 | tf_op jit(solution)/shard_map/psum | solution.py:107
  596.7 2.3 copy.26
  599.0 154.2 %reduce-scatter.8.cloned.1.call-done = f32[32,64]{1,0:T(8,128)} async-done(((f32[1024,64]{1,0:T(8,128)}), f32[32,64]{1,0:T(8,128)}) %reduce-scatter.8.cloned.1.call-update) | async-done | bytes 8208 | tf_op jit(solution)/shard_map/reduce_scatter | solution.py:94
  (128 shorter events, 36.0 us)
Async XLA Ops:
  7.2 2.9 copy-start.6
  7.2 205.5 %reduce-scatter.4.cloned.1.call-start = ((), (), s32[]{:S(2)}) async-start(), calls=%async_computation.3 | async-start | bytes 1114112 | tf_op jit(solution)/shard_map/reduce_scatter | solution.py:83
  20.9 2.2 copy-start.2
  23.7 0.8 copy-start.3
  35.3 2.2 copy-start.2
  38.1 0.8 copy-start.3
  49.7 2.2 copy-start.2
  52.5 0.8 copy-start.3
  53.3 2.6 copy-start.8
  53.3 212.0 %copy-start.7 = (f32[128,64]{0,1:T(8,128)S(1)}, f32[128,64]{0,1:T(8,128)}, u32[]{:S(2)}) copy-start(f32[128,64]{0,1:T(8,128)} %param.13) | copy-start | bytes 98308
  55.8 330.0 %reduce-scatter.6.cloned.1.call-start = ((), (), s32[]{:S(2)}) async-start(), calls=%async_computation.4 | async-start | bytes 557056 | tf_op jit(solution)/shard_map/reduce_scatter | solution.py:90
  262.9 0.8 copy-start.4
  266.8 329.9 %all-reduce.2.cloned.1.call-start = ((), (), s32[]{:S(2)}) async-start(), calls=%async_computation.5 | async-start | bytes 2097152 | tf_op jit(solution)/shard_map/psum | solution.py:107
  435.1 2.2 copy-start
  437.9 0.8 copy-start.1
  450.9 2.2 copy-start
  453.8 0.8 copy-start.1
  466.8 2.2 copy-start
  469.6 0.8 copy-start.1
  470.4 2.6 copy-start.5
  472.9 280.3 %reduce-scatter.8.cloned.1.call-start = ((), (), s32[]{:S(2)}) async-start(), calls=%async_computation.6 | async-start | bytes 540672 | tf_op jit(solution)/shard_map/reduce_scatter | solution.py:94
Sparse Core Ops, SparseCore 0:
  56.0 156.6 reduce-scatter.3
  266.9 118.9 reduce-scatter.5
  473.0 123.6 all-reduce.1
  600.1 153.0 reduce-scatter.7
where the time goes:
time: 761 us; the launch traced here: 760 us
  waiting for transfers between devices  413 us (54%)
  blocking collectives  224 us (29%)
  matrix products  59 us (8%)
  local copies, waits for them, and re-layouts  42.9 us (6%)
  between operations  14.5 us (2%)
    reduce_scatter x1, waiting for transfers between devices, per_device(): lax.psum_scatter(weight_terms, ('row', 'nbr'), scatter_dimension=0, tiled...  154 us
    all_gather x1, blocking collectives, per_device(): weight_cols = lax.all_gather(weight, ('row', 'nbr'), axis=0, tiled=True)  139 us
    psum x1, waiting for transfers between devices, per_device(): feature_grad = lax.psum(column_part.T, 'row')  122 us
    reduce_scatter x1, waiting for transfers between devices, per_device(): lax.psum_scatter(jnp.dot(grad_pre, weight_cols.T, precision=highest), 'fe...  119 us
    all_gather x1, blocking collectives, per_device(): hidden_all = lax.all_gather(hidden, 'feat', axis=1, tiled=True)  49.4 us
    all_gather x1, blocking collectives, per_device(): grad_block = lax.all_gather(grad_hidden, 'nbr', axis=0, tiled=True)  35.9 us
    dot_general x3, matrix products, advance(): jnp.einsum('tab,taf->tbf', values, source[row_picks], precision=highest)  27.6 us
    dot_general x3, matrix products, advance(): jnp.einsum('tab,tbf->taf', values, source[col_picks], precision=highest)  23.3 us
  transfers between devices with their start and end apart: 4, of which 4 were waited for; matrix products, arithmetic and copies ran while one was open for 0% of the time, Pallas kernels for 0%

commit v1 on v0

v1 whole, which is shorter than its diff:
```python
import functools

import jax
import jax.numpy as jnp
from jax import lax
from jax.experimental import pallas as pl
from jax.experimental.pallas import tpu as pltpu
from jax.sharding import Mesh
from jax.sharding import PartitionSpec as P

TILE = 128
MODULUS = 32749
INVERSE = 1.0 / MODULUS
HALF_STEP = 0.5 / MODULUS
highest = lax.Precision.HIGHEST
f32, bf16, i32 = jnp.float32, jnp.bfloat16, jnp.int32


def residue(value):
    quotient = jnp.floor(value.astype(f32) * INVERSE).astype(i32)
    rest = value - quotient * MODULUS
    rest = jnp.where(rest < 0, rest + MODULUS, rest)
    return jnp.where(rest >= MODULUS, rest - MODULUS, rest)


def split(value):
    high = value.astype(bf16)
    return high, (value - high.astype(f32)).astype(bf16)


def product_kernel(
    lane_blocks, sub_blocks, swap, sub_poly, lane_poly, scale,
    base_ref, count_ref, pairs_ref, source_ref, out_ref,
    sub_table, step_table, lane_table, mask_table, source_parts,
):
    sub_base, lane_base = base_ref[0], base_ref[1]
    width = source_parts.shape[0] // 2
    n_sub = sub_blocks * TILE
    slots = pairs_ref.shape[1]
    major, minor = (pairs_ref[1:2, :], pairs_ref[0:1, :]) if swap else (pairs_ref[0:1, :], pairs_ref[1:2, :])
    code = major * sub_blocks + minor
    code = jnp.where(lax.broadcasted_iota(i32, (1, slots), 1) < count_ref[0], code, -1)
    tiles = lane_blocks * sub_blocks
    listed = (lax.broadcasted_iota(i32, (tiles, slots), 0) == code).astype(f32)
    mask_table[...] = jnp.broadcast_to(jnp.sum(listed, axis=1, keepdims=True), (tiles, TILE))

    sub = sub_base + lax.broadcasted_iota(i32, (n_sub, TILE), 0)
    sub_table[...] = residue(sub * residue(sub_poly[0] * sub + sub_poly[1])).astype(f32) * INVERSE
    for l in range(sub_blocks):
        columns = slice(l * TILE, (l + 1) * TILE)
        piece = source_ref[l] if len(source_ref.shape) == 3 else source_ref[:, columns]
        high, low = split(piece)
        source_parts[:width, columns] = high
        source_parts[width:, columns] = low

    def block(j, carry):
        first_lane = lane_base + j * TILE
        lane = first_lane + lax.broadcasted_iota(i32, (TILE, TILE), 1)
        k = lax.broadcasted_iota(i32, (TILE, TILE), 0)
        step_table[...] = residue(7 * k * lane).astype(f32) * INVERSE
        lane = first_lane + lax.broadcasted_iota(i32, (sub_blocks, TILE), 1)
        first = sub_base + TILE * lax.broadcasted_iota(i32, (sub_blocks, TILE), 0)
        inner = residue(lane_poly[0] * lane + lane_poly[1] + 7 * first)
        lane_table[...] = residue(lane * inner).astype(f32) * INVERSE - 0.5
        total = jnp.zeros((2 * width, 2 * TILE), f32)
        for l in range(0, sub_blocks, 2):
            halves = []
            for at in (l, l + 1):
                turn = sub_table[at * TILE:(at + 1) * TILE, :] + step_table[...] + lane_table[at:at + 1, :]
                edge = turn - jnp.floor(turn + (0.5 + HALF_STEP))
                edge = edge * mask_table[pl.ds(j * sub_blocks + at, 1), :]
                halves.append(jnp.concatenate(split(edge), axis=1))
            total += jnp.dot(
                source_parts[:, l * TILE:(l + 2) * TILE], jnp.concatenate(halves, axis=0),
                preferred_element_type=f32,
            )
        total = total[:, :TILE] + total[:, TILE:]
        result = (total[:width] + total[width:]) * scale
        if len(out_ref.shape) == 3:
            out_ref[j] = result
        else:
            out_ref[:, pl.ds(pl.multiple_of(j * TILE, TILE), TILE)] = result
        return carry

    lax.fori_loop(0, lane_blocks, block, 0)


def edge_product(base, count, pairs, source, lane_blocks, sub_blocks, swap, sub_poly, lane_poly, scale, stacked):
    width = source.shape[1] if source.ndim == 3 else source.shape[0]
    shape = (lane_blocks, width, TILE) if stacked else (width, lane_blocks * TILE)
    tiles = lane_blocks * sub_blocks
    return pl.pallas_call(
        functools.partial(product_kernel, lane_blocks, sub_blocks, swap, sub_poly, lane_poly, scale),
        out_shape=jax.ShapeDtypeStruct(shape, f32),
        in_specs=[
            pl.BlockSpec(memory_space=pltpu.SMEM),
            pl.BlockSpec(memory_space=pltpu.SMEM),
            pl.BlockSpec(memory_space=pltpu.VMEM),
            pl.BlockSpec(memory_space=pltpu.VMEM),
        ],
        out_specs=pl.BlockSpec(memory_space=pltpu.VMEM),
        scratch_shapes=[
            pltpu.VMEM((sub_blocks * TILE, TILE), f32),
            pltpu.VMEM((TILE, TILE), f32),
            pltpu.VMEM((sub_blocks, TILE), f32),
            pltpu.VMEM((tiles, TILE), f32),
            pltpu.VMEM((2 * width, sub_blocks * TILE), bf16),
        ],
        compiler_params=pltpu.CompilerParams(vmem_limit_bytes=24 << 20),
        cost_estimate=pl.CostEstimate(flops=8 << 30, bytes_accessed=1 << 21, transcendentals=0),
    )(base, count, pairs, source)


def dot(a, b, dims=((1,), (0,))):
    return lax.dot_general(a, b, (dims, ((), ())), precision=highest, preferred_element_type=f32)


def layer_kernel(
    n_x, n_zh, at_ref, hidden_ref, own_ref, other_ref, cot_ref,
    act_ref, grad_ref, own_terms_ref, other_terms_ref, weight,
):
    core, zh = at_ref[0], at_ref[1]
    half = own_ref.shape[0]
    rows, width = own_ref.shape[2], own_ref.shape[3]
    weight[pl.ds(core * half, half)] = own_ref[...]
    weight[pl.ds((1 - core) * half, half)] = other_ref[...]
    hidden = hidden_ref[...].T
    depth = hidden.shape[1]
    grads = []
    for z in range(n_zh):
        columns = weight[:, z].reshape(depth, width)
        pre = dot(hidden, columns)
        squash = 1.0 / (1.0 + jnp.exp(-pre))
        grad_pre = cot_ref[z] * squash * (1.0 + pre * (1.0 - squash))
        grads.append(grad_pre)

        @pl.when(zh == z)
        def _():
            act_ref[...] = pre * squash
            own = hidden_ref[pl.ds(pl.multiple_of(core * (depth // 2), 8), depth // 2), :]
            other = hidden_ref[pl.ds(pl.multiple_of((1 - core) * (depth // 2), 8), depth // 2), :]
            own_terms_ref[...] = dot(own, grad_pre).reshape(own_terms_ref.shape)
            other_terms_ref[...] = dot(other, grad_pre).reshape(other_terms_ref.shape)

    per_block = width // rows
    for x in range(n_x):
        total = None
        for z in range(n_zh):
            picked = weight[pl.ds((x * n_zh + zh) * per_block, per_block), z].reshape(width, width)
            term = dot(picked, grads[z], ((1,), (1,)))
            total = term if total is None else total + term
        grad_ref[x] = total


def layer(at, hidden_all, own, other, cot, n_x, n_zh):
    half, _, rows, width = own.shape
    n_rows = hidden_all.shape[1]
    terms = jax.ShapeDtypeStruct((half, rows, width), f32)
    vmem = pl.BlockSpec(memory_space=pltpu.VMEM)
    return pl.pallas_call(
        functools.partial(layer_kernel, n_x, n_zh),
        out_shape=(
            jax.ShapeDtypeStruct((n_rows, width), f32),
            jax.ShapeDtypeStruct((n_x, width, n_rows), f32),
            terms, terms,
        ),
        in_specs=[pl.BlockSpec(memory_space=pltpu.SMEM), vmem, vmem, vmem, vmem],
        out_specs=(vmem, vmem, vmem, vmem),
        scratch_shapes=[pltpu.VMEM((2 * half, n_zh, rows, width), f32)],
        compiler_params=pltpu.CompilerParams(vmem_limit_bytes=32 << 20),
        cost_estimate=pl.CostEstimate(flops=1 << 30, bytes_accessed=1 << 21, transcendentals=0),
    )(at, hidden_all, own, other, cot)


def spread(value, axes, n):
    return lax.all_to_all(jnp.broadcast_to(value[None], (n,) + value.shape), axes, 0, 0)


def per_device(features, tile_list, tile_count, weight, cotangent):
    nbr, feat = ("zl", "y"), ("x", "zh")
    pairs, count = tile_list[0, 0], tile_count[0]
    n_nbr = lax.axis_size(nbr)
    n_x, n_zh = lax.axis_size("x"), lax.axis_size("zh")
    core, nbr_id = lax.axis_index("core"), lax.axis_index(nbr)
    width, c_dev = features.shape
    n_rows = cotangent.shape[0]
    r_dev = n_rows * n_nbr
    scale = (12.0 / (c_dev * n_nbr / 2)) ** 0.5
    row_blocks, col_blocks = r_dev // TILE, c_dev // TILE
    swap_core = [(0, 1), (1, 0)]

    weight_z = spread(weight, "zh", n_zh)
    cot_z = spread(cotangent, "zh", n_zh)
    own = spread(weight_z, nbr, n_nbr)
    other = lax.ppermute(own, "core", swap_core)

    bases = jnp.stack([nbr_id * c_dev, core * r_dev]).astype(i32)
    partial = edge_product(bases, count, pairs, features, row_blocks, col_blocks, False, (5, 13), (3, 11), scale, True)
    hidden = jnp.sum(lax.all_to_all(partial, nbr, 0, 0), axis=0)
    hidden_all = lax.all_gather(hidden, "zh", axis=0, tiled=True)
    hidden_all = lax.all_gather(hidden_all, "x", axis=0, tiled=True)

    at = jnp.stack([core, lax.axis_index("zh")]).astype(i32)
    activations, grad_terms, own_terms, other_terms = layer(at, hidden_all, own, other, cot_z, n_x, n_zh)

    grad_hidden = jnp.sum(lax.all_to_all(grad_terms, "x", 0, 0), axis=0)
    grad_block = spread(grad_hidden, nbr, n_nbr)
    terms = own_terms + lax.ppermute(other_terms, "core", swap_core)
    weight_grad = jnp.sum(lax.all_to_all(terms, nbr, 0, 0), axis=0)

    column_part = edge_product(
        bases[::-1], count, pairs, grad_block, col_blocks, row_blocks, True, (3, 11), (5, 13), scale, False
    )
    feature_grad = column_part + lax.ppermute(column_part, "core", swap_core)
    return activations, feature_grad, weight_grad


def halves(n):
    minor = 1
    while minor * minor < n:
        minor *= 2
    return n // minor, minor


def solution(mesh):
    sizes = (mesh.shape["row"], *halves(mesh.shape["nbr"]), *halves(mesh.shape["feat"]))
    fine = Mesh(mesh.devices.reshape(sizes), ("core", "zl", "y", "x", "zh"))
    nbr, feat = ("zl", "y"), ("x", "zh")
    rows = ("core", *nbr)
    in_specs = (P(feat, nbr), P("core", nbr, None, None), P("core", nbr), P(rows, feat), P(rows, feat))
    out_specs = (P(rows, feat), P(feat, nbr), P(rows, feat))
    return jax.shard_map(per_device, mesh=fine, in_specs=in_specs, out_specs=out_specs, check_vma=False)
```

time: 761 us -> 181 us (0.24)
  waiting for transfers between devices: 413 us -> 18.1 us
  blocking collectives: 224 us -> 60.8 us
  matrix products: 59 us -> 0 us
  starting transfers between devices: 0.16 us -> 58.2 us
  local copies, waits for them, and re-layouts: 42.9 us -> 7.55 us
  Pallas kernels: 0 us -> 28.4 us
  between operations: 14.5 us -> 1.46 us
    reduce_scatter x3 -> x0, waiting for transfers between devices: 291 us -> none  [the longest x1 154 us: per_device(): lax.psum_scatter(weight_terms, ('row', 'nbr'), scatter_dimension=0, tiled...]
    all_gather x3 -> x2, blocking collectives: 224 us -> 25.3 us  [the longest x1 15.1 us: per_device(): hidden_all = lax.all_gather(hidden, 'zh', axis=0, tiled=True)]
    psum x1 -> x0, waiting for transfers between devices: 122 us -> none  [per_device(): feature_grad = lax.psum(column_part.T, 'row')]
    dot_general x15 -> x0, matrix products: 59 us -> none  [the longest x3 27.6 us: advance(): jnp.einsum('tab,taf->tbf', values, source[row_picks], precision=highest)]
    all_to_all x0 -> x2, blocking collectives: none -> 35.6 us  [the longest x1 27.2 us: spread(): lax.all_to_all(jnp.broadcast_to(value[None], (n,) + value.shape), axes, 0...]
    ppermute x0 -> x3, starting transfers between devices: none -> 31.9 us  [the longest x1 12.6 us: per_device(): terms = own_terms + lax.ppermute(other_terms, 'core', swap_core)]
    pallas_call x0 -> x3, Pallas kernels: none -> 28.4 us  [the longest x2 22.6 us: edge_product(): pl.pallas_call(functools.partial(product_kernel, lane_blocks, sub_blocks,...]
    all_to_all x0 -> x5, starting transfers between devices: none -> 26.3 us  [the longest x3 15.8 us: spread(): lax.all_to_all(jnp.broadcast_to(value[None], (n,) + value.shape), axes, 0...]
  transfers between devices with their start and end apart: 4 -> 8, of which waited for: 4 -> 3; matrix products, arithmetic and copies ran while one was open for 0% -> 5% of each run, Pallas kernels for 0% -> 13%
where the time goes in v1:
time: 181 us; the launch traced here: 180 us
  blocking collectives  60.8 us (34%)
  starting transfers between devices  58.2 us (32%)
  Pallas kernels  28.4 us (16%)
  waiting for transfers between devices  18.1 us (10%)
  local copies, waits for them, and re-layouts  7.55 us (4%)
  other arithmetic  5.42 us (3%)
    all_to_all x1, blocking collectives, spread(): lax.all_to_all(jnp.broadcast_to(value[None], (n,) + value.shape), axes, 0...  27.2 us
    pallas_call x2, Pallas kernels, edge_product(): pl.pallas_call(functools.partial(product_kernel, lane_blocks, sub_blocks,...  22.6 us
    all_to_all x3, starting transfers between devices, spread(): lax.all_to_all(jnp.broadcast_to(value[None], (n,) + value.shape), axes, 0...  15.8 us
    all_gather x1, blocking collectives, per_device(): hidden_all = lax.all_gather(hidden, 'zh', axis=0, tiled=True)  15.1 us
    ppermute x1, starting transfers between devices, per_device(): terms = own_terms + lax.ppermute(other_terms, 'core', swap_core)  12.6 us
    ppermute x1, starting transfers between devices, per_device(): feature_grad = column_part + lax.ppermute(column_part, 'core', swap_core)  11.9 us
    all_gather x1, blocking collectives, per_device(): hidden_all = lax.all_gather(hidden_all, 'x', axis=0, tiled=True)  10.2 us
    all_to_all x3, waiting for transfers between devices, spread(): lax.all_to_all(jnp.broadcast_to(value[None], (n,) + value.shape), axes, 0...  9.08 us
  transfers between devices with their start and end apart: 8, of which 3 were waited for; matrix products, arithmetic and copies ran while one was open for 5% of the time, Pallas kernels for 13%

profile of v1, /device:TPU:1, one launch (start us, length us, event | category | flops | bytes accessed | tf_op | source)
XLA Modules:
  0.0 179.9 jit_solution(13428364636151398641)
XLA Ops:
  1.5 27.2 %all_to_all.35 = f32[4,1,2048]{2,1,0:T(1,128)S(1)} all-to-all(f32[4,1,2048]{2,1,0:T(1,128)S(1)} %reshape.10), channel_id=1, replica_groups=mesh['core'=2,'zl'=4,'y'=4,'x'=4,'zh'=4] {'zh'}, dimensions={0} | all-to-all | bytes 65536 | tf_op jit(solution)/shard_map/all_to_all | solution.py:176
  29.3 3.3 %all-to-all-start.3 = ((f32[4,128,64]{1,2,0:T(8,128)}), f32[4,128,64]{1,2,0:T(8,128)S(1)}, u32[]{:S(2)}, u32[]{:S(2)}) async-start(f32[4,128,64]{1,2,0:T(8,128)} %broadcast_in_dim.10), calls=%async_computation.3 | async-start | bytes 262144 | tf_op jit(solution)/shard_map/all_to_all | solution.py:176
  34.3 1.4 reshape.12
  35.7 9.1 %all-to-all-done.3 = f32[4,128,64]{1,2,0:T(8,128)S(1)} async-done(((f32[4,128,64]{1,2,0:T(8,128)}), f32[4,128,64]{1,2,0:T(8,128)S(1)}, u32[]{:S(2)}, u32[]{:S(2)}) %all-to-all-start.3) | async-done | bytes 131104 | tf_op jit(solution)/shard_map/all_to_all | solution.py:176
  44.8 5.6 %all-to-all-start.2 = ((f32[16,1,8192]{2,1,0:T(1,128)}), f32[16,1,8192]{2,1,0:T(1,128)S(1)}, u32[]{:S(2)}, u32[]{:S(2)}) async-start(f32[16,1,8192]{2,1,0:T(1,128)} %reshape.12), calls=%async_computation.2 | async-start | bytes 1048576 | tf_op jit(solution)/shard_map/all_to_all | solution.py:176
  51.9 11.7 %shard_map.76 = f32[16,64,128]{2,1,0:T(8,128)} custom-call(s32[2]{0:T(128)S(1)} %pad_add_fusion.1.base_ref, s32[1]{0:T(128)} %bitcast.6.count_ref, s32[2,256]{1,0:T(2,128)S(1)} %bitcast.8, f32[64,2048]{1,0:T(8,128)S(1)} %copy-done), custom_call_target="tpu_custom_call" | custom-call | flops 8589934592 | bytes 2097152 | tf_op jit(solution)/shard_map/pallas_call | solution.py:92
  63.6 7.0 %all-to-all-start = ((f32[16,64,128]{2,1,0:T(8,128)}), f32[16,64,128]{2,1,0:T(8,128)S(1)}, u32[]{:S(2)}, u32[]{:S(2)}) async-start(f32[16,64,128]{2,1,0:T(8,128)} %shard_map.76), calls=%async_computation | async-start | bytes 1048576 | tf_op jit(solution)/shard_map/all_to_all | solution.py:199
  70.5 1.9 %reduce.1 = f32[16,8192]{1,0:T(8,128)S(1)} reduce(f32[16,1,8192]{2,1,0:T(1,128)S(1)} %all-to-all-done.2, f32[]{:T(128)} %broadcast.4), dimensions={1}, to_apply=%all_to_all.23.reduce_sub_computation | reduce | bytes 1048580 | tf_op jit(solution)/shard_map/all_to_all | solution.py:176
  72.9 7.3 %collective-permute-start = (f32[16,4,32,64]{3,2,1,0:T(8,128)S(1)}, f32[16,4,32,64]{3,2,1,0:T(8,128)S(1)}, u32[]{:S(2)}, u32[]{:S(2)}) collective-permute-start(f32[16,4,32,64]{3,2,1,0:T(8,128)S(1)} %reshape.13.own_ref), channel_id=1, source_target_pairs={{0,256},{256,0},{1,257},{257,1},{2,258},{258,2},{3,259},{259,3},{4... | collective-permute-start | bytes 1572872 | tf_op jit(solution)/shard_map/ppermute | solution.py:195
  80.5 1.3 all-to-all-done
  81.8 15.1 %all_gather.6 = f32[256,128]{1,0:T(8,128)S(1)} all-gather(f32[64,128]{1,0:T(8,128)S(1)} %reduce_sum.27), channel_id=1, replica_groups=mesh['core'=2,'zl'=4,'y'=4,'x'=4,'zh'=4] {'zh'}, dimensions={0}, use_global_device_ids=true | all-gather | bytes 163840 | tf_op jit(solution)/shard_map/all_gather | solution.py:200
  96.8 10.2 %all_gather.7.hidden_ref = f32[1024,128]{1,0:T(8,128)S(1)} all-gather(f32[256,128]{1,0:T(8,128)S(1)} %all_gather.6), channel_id=1, replica_groups=mesh['core'=2,'zl'=4,'y'=4,'x'=4,'zh'=4] {'x'}, dimensions={0}, use_global_device_ids=true | all-gather | bytes 655360 | tf_op jit(solution)/shard_map/all_gather | solution.py:201
  107.1 5.7 %shard_map.77 = (f32[128,64]{1,0:T(8,128)S(1)}, f32[4,64,128]{2,1,0:T(8,128)S(1)}, f32[16,32,64]{2,1,0:T(8,128)S(1)}, f32[16,32,64]{2,1,0:T(8,128)S(1)}) custom-call(s32[2]{0:T(128)S(1)} %pad_add_fusion.at_ref, f32[1024,128]{1,0:T(8,128)S(1)} %all_gather.7.hidden_ref, f32[16,4,32,64]{3,2,1,0:T(8,128)S(1)} %reshape.13.own_ref, ...), custom_call_target="tpu_custom_call" | custom-call | flops 1073741824 | bytes 2097152 | tf_op jit(solution)/shard_map/pallas_call | solution.py:160
  112.8 8.3 %all_to_all.36 = f32[4,64,128]{2,1,0:T(8,128)S(1)} all-to-all(f32[4,64,128]{2,1,0:T(8,128)S(1)} %get-tuple-element.8), channel_id=1, replica_groups=mesh['core'=2,'zl'=4,'y'=4,'x'=4,'zh'=4] {'x'}, dimensions={0} | all-to-all | bytes 262144 | tf_op jit(solution)/shard_map/all_to_all | solution.py:206
  121.1 0.8 broadcast_in_dim.11
  122.0 6.9 %all-to-all-start.5 = ((f32[16,64,128]{2,1,0:T(8,128)}), f32[16,64,128]{2,1,0:T(8,128)S(1)}, u32[]{:S(2)}, u32[]{:S(2)}) async-start(f32[16,64,128]{2,1,0:T(8,128)} %broadcast_in_dim.11), calls=%async_computation.5 | async-start | bytes 1048576 | tf_op jit(solution)/shard_map/all_to_all | solution.py:176
  129.0 12.6 %collective-permute-start.2 = (f32[16,32,64]{2,1,0:T(8,128)S(1)}, f32[16,32,64]{2,1,0:T(8,128)S(1)}, u32[]{:S(2)}, u32[]{:S(2)}) collective-permute-start(f32[16,32,64]{2,1,0:T(8,128)S(1)} %get-tuple-element.10), channel_id=1, source_target_pairs={{0,256},{256,0},{1,257},{257,1},{2,258},{258,2},{3,259},{259,3},{4... | collective-permute-start | bytes 393224 | tf_op jit(solution)/shard_map/ppermute | solution.py:208
  141.6 10.9 %shard_map.78 = f32[64,2048]{1,0:T(8,128)S(1)} custom-call(s32[2]{0:T(128)S(1)} %rev.3.base_ref, s32[1]{0:T(128)} %bitcast.7.count_ref, s32[2,256]{1,0:T(2,128)S(1)} %bitcast.9, f32[16,64,128]{2,1,0:T(8,128)S(1)} %all-to-all-done.5.source_ref), custom_call_target="tpu_custom_call" | custom-call | flops 8589934592 | bytes 2097152 | tf_op jit(solution)/shard_map/pallas_call | solution.py:92
  152.5 11.9 %collective-permute-start.1 = (f32[64,2048]{1,0:T(8,128)S(1)}, f32[64,2048]{1,0:T(8,128)S(1)}, u32[]{:S(2)}, u32[]{:S(2)}) collective-permute-start(f32[64,2048]{1,0:T(8,128)S(1)} %shard_map.78), channel_id=1, source_target_pairs={{0,256},{256,0},{1,257},{257,1},{2,258},{258,2},{3,259},{259,3},{4... | collective-permute-start | bytes 1572872 | tf_op jit(solution)/shard_map/ppermute | solution.py:214
  164.5 0.8 reshape.14
  165.4 3.5 %all-to-all-start.6 = ((f32[16,1,2048]{2,1,0:T(1,128)}), f32[16,1,2048]{2,1,0:T(1,128)S(1)}, u32[]{:S(2)}, u32[]{:S(2)}) async-start(f32[16,1,2048]{2,1,0:T(1,128)} %reshape.14), calls=%async_computation.6 | async-start | bytes 262144 | tf_op jit(solution)/shard_map/all_to_all | solution.py:209
  169.6 7.7 %all-to-all-done.6 = f32[16,1,2048]{2,1,0:T(1,128)S(1)} async-done(((f32[16,1,2048]{2,1,0:T(1,128)}), f32[16,1,2048]{2,1,0:T(1,128)S(1)}, u32[]{:S(2)}, u32[]{:S(2)}) %all-to-all-start.6) | async-done | bytes 131104 | tf_op jit(solution)/shard_map/all_to_all | solution.py:209
  177.3 1.0 reduce.2
  179.0 0.8 add.10
  (29 shorter events, 6.1 us)
Async XLA Ops:
  1.5 27.2 %copy-start.2 = (f32[128,64]{0,1:T(8,128)S(1)}, f32[128,64]{0,1:T(8,128)}, u32[]{:S(2)}) copy-start(f32[128,64]{0,1:T(8,128)} %param.9) | copy-start | bytes 98308
  29.3 15.4 %all-to-all-start.3 = ((f32[4,128,64]{1,2,0:T(8,128)}), f32[4,128,64]{1,2,0:T(8,128)S(1)}, u32[]{:S(2)}, u32[]{:S(2)}) async-start(f32[4,128,64]{1,2,0:T(8,128)} %broadcast_in_dim.10), calls=%async_computation.3 | async-start | bytes 262144 | tf_op jit(solution)/shard_map/all_to_all | solution.py:176
  35.7 15.5 %copy-start = (f32[64,2048]{1,0:T(8,128)S(1)}, f32[64,2048]{1,0:T(8,128)}, u32[]{:S(2)}) copy-start(f32[64,2048]{1,0:T(8,128)} %source_ref.1) | copy-start | bytes 1572868
  44.8 18.8 %all-to-all-start.2 = ((f32[16,1,8192]{2,1,0:T(1,128)}), f32[16,1,8192]{2,1,0:T(1,128)S(1)}, u32[]{:S(2)}, u32[]{:S(2)}) async-start(f32[16,1,8192]{2,1,0:T(1,128)} %reshape.12), calls=%async_computation.2 | async-start | bytes 1048576 | tf_op jit(solution)/shard_map/all_to_all | solution.py:176
  51.2 0.7 copy-start.1
  63.6 18.2 %all-to-all-start = ((f32[16,64,128]{2,1,0:T(8,128)}), f32[16,64,128]{2,1,0:T(8,128)S(1)}, u32[]{:S(2)}, u32[]{:S(2)}) async-start(f32[16,64,128]{2,1,0:T(8,128)} %shard_map.76), calls=%async_computation | async-start | bytes 1048576 | tf_op jit(solution)/shard_map/all_to_all | solution.py:199
  72.9 34.2 %collective-permute-start = (f32[16,4,32,64]{3,2,1,0:T(8,128)S(1)}, f32[16,4,32,64]{3,2,1,0:T(8,128)S(1)}, u32[]{:S(2)}, u32[]{:S(2)}) collective-permute-start(f32[16,4,32,64]{3,2,1,0:T(8,128)S(1)} %reshape.13.own_ref), channel_id=1, source_target_pairs={{0,256},{256,0},{1,257},{257,1},{2,258},{258,2},{3,259},{259,3},{4... | collective-permute-start | bytes 1572872 | tf_op jit(solution)/shard_map/ppermute | solution.py:195
  122.0 19.6 %all-to-all-start.5 = ((f32[16,64,128]{2,1,0:T(8,128)}), f32[16,64,128]{2,1,0:T(8,128)S(1)}, u32[]{:S(2)}, u32[]{:S(2)}) async-start(f32[16,64,128]{2,1,0:T(8,128)} %broadcast_in_dim.11), calls=%async_computation.5 | async-start | bytes 1048576 | tf_op jit(solution)/shard_map/all_to_all | solution.py:176
  129.0 35.5 %collective-permute-start.2 = (f32[16,32,64]{2,1,0:T(8,128)S(1)}, f32[16,32,64]{2,1,0:T(8,128)S(1)}, u32[]{:S(2)}, u32[]{:S(2)}) collective-permute-start(f32[16,32,64]{2,1,0:T(8,128)S(1)} %get-tuple-element.10), channel_id=1, source_target_pairs={{0,256},{256,0},{1,257},{257,1},{2,258},{258,2},{3,259},{259,3},{4... | collective-permute-start | bytes 393224 | tf_op jit(solution)/shard_map/ppermute | solution.py:208
  152.5 26.5 %collective-permute-start.1 = (f32[64,2048]{1,0:T(8,128)S(1)}, f32[64,2048]{1,0:T(8,128)S(1)}, u32[]{:S(2)}, u32[]{:S(2)}) collective-permute-start(f32[64,2048]{1,0:T(8,128)S(1)} %shard_map.78), channel_id=1, source_target_pairs={{0,256},{256,0},{1,257},{257,1},{2,258},{258,2},{3,259},{259,3},{4... | collective-permute-start | bytes 1572872 | tf_op jit(solution)/shard_map/ppermute | solution.py:214
  165.4 11.9 %all-to-all-start.6 = ((f32[16,1,2048]{2,1,0:T(1,128)}), f32[16,1,2048]{2,1,0:T(1,128)S(1)}, u32[]{:S(2)}, u32[]{:S(2)}) async-start(f32[16,1,2048]{2,1,0:T(1,128)} %reshape.14), calls=%async_computation.6 | async-start | bytes 262144 | tf_op jit(solution)/shard_map/all_to_all | solution.py:209

commit v2 on v1

--- a/solution.py
+++ b/solution.py
@@ -89,16 +89,12 @@
     width = source.shape[1] if source.ndim == 3 else source.shape[0]
     shape = (lane_blocks, width, TILE) if stacked else (width, lane_blocks * TILE)
     tiles = lane_blocks * sub_blocks
+    smem, vmem = pl.BlockSpec(memory_space=pltpu.SMEM), pl.BlockSpec(memory_space=pltpu.VMEM)
     return pl.pallas_call(
         functools.partial(product_kernel, lane_blocks, sub_blocks, swap, sub_poly, lane_poly, scale),
         out_shape=jax.ShapeDtypeStruct(shape, f32),
-        in_specs=[
-            pl.BlockSpec(memory_space=pltpu.SMEM),
-            pl.BlockSpec(memory_space=pltpu.SMEM),
-            pl.BlockSpec(memory_space=pltpu.VMEM),
-            pl.BlockSpec(memory_space=pltpu.VMEM),
-        ],
-        out_specs=pl.BlockSpec(memory_space=pltpu.VMEM),
+        in_specs=[smem, smem, vmem, vmem],
+        out_specs=vmem,
         scratch_shapes=[
             pltpu.VMEM((sub_blocks * TILE, TILE), f32),
             pltpu.VMEM((TILE, TILE), f32),
@@ -116,14 +112,18 @@
 
 
 def layer_kernel(
-    n_x, n_zh, at_ref, hidden_ref, own_ref, other_ref, cot_ref,
+    n_x, n_zh, at_ref, hidden_ref, own_ref, other_ref, both_ref,
     act_ref, grad_ref, own_terms_ref, other_terms_ref, weight,
 ):
     core, zh = at_ref[0], at_ref[1]
     half = own_ref.shape[0]
-    rows, width = own_ref.shape[2], own_ref.shape[3]
-    weight[pl.ds(core * half, half)] = own_ref[...]
-    weight[pl.ds((1 - core) * half, half)] = other_ref[...]
+    rows, width = weight.shape[2], weight.shape[3]
+    packed = rows // 2
+    for which, ref in ((core, own_ref), (1 - core, other_ref)):
+        for z in range(n_zh):
+            blocks = ref[:, z * packed:(z + 1) * packed, :]
+            weight[pl.ds(which * half, half), z, :packed, :] = blocks[:, :, :width]
+            weight[pl.ds(which * half, half), z, packed:, :] = blocks[:, :, width:]
     hidden = hidden_ref[...].T
     depth = hidden.shape[1]
     grads = []
@@ -131,7 +131,7 @@
         columns = weight[:, z].reshape(depth, width)
         pre = dot(hidden, columns)
         squash = 1.0 / (1.0 + jnp.exp(-pre))
-        grad_pre = cot_ref[z] * squash * (1.0 + pre * (1.0 - squash))
+        grad_pre = unpack(both_ref[z, packed:, :]) * squash * (1.0 + pre * (1.0 - squash))
         grads.append(grad_pre)
 
         @pl.when(zh == z)
@@ -139,8 +139,8 @@
             act_ref[...] = pre * squash
             own = hidden_ref[pl.ds(pl.multiple_of(core * (depth // 2), 8), depth // 2), :]
             other = hidden_ref[pl.ds(pl.multiple_of((1 - core) * (depth // 2), 8), depth // 2), :]
-            own_terms_ref[...] = dot(own, grad_pre).reshape(own_terms_ref.shape)
-            other_terms_ref[...] = dot(other, grad_pre).reshape(other_terms_ref.shape)
+            own_terms_ref[...] = pack(dot(own, grad_pre).reshape(half, rows, width))
+            other_terms_ref[...] = pack(dot(other, grad_pre).reshape(half, rows, width))
 
     per_block = width // rows
     for x in range(n_x):
@@ -152,10 +152,11 @@
         grad_ref[x] = total
 
 
-def layer(at, hidden_all, own, other, cot, n_x, n_zh):
-    half, _, rows, width = own.shape
+def layer(at, hidden_all, own, other, both, n_x, n_zh, rows):
+    half = own.shape[0]
+    width = own.shape[2] // 2
     n_rows = hidden_all.shape[1]
-    terms = jax.ShapeDtypeStruct((half, rows, width), f32)
+    terms = jax.ShapeDtypeStruct((half, rows // 2, 2 * width), f32)
     vmem = pl.BlockSpec(memory_space=pltpu.VMEM)
     return pl.pallas_call(
         functools.partial(layer_kernel, n_x, n_zh),
@@ -169,11 +170,25 @@
         scratch_shapes=[pltpu.VMEM((2 * half, n_zh, rows, width), f32)],
         compiler_params=pltpu.CompilerParams(vmem_limit_bytes=32 << 20),
         cost_estimate=pl.CostEstimate(flops=1 << 30, bytes_accessed=1 << 21, transcendentals=0),
-    )(at, hidden_all, own, other, cot)
-
-
-def spread(value, axes, n):
-    return lax.all_to_all(jnp.broadcast_to(value[None], (n,) + value.shape), axes, 0, 0)
+    )(at, hidden_all, own, other, both)
+
+
+def pack(value):
+    n = value.shape[-2] // 2
+    return jnp.concatenate([value[..., :n, :], value[..., n:, :]], axis=-1)
+
+
+def unpack(value):
+    width = value.shape[-1] // 2
+    return jnp.concatenate([value[..., :width], value[..., width:]], axis=-2)
+
+
+def copies(value, n):
+    return jnp.broadcast_to(value[None], (n,) + value.shape)
+
+
+def exchange(value, axes):
+    return lax.all_to_all(value, axes, 0, 0)
 
 
 def per_device(features, tile_list, tile_count, weight, cotangent):
@@ -189,29 +204,35 @@
     row_blocks, col_blocks = r_dev // TILE, c_dev // TILE
     swap_core = [(0, 1), (1, 0)]
 
-    weight_z = spread(weight, "zh", n_zh)
-    cot_z = spread(cotangent, "zh", n_zh)
-    own = spread(weight_z, nbr, n_nbr)
-    other = lax.ppermute(own, "core", swap_core)
+    both = jnp.concatenate([pack(weight), pack(cotangent)], axis=0)
+    both_z = exchange(copies(both, n_zh), "zh")
 
     bases = jnp.stack([nbr_id * c_dev, core * r_dev]).astype(i32)
     partial = edge_product(bases, count, pairs, features, row_blocks, col_blocks, False, (5, 13), (3, 11), scale, True)
-    hidden = jnp.sum(lax.all_to_all(partial, nbr, 0, 0), axis=0)
-    hidden_all = lax.all_gather(hidden, "zh", axis=0, tiled=True)
-    hidden_all = lax.all_gather(hidden_all, "x", axis=0, tiled=True)
+    both_z, partial = lax.optimization_barrier((both_z, partial))
+    weight_z = both_z[:, :weight.shape[0] // 2].reshape(-1, both.shape[1])
+    hidden = jnp.sum(exchange(partial, nbr), axis=0)
+    hidden, weight_z = lax.optimization_barrier((hidden, copies(weight_z, n_nbr)))
+    own = exchange(weight_z, nbr)
+    hidden_z = lax.all_gather(hidden, "zh", axis=0, tiled=True)
+    hidden_z, own = lax.optimization_barrier((hidden_z, own))
+    other = lax.ppermute(own, "core", swap_core)
+    hidden_all = lax.all_gather(hidden_z, "x", axis=0, tiled=True)
 
     at = jnp.stack([core, lax.axis_index("zh")]).astype(i32)
-    activations, grad_terms, own_terms, other_terms = layer(at, hidden_all, own, other, cot_z, n_x, n_zh)
-
-    grad_hidden = jnp.sum(lax.all_to_all(grad_terms, "x", 0, 0), axis=0)
-    grad_block = spread(grad_hidden, nbr, n_nbr)
+    activations, grad_terms, own_terms, other_terms = layer(at, hidden_all, own, other, both_z, n_x, n_zh, weight.shape[0])
+
+    grad_hidden = jnp.sum(exchange(grad_terms, "x"), axis=0)
+    grad_block = exchange(copies(grad_hidden, n_nbr), nbr)
     terms = own_terms + lax.ppermute(other_terms, "core", swap_core)
-    weight_grad = jnp.sum(lax.all_to_all(terms, nbr, 0, 0), axis=0)
-
+    grad_block, terms = lax.optimization_barrier((grad_block, terms))
+    terms = exchange(terms, nbr)
     column_part = edge_product(
         bases[::-1], count, pairs, grad_block, col_blocks, row_blocks, True, (3, 11), (5, 13), scale, False
     )
+    column_part, terms = lax.optimization_barrier((column_part, terms))
     feature_grad = column_part + lax.ppermute(column_part, "core", swap_core)
+    weight_grad = unpack(jnp.sum(terms, axis=0))
     return activations, feature_grad, weight_grad
 
 

time: 181 us -> 158 us (0.87)
  blocking collectives: 60.8 us -> 39.5 us
  starting transfers between devices: 58.2 us -> 63.7 us
  other arithmetic: 5.42 us -> 2.51 us
  waiting for transfers between devices: 18.1 us -> 15.7 us
  local copies, waits for them, and re-layouts: 7.55 us -> 5.48 us
    all_to_all x2 -> x1, blocking collectives: 35.6 us -> 8.02 us  [exchange(): return lax.all_to_all(value, axes, 0, 0)]
    all_to_all x5, starting transfers between devices: 26.3 us -> 43.8 us  [exchange(): return lax.all_to_all(value, axes, 0, 0)]
    all_gather x2, blocking collectives: 25.3 us -> 31.5 us  [the longest x1 20.5 us: per_device(): hidden_z = lax.all_gather(hidden, 'zh', axis=0, tiled=True)]
    ppermute x1, starting transfers between devices: 12.6 us -> 6.57 us  [per_device(): terms = own_terms + lax.ppermute(other_terms, 'core', swap_core)]
    ppermute x1, starting transfers between devices: 11.9 us -> 6.92 us  [per_device(): feature_grad = column_part + lax.ppermute(column_part, 'core', swap_core)]
    all_to_all x3 -> x0, other arithmetic: 3.7 us -> none  [the longest x2 2.7 us: spread(): lax.all_to_all(jnp.broadcast_to(value[None], (n,) + value.shape), axes, 0...]
    all_to_all x5, waiting for transfers between devices: 18.1 us -> 14.7 us  [exchange(): return lax.all_to_all(value, axes, 0, 0)]
    unnamed x13 -> x11, local copies, waits for them, and re-layouts: 4.38 us -> 1.97 us
  transfers between devices with their start and end apart: 8 -> 8, of which waited for: 3 -> 4; matrix products, arithmetic and copies ran while one was open for 5% -> 1% of each run, Pallas kernels for 13% -> 14%
where the time goes in v2:
time: 158 us; the launch traced here: 157 us
  starting transfers between devices  63.7 us (40%)
  blocking collectives  39.5 us (25%)
  Pallas kernels  28.7 us (18%)
  waiting for transfers between devices  15.7 us (10%)
  local copies, waits for them, and re-layouts  5.48 us (3%)
  other arithmetic  2.51 us (2%)
    all_to_all x5, starting transfers between devices, exchange(): return lax.all_to_all(value, axes, 0, 0)  43.8 us
    pallas_call x2, Pallas kernels, edge_product(): pl.pallas_call(functools.partial(product_kernel, lane_blocks, sub_blocks,...  22.7 us
    all_gather x1, blocking collectives, per_device(): hidden_z = lax.all_gather(hidden, 'zh', axis=0, tiled=True)  20.5 us
    all_to_all x5, waiting for transfers between devices, exchange(): return lax.all_to_all(value, axes, 0, 0)  14.7 us
    all_gather x1, blocking collectives, per_device(): hidden_all = lax.all_gather(hidden_z, 'x', axis=0, tiled=True)  11 us
    all_to_all x1, blocking collectives, exchange(): return lax.all_to_all(value, axes, 0, 0)  8.02 us
    ppermute x1, starting transfers between devices, per_device(): feature_grad = column_part + lax.ppermute(column_part, 'core', swap_core)  6.92 us
    ppermute x1, starting transfers between devices, per_device(): terms = own_terms + lax.ppermute(other_terms, 'core', swap_core)  6.57 us
  transfers between devices with their start and end apart: 8, of which 4 were waited for; matrix products, arithmetic and copies ran while one was open for 1% of the time, Pallas kernels for 14%

profile of v2, /device:TPU:1, one launch (start us, length us, event | category | flops | bytes accessed | tf_op | source)
XLA Modules:
  0.0 157.0 jit_solution(10500520374768111374)
XLA Ops:
  0.6 0.7 fusion.1
  2.4 0.7 broadcast_in_dim.8
  3.0 15.6 %all-to-all-start = ((f32[4,80,128]{2,1,0:T(8,128)}), f32[4,80,128]{2,1,0:T(8,128)S(1)}, u32[]{:S(2)}, u32[]{:S(2)}) async-start(f32[4,80,128]{2,1,0:T(8,128)} %broadcast_in_dim.8), calls=%async_computation | async-start | bytes 327680 | tf_op jit(solution)/shard_map/all_to_all | solution.py:191
  19.4 0.7 copy-done.3
  20.1 11.7 %shard_map.76 = f32[16,64,128]{2,1,0:T(8,128)} custom-call(s32[2]{0:T(128)S(1)} %pad_add_fusion.1.base_ref, s32[1]{0:T(128)} %bitcast.7.count_ref, s32[2,256]{1,0:T(2,128)S(1)} %bitcast.10, f32[64,2048]{1,0:T(8,128)S(1)} %copy-done.2), custom_call_target="tpu_custom_call" | custom-call | flops 8589934592 | bytes 2097152 | tf_op jit(solution)/shard_map/pallas_call | solution.py:93
  31.8 7.2 %all-to-all-start.1 = ((f32[16,64,128]{2,1,0:T(8,128)}), f32[16,64,128]{2,1,0:T(8,128)S(1)}, u32[]{:S(2)}, u32[]{:S(2)}) async-start(f32[16,64,128]{2,1,0:T(8,128)} %shard_map.76), calls=%async_computation.1 | async-start | bytes 1048576 | tf_op jit(solution)/shard_map/all_to_all | solution.py:191
  39.0 11.7 %all-to-all-done.1 = f32[16,64,128]{2,1,0:T(8,128)S(1)} async-done(((f32[16,64,128]{2,1,0:T(8,128)}), f32[16,64,128]{2,1,0:T(8,128)S(1)}, u32[]{:S(2)}, u32[]{:S(2)}) %all-to-all-start.1) | async-done | bytes 524320 | tf_op jit(solution)/shard_map/all_to_all | solution.py:191
  50.8 0.8 broadcast_in_dim.10
  51.7 6.8 %all-to-all-start.2 = ((f32[16,64,128]{2,1,0:T(8,128)}), f32[16,64,128]{2,1,0:T(8,128)S(1)}, u32[]{:S(2)}, u32[]{:S(2)}) async-start(f32[16,64,128]{2,1,0:T(8,128)} %broadcast_in_dim.10), calls=%async_computation.2 | async-start | bytes 1048576 | tf_op jit(solution)/shard_map/all_to_all | solution.py:191
  58.4 20.5 %all_gather.6 = f32[256,128]{1,0:T(8,128)S(1)} all-gather(f32[64,128]{1,0:T(8,128)S(1)} %reduce_sum.27), channel_id=1, replica_groups=mesh['core'=2,'zl'=4,'y'=4,'x'=4,'zh'=4] {'zh'}, dimensions={0}, use_global_device_ids=true | all-gather | bytes 163840 | tf_op jit(solution)/shard_map/all_gather | solution.py:217
  79.0 6.4 %collective-permute-start = (f32[16,64,128]{2,1,0:T(8,128)S(1)}, f32[16,64,128]{2,1,0:T(8,128)S(1)}, u32[]{:S(2)}, u32[]{:S(2)}) collective-permute-start(f32[16,64,128]{2,1,0:T(8,128)S(1)} %all-to-all-done.2.own_ref), channel_id=1, source_target_pairs={{0,256},{256,0},{1,257},{257,1},{2,258},{258,2},{3,259},{259,3},{4... | collective-permute-start | bytes 1572872 | tf_op jit(solution)/shard_map/ppermute | solution.py:219
  85.4 11.0 %all_gather.7.hidden_ref = f32[1024,128]{1,0:T(8,128)S(1)} all-gather(f32[256,128]{1,0:T(8,128)S(1)} %all_gather.6), channel_id=1, replica_groups=mesh['core'=2,'zl'=4,'y'=4,'x'=4,'zh'=4] {'x'}, dimensions={0}, use_global_device_ids=true | all-gather | bytes 655360 | tf_op jit(solution)/shard_map/all_gather | solution.py:220
  96.4 6.0 %shard_map.77 = (f32[128,64]{1,0:T(8,128)S(1)}, f32[4,64,128]{2,1,0:T(8,128)S(1)}, f32[16,16,128]{2,1,0:T(8,128)S(1)}, f32[16,16,128]{2,1,0:T(8,128)S(1)}) custom-call(s32[2]{0:T(128)S(1)} %pad_add_fusion.at_ref, f32[1024,128]{1,0:T(8,128)S(1)} %all_gather.7.hidden_ref, f32[16,64,128]{2,1,0:T(8,128)S(1)} %all-to-all-done.2.own_ref, ...), custom_call_target="tpu_custom_call" | custom-call | flops 1073741824 | bytes 2097152 | tf_op jit(solution)/shard_map/pallas_call | solution.py:161
  102.5 8.0 %all_to_all.30 = f32[4,64,128]{2,1,0:T(8,128)S(1)} all-to-all(f32[4,64,128]{2,1,0:T(8,128)S(1)} %get-tuple-element.24), channel_id=1, replica_groups=mesh['core'=2,'zl'=4,'y'=4,'x'=4,'zh'=4] {'x'}, dimensions={0} | all-to-all | bytes 262144 | tf_op jit(solution)/shard_map/all_to_all | solution.py:191
  110.5 0.8 broadcast_in_dim.22
  111.3 9.5 %all-to-all-start.4 = ((f32[16,64,128]{2,1,0:T(8,128)}), f32[16,64,128]{2,1,0:T(8,128)S(1)}, u32[]{:S(2)}, u32[]{:S(2)}) async-start(f32[16,64,128]{2,1,0:T(8,128)} %broadcast_in_dim.22), calls=%async_computation.4 | async-start | bytes 1048576 | tf_op jit(solution)/shard_map/all_to_all | solution.py:191
  120.9 6.6 %collective-permute-start.1 = (f32[16,16,128]{2,1,0:T(8,128)S(1)}, f32[16,16,128]{2,1,0:T(8,128)S(1)}, u32[]{:S(2)}, u32[]{:S(2)}) collective-permute-start(f32[16,16,128]{2,1,0:T(8,128)S(1)} %get-tuple-element.26), channel_id=1, source_target_pairs={{0,256},{256,0},{1,257},{257,1},{2,258},{258,2},{3,259},{259,3},{4... | collective-permute-start | bytes 393224 | tf_op jit(solution)/shard_map/ppermute | solution.py:227
  127.5 0.9 collective-permute-done.1
  129.1 2.9 %all-to-all-done.4.source_ref = f32[16,64,128]{2,1,0:T(8,128)S(1)} async-done(((f32[16,64,128]{2,1,0:T(8,128)}), f32[16,64,128]{2,1,0:T(8,128)S(1)}, u32[]{:S(2)}, u32[]{:S(2)}) %all-to-all-start.4) | async-done | bytes 524320 | tf_op jit(solution)/shard_map/all_to_all | solution.py:191
  132.0 4.7 %all-to-all-start.5 = ((f32[16,16,128]{2,1,0:T(8,128)}), f32[16,16,128]{2,1,0:T(8,128)S(1)}, u32[]{:S(2)}, u32[]{:S(2)}) async-start(f32[16,16,128]{2,1,0:T(8,128)} %add.10), calls=%async_computation.5 | async-start | bytes 262144 | tf_op jit(solution)/shard_map/all_to_all | solution.py:191
  136.7 10.9 %shard_map.78 = f32[64,2048]{1,0:T(8,128)S(1)} custom-call(s32[2]{0:T(128)S(1)} %rev.3.base_ref, s32[1]{0:T(128)} %bitcast.8.count_ref, s32[2,256]{1,0:T(2,128)S(1)} %bitcast.11, f32[16,64,128]{2,1,0:T(8,128)S(1)} %all-to-all-done.4.source_ref), custom_call_target="tpu_custom_call" | custom-call | flops 8589934592 | bytes 2097152 | tf_op jit(solution)/shard_map/pallas_call | solution.py:93
  147.7 6.9 %collective-permute-start.2 = (f32[64,2048]{1,0:T(8,128)S(1)}, f32[64,2048]{1,0:T(8,128)S(1)}, u32[]{:S(2)}, u32[]{:S(2)}) collective-permute-start(f32[64,2048]{1,0:T(8,128)S(1)} %shard_map.78), channel_id=1, source_target_pairs={{0,256},{256,0},{1,257},{257,1},{2,258},{258,2},{3,259},{259,3},{4... | collective-permute-start | bytes 1572872 | tf_op jit(solution)/shard_map/ppermute | solution.py:234
  154.6 0.7 copy.14
  156.1 0.8 add.11
  (30 shorter events, 2.8 us)
Async XLA Ops:
  1.3 0.8 copy-start.4
  1.4 18.0 %copy-start.2 = (f32[64,2048]{1,0:T(8,128)S(1)}, f32[64,2048]{1,0:T(8,128)}, u32[]{:S(2)}) copy-start(f32[64,2048]{1,0:T(8,128)} %source_ref.1) | copy-start | bytes 1572868
  3.0 28.8 %all-to-all-start = ((f32[4,80,128]{2,1,0:T(8,128)}), f32[4,80,128]{2,1,0:T(8,128)S(1)}, u32[]{:S(2)}, u32[]{:S(2)}) async-start(f32[4,80,128]{2,1,0:T(8,128)} %broadcast_in_dim.8), calls=%async_computation | async-start | bytes 327680 | tf_op jit(solution)/shard_map/all_to_all | solution.py:191
  19.4 0.7 copy-start.3
  31.8 7.2 %copy-start = (f32[4,80,128]{2,1,0:T(8,128)}, f32[4,80,128]{2,1,0:T(8,128)S(1)}, u32[]{:S(2)}) copy-start(f32[4,80,128]{2,1,0:T(8,128)S(1)} %all-to-all-done.both_ref) | copy-start | bytes 491524
  31.8 19.0 %all-to-all-start.1 = ((f32[16,64,128]{2,1,0:T(8,128)}), f32[16,64,128]{2,1,0:T(8,128)S(1)}, u32[]{:S(2)}, u32[]{:S(2)}) async-start(f32[16,64,128]{2,1,0:T(8,128)} %shard_map.76), calls=%async_computation.1 | async-start | bytes 1048576 | tf_op jit(solution)/shard_map/all_to_all | solution.py:191
  39.0 11.8 %slice-start = ((f32[4,80,128]{2,1,0:T(8,128)}), f32[4,16,128]{2,1,0:T(8,128)S(1)}, s32[]{:S(2)}) async-start(f32[4,80,128]{2,1,0:T(8,128)} %copy-done), calls=%async_computation.6 | async-start | bytes 65536 | tf_op jit(solution)/shard_map/slice | solution.py:213
  51.7 27.3 %all-to-all-start.2 = ((f32[16,64,128]{2,1,0:T(8,128)}), f32[16,64,128]{2,1,0:T(8,128)S(1)}, u32[]{:S(2)}, u32[]{:S(2)}) async-start(f32[16,64,128]{2,1,0:T(8,128)} %broadcast_in_dim.10), calls=%async_computation.2 | async-start | bytes 1048576 | tf_op jit(solution)/shard_map/all_to_all | solution.py:191
  79.0 17.4 %collective-permute-start = (f32[16,64,128]{2,1,0:T(8,128)S(1)}, f32[16,64,128]{2,1,0:T(8,128)S(1)}, u32[]{:S(2)}, u32[]{:S(2)}) collective-permute-start(f32[16,64,128]{2,1,0:T(8,128)S(1)} %all-to-all-done.2.own_ref), channel_id=1, source_target_pairs={{0,256},{256,0},{1,257},{257,1},{2,258},{258,2},{3,259},{259,3},{4... | collective-permute-start | bytes 1572872 | tf_op jit(solution)/shard_map/ppermute | solution.py:219
  85.4 11.0 %copy-start.1 = (f32[4,80,128]{2,1,0:T(8,128)S(1)}, f32[4,80,128]{2,1,0:T(8,128)}, u32[]{:S(2)}) copy-start(f32[4,80,128]{2,1,0:T(8,128)} %copy-done) | copy-start | bytes 491524
  111.3 20.7 %all-to-all-start.4 = ((f32[16,64,128]{2,1,0:T(8,128)}), f32[16,64,128]{2,1,0:T(8,128)S(1)}, u32[]{:S(2)}, u32[]{:S(2)}) async-start(f32[16,64,128]{2,1,0:T(8,128)} %broadcast_in_dim.22), calls=%async_computation.4 | async-start | bytes 1048576 | tf_op jit(solution)/shard_map/all_to_all | solution.py:191
  120.9 7.5 %collective-permute-start.1 = (f32[16,16,128]{2,1,0:T(8,128)S(1)}, f32[16,16,128]{2,1,0:T(8,128)S(1)}, u32[]{:S(2)}, u32[]{:S(2)}) collective-permute-start(f32[16,16,128]{2,1,0:T(8,128)S(1)} %get-tuple-element.26), channel_id=1, source_target_pairs={{0,256},{256,0},{1,257},{257,1},{2,258},{258,2},{3,259},{259,3},{4... | collective-permute-start | bytes 393224 | tf_op jit(solution)/shard_map/ppermute | solution.py:227
  132.0 15.7 %all-to-all-start.5 = ((f32[16,16,128]{2,1,0:T(8,128)}), f32[16,16,128]{2,1,0:T(8,128)S(1)}, u32[]{:S(2)}, u32[]{:S(2)}) async-start(f32[16,16,128]{2,1,0:T(8,128)} %add.10), calls=%async_computation.5 | async-start | bytes 262144 | tf_op jit(solution)/shard_map/all_to_all | solution.py:191
  147.7 8.4 %collective-permute-start.2 = (f32[64,2048]{1,0:T(8,128)S(1)}, f32[64,2048]{1,0:T(8,128)S(1)}, u32[]{:S(2)}, u32[]{:S(2)}) collective-permute-start(f32[64,2048]{1,0:T(8,128)S(1)} %shard_map.78), channel_id=1, source_target_pairs={{0,256},{256,0},{1,257},{257,1},{2,258},{258,2},{3,259},{259,3},{4... | collective-permute-start | bytes 1572872 | tf_op jit(solution)/shard_map/ppermute | solution.py:234

commit v3 on v1

v3 whole, which is shorter than its diff:
```python
import functools

import jax
import jax.numpy as jnp
from jax import lax
from jax.experimental import pallas as pl
from jax.experimental.pallas import tpu as pltpu
from jax.sharding import Mesh
from jax.sharding import PartitionSpec as P

TILE = 128
MODULUS = 32749
INVERSE = 1.0 / MODULUS
HALF_STEP = 0.5 / MODULUS
f32, bf16, i32 = jnp.float32, jnp.bfloat16, jnp.int32


def residue(value):
    quotient = jnp.floor(value.astype(f32) * INVERSE).astype(i32)
    rest = value - quotient * MODULUS
    rest = jnp.where(rest < 0, rest + MODULUS, rest)
    return jnp.where(rest >= MODULUS, rest - MODULUS, rest)


def split(value):
    high = value.astype(bf16)
    return high, (value - high.astype(f32)).astype(bf16)


def pack(value):
    n = value.shape[-2] // 2
    return jnp.concatenate([value[..., :n, :], value[..., n:, :]], axis=-1)


def unpack(value):
    width = value.shape[-1] // 2
    return jnp.concatenate([value[..., :width], value[..., width:]], axis=-2)


def listed_tiles(swap, sub_blocks, count_ref, pairs_ref, tiles):
    slots = pairs_ref.shape[1]
    major, minor = (pairs_ref[1:2, :], pairs_ref[0:1, :]) if swap else (pairs_ref[0:1, :], pairs_ref[1:2, :])
    code = major * sub_blocks + minor
    code = jnp.where(lax.broadcasted_iota(i32, (1, slots), 1) < count_ref[0], code, -1)
    listed = (lax.broadcasted_iota(i32, (tiles, slots), 0) == code).astype(f32)
    return jnp.broadcast_to(jnp.sum(listed, axis=1, keepdims=True), (tiles, TILE))


def sub_turns(sub_base, n_sub, sub_poly):
    sub = sub_base + lax.broadcasted_iota(i32, (n_sub, TILE), 0)
    return residue(sub * residue(sub_poly[0] * sub + sub_poly[1])).astype(f32) * INVERSE


def lane_turns(j, sub_base, lane_base, sub_blocks, lane_poly):
    first_lane = lane_base + j * TILE
    lane = first_lane + lax.broadcasted_iota(i32, (TILE, TILE), 1)
    k = lax.broadcasted_iota(i32, (TILE, TILE), 0)
    steps = residue(7 * k * lane).astype(f32) * INVERSE
    lane = first_lane + lax.broadcasted_iota(i32, (sub_blocks, TILE), 1)
    first = sub_base + TILE * lax.broadcasted_iota(i32, (sub_blocks, TILE), 0)
    inner = residue(lane_poly[0] * lane + lane_poly[1] + 7 * first)
    return steps, residue(lane * inner).astype(f32) * INVERSE - 0.5


def edge_parts(turn, listed):
    edge = turn - jnp.floor(turn + (0.5 + HALF_STEP))
    return jnp.concatenate(split(edge * listed), axis=1)


def fold(total, scale):
    width = total.shape[0] // 2
    total = total[:, :TILE] + total[:, TILE:]
    return (total[:width] + total[width:]) * scale


def first_kernel(
    lane_blocks, sub_blocks, sub_poly, lane_poly, scale,
    base_ref, count_ref, pairs_ref, source_ref, out_ref,
    sub_table, step_table, lane_table, mask_table, source_parts,
):
    sub_base, lane_base = base_ref[0], base_ref[1]
    width = source_ref.shape[0]
    mask_table[...] = listed_tiles(False, sub_blocks, count_ref, pairs_ref, lane_blocks * sub_blocks)
    sub_table[...] = sub_turns(sub_base, sub_blocks * TILE, sub_poly)
    for l in range(sub_blocks):
        columns = slice(l * TILE, (l + 1) * TILE)
        source_parts[:width, columns], source_parts[width:, columns] = split(source_ref[:, columns])

    def block(j, carry):
        step_table[...], lane_table[...] = lane_turns(j, sub_base, lane_base, sub_blocks, lane_poly)
        total = jnp.zeros((2 * width, 2 * TILE), f32)
        for l in range(0, sub_blocks, 2):
            parts = []
            for at in (l, l + 1):
                turn = sub_table[at * TILE:(at + 1) * TILE, :] + step_table[...] + lane_table[at:at + 1, :]
                parts.append(edge_parts(turn, mask_table[pl.ds(j * sub_blocks + at, 1), :]))
            total += jnp.dot(
                source_parts[:, l * TILE:(l + 2) * TILE], jnp.concatenate(parts, axis=0),
                preferred_element_type=f32,
            )
        out_ref[j, :width, :] = fold(total, scale)
        return carry

    lax.fori_loop(0, lane_blocks, block, 0)


SMEM, VMEM = pl.BlockSpec(memory_space=pltpu.SMEM), pl.BlockSpec(memory_space=pltpu.VMEM)


def tables(sub_blocks, lane_blocks):
    return [
        pltpu.VMEM((sub_blocks * TILE, TILE), f32),
        pltpu.VMEM((TILE, TILE), f32),
        pltpu.VMEM((sub_blocks, TILE), f32),
        pltpu.VMEM((lane_blocks * sub_blocks, TILE), f32),
    ]


def cost(flops, traffic):
    return pl.CostEstimate(flops=flops, bytes_accessed=traffic, transcendentals=0)


def first_product(base, count, pairs, source, lane_blocks, sub_blocks, sub_poly, lane_poly, scale, room):
    width = source.shape[0]
    return pl.pallas_call(
        functools.partial(first_kernel, lane_blocks, sub_blocks, sub_poly, lane_poly, scale),
        out_shape=jax.ShapeDtypeStruct((lane_blocks, room, TILE), f32),
        in_specs=[SMEM, SMEM, VMEM, VMEM],
        out_specs=VMEM,
        scratch_shapes=tables(sub_blocks, lane_blocks) + [pltpu.VMEM((2 * width, sub_blocks * TILE), bf16)],
        compiler_params=pltpu.CompilerParams(vmem_limit_bytes=24 << 20),
        cost_estimate=cost(8 << 30, 1 << 21),
    )(base, count, pairs, source)


def edges_kernel(
    lane_blocks, sub_blocks, sub_poly, lane_poly, base_ref, count_ref, pairs_ref, out_ref,
    sub_table, step_table, lane_table, mask_table,
):
    j = pl.program_id(0)
    sub_base, lane_base = base_ref[0], base_ref[1]

    @pl.when(j == 0)
    def _():
        mask_table[...] = listed_tiles(True, sub_blocks, count_ref, pairs_ref, lane_blocks * sub_blocks)
        sub_table[...] = sub_turns(sub_base, sub_blocks * TILE, sub_poly)

    step_table[...], lane_table[...] = lane_turns(j, sub_base, lane_base, sub_blocks, lane_poly)
    for at in range(sub_blocks):
        rows = slice(at * TILE, (at + 1) * TILE)
        turn = sub_table[rows, :] + step_table[...] + lane_table[at:at + 1, :]
        out_ref[0, rows, :] = edge_parts(turn, mask_table[pl.ds(j * sub_blocks + at, 1), :])


def all_edges(base, count, pairs, lane_blocks, sub_blocks, sub_poly, lane_poly):
    n_sub = sub_blocks * TILE
    return pl.pallas_call(
        functools.partial(edges_kernel, lane_blocks, sub_blocks, sub_poly, lane_poly),
        grid=(lane_blocks,),
        out_shape=jax.ShapeDtypeStruct((lane_blocks, n_sub, 2 * TILE), bf16),
        in_specs=[SMEM, SMEM, VMEM],
        out_specs=pl.BlockSpec((1, n_sub, 2 * TILE), lambda j: (j, 0, 0)),
        scratch_shapes=tables(sub_blocks, lane_blocks),
        compiler_params=pltpu.CompilerParams(vmem_limit_bytes=50 << 20),
        cost_estimate=cost(8 << 30, 1 << 24),
    )(base, count, pairs)


def last_kernel(width, scale, edges_ref, source_ref, out_ref, weight_grad_ref, source_parts):
    @pl.when(pl.program_id(0) == 0)
    def _():
        for l in range(source_ref.shape[0]):
            columns = slice(l * TILE, (l + 1) * TILE)
            source_parts[:width, columns], source_parts[width:, columns] = split(source_ref[l, :width, :])
        weight_grad_ref[...] = unpack(jnp.sum(source_ref[:, width:, :], axis=0))

    total = jnp.dot(source_parts[...], edges_ref[0], preferred_element_type=f32)
    out_ref[...] = fold(total, scale)


def last_product(edges, source, width, scale):
    lane_blocks, n_sub, _ = edges.shape
    rows = 2 * (source.shape[1] - width)
    return pl.pallas_call(
        functools.partial(last_kernel, width, scale),
        grid=(lane_blocks,),
        out_shape=(
            jax.ShapeDtypeStruct((width, lane_blocks * TILE), f32),
            jax.ShapeDtypeStruct((rows, TILE // 2), f32),
        ),
        in_specs=[
            pl.BlockSpec((1, n_sub, 2 * TILE), lambda j: (j, 0, 0)),
            pl.BlockSpec(source.shape, lambda j: (0, 0, 0)),
        ],
        out_specs=(pl.BlockSpec((width, TILE), lambda j: (0, j)), pl.BlockSpec((rows, TILE // 2), lambda j: (0, 0))),
        scratch_shapes=[pltpu.VMEM((2 * width, n_sub), bf16)],
        compiler_params=pltpu.CompilerParams(vmem_limit_bytes=50 << 20),
        cost_estimate=cost(4 << 30, 1 << 24),
    )(edges, source)


def dot3(a, b):
    a_high, a_low = split(a)
    b_high, b_low = split(b)
    product = functools.partial(jnp.dot, preferred_element_type=f32)
    return product(a_high, b_high) + (product(a_high, b_low) + product(a_low, b_high))


def beside(values):
    return jnp.concatenate(values, axis=-1)


def layer_kernel(
    n_x, n_zh, skip, at_ref, hidden_ref, own_ref, other_ref, both_ref,
    act_ref, grad_ref, own_terms_ref, other_terms_ref, weight,
):
    core, zh = at_ref[0], at_ref[1]
    half = own_ref.shape[0]
    packed, rows, width = own_terms_ref.shape[1], 2 * own_terms_ref.shape[1], own_ref.shape[2] // 2
    depth = hidden_ref.shape[0]
    for which, ref in ((core, own_ref), (1 - core, other_ref)):
        for z in range(0, n_zh, 2):
            pair = [ref[:, skip + at * packed:skip + (at + 1) * packed, :] for at in (z, z + 1)]
            wide = [beside([p[..., :width] for p in pair]), beside([p[..., width:] for p in pair])]
            wide = jnp.concatenate(wide, axis=1).reshape(half * rows, 2 * width)
            weight[pl.ds(pl.multiple_of(which * half * rows, 8), half * rows), z * width:(z + 2) * width] = wide
    pairs = []
    for z in range(0, n_zh, 2):
        pair = [both_ref[at, packed:, :] for at in (z, z + 1)]
        pairs.append(jnp.concatenate([beside([p[:, :width] for p in pair]), beside([p[:, width:] for p in pair])], axis=0))
    cotangent = beside(pairs)

    pre = dot3(hidden_ref[...].T, weight[...])
    squash = 1.0 / (1.0 + jnp.exp(-pre))
    activations = pre * squash
    grad_pre = cotangent * squash * (1.0 + pre * (1.0 - squash))
    n_rows = pre.shape[0]
    picked = [weight[pl.ds(pl.multiple_of((x * n_zh + zh) * width, 8), width), :] for x in range(n_x)]
    grad_ref[...] = dot3(jnp.concatenate(picked, axis=0), grad_pre.T).reshape(n_x, width, n_rows)

    for z in range(n_zh):
        columns = slice(z * width, (z + 1) * width)

        @pl.when(zh == z)
        def _():
            act_ref[...] = activations[:, columns]
            for which, ref in ((core, own_terms_ref), (1 - core, other_terms_ref)):
                part = hidden_ref[pl.ds(pl.multiple_of(which * (depth // 2), 8), depth // 2), :]
                ref[...] = pack(dot3(part, grad_pre[:, columns]).reshape(half, rows, width))


def layer(at, hidden_all, own, other, both, n_x, n_zh, rows, skip):
    half = own.shape[0]
    width = own.shape[2] // 2
    n_rows = hidden_all.shape[1]
    terms = jax.ShapeDtypeStruct((half, rows // 2, 2 * width), f32)
    return pl.pallas_call(
        functools.partial(layer_kernel, n_x, n_zh, skip),
        out_shape=(
            jax.ShapeDtypeStruct((n_rows, width), f32),
            jax.ShapeDtypeStruct((n_x, width, n_rows), f32),
            terms, terms,
        ),
        in_specs=[SMEM, VMEM, VMEM, VMEM, VMEM],
        out_specs=(VMEM, VMEM, VMEM, VMEM),
        scratch_shapes=[pltpu.VMEM((2 * half * rows, n_zh * width), f32)],
        compiler_params=pltpu.CompilerParams(vmem_limit_bytes=32 << 20),
        cost_estimate=cost(1 << 30, 1 << 21),
    )(at, hidden_all, own, other, both)


def join_kernel(grad_ref, own_ref, other_ref, out_ref):
    width = grad_ref.shape[1]
    grad = jnp.sum(grad_ref[...], axis=0)
    for n in range(out_ref.shape[0]):
        out_ref[n, :width, :] = grad
    out_ref[:, width:, :] = own_ref[...] + other_ref[...]


def join(grad_terms, own_terms, other_terms):
    n, packed, lanes = own_terms.shape
    return pl.pallas_call(
        join_kernel,
        out_shape=jax.ShapeDtypeStruct((n, grad_terms.shape[1] + packed, lanes), f32),
        in_specs=[VMEM] * 3,
        out_specs=VMEM,
        cost_estimate=cost(1 << 20, 1 << 20),
    )(grad_terms, own_terms, other_terms)


def start_kernel(weight_ref, cotangent_ref, out_ref):
    both = jnp.concatenate([pack(weight_ref[...]), pack(cotangent_ref[...])], axis=0)
    for n in range(out_ref.shape[0]):
        out_ref[n] = both


def start(weight, cotangent, n):
    rows = (weight.shape[0] + cotangent.shape[0]) // 2
    return pl.pallas_call(
        start_kernel,
        out_shape=jax.ShapeDtypeStruct((n, rows, 2 * weight.shape[1]), f32),
        in_specs=[VMEM] * 2,
        out_specs=VMEM,
        cost_estimate=cost(1 << 16, 1 << 18),
    )(weight, cotangent)


def copies(value, n):
    return jnp.broadcast_to(value[None], (n,) + value.shape)


def exchange(value, axes):
    return lax.all_to_all(value, axes, 0, 0)


def per_device(features, tile_list, tile_count, weight, cotangent):
    nbr, feat = ("zl", "y"), ("x", "zh")
    pairs, count = tile_list[0, 0], tile_count[0]
    n_nbr = lax.axis_size(nbr)
    n_x, n_zh = lax.axis_size("x"), lax.axis_size("zh")
    core, nbr_id = lax.axis_index("core"), lax.axis_index(nbr)
    width, c_dev = features.shape
    n_rows = cotangent.shape[0]
    r_dev = n_rows * n_nbr
    scale = (12.0 / (c_dev * n_nbr / 2)) ** 0.5
    row_blocks, col_blocks = r_dev // TILE, c_dev // TILE
    swap_core = [(0, 1), (1, 0)]

    rows_poly, cols_poly = (3, 11), (5, 13)
    packed = weight.shape[0] // 2
    both_z = exchange(start(weight, cotangent, n_zh), "zh")

    bases = jnp.stack([nbr_id * c_dev, core * r_dev]).astype(i32)
    payload = first_product(
        bases, count, pairs, features, row_blocks, col_blocks, cols_poly, rows_poly, scale, width + n_zh * packed
    )
    both_z, payload, later = lax.optimization_barrier((both_z, payload, bases))
    weight_z = both_z[:, :packed].reshape(-1, TILE)
    payload = lax.dynamic_update_slice(payload, copies(weight_z, n_nbr), (0, width, 0))
    own = exchange(payload, nbr)
    edges = all_edges(later[::-1], count, pairs, col_blocks, row_blocks, rows_poly, cols_poly)
    own, edges = lax.optimization_barrier((own, edges))
    hidden = jnp.sum(own[:, :width], axis=0)
    other = lax.ppermute(own, "core", swap_core)
    hidden_z = lax.all_gather(hidden, "zh", axis=0, tiled=True)
    hidden_all = lax.all_gather(hidden_z, "x", axis=0, tiled=True)

    at = jnp.stack([core, lax.axis_index("zh")]).astype(i32)
    activations, grad_terms, own_terms, other_terms = layer(
        at, hidden_all, own, other, both_z, n_x, n_zh, weight.shape[0], width
    )
    other_terms = lax.ppermute(other_terms, "core", swap_core)
    grad_terms = exchange(grad_terms, "x")
    grad_block = exchange(join(grad_terms, own_terms, other_terms), nbr)
    column_part, weight_grad = last_product(edges, grad_block, width, scale)
    feature_grad = column_part + lax.ppermute(column_part, "core", swap_core)
    return activations, feature_grad, weight_grad


def halves(n):
    minor = 1
    while minor * minor < n:
        minor *= 2
    return n // minor, minor


def solution(mesh):
    sizes = (mesh.shape["row"], *halves(mesh.shape["nbr"]), *halves(mesh.shape["feat"]))
    fine = Mesh(mesh.devices.reshape(sizes), ("core", "zl", "y", "x", "zh"))
    nbr, feat = ("zl", "y"), ("x", "zh")
    rows = ("core", *nbr)
    in_specs = (P(feat, nbr), P("core", nbr, None, None), P("core", nbr), P(rows, feat), P(rows, feat))
    out_specs = (P(rows, feat), P(feat, nbr), P(rows, feat))
    return jax.shard_map(per_device, mesh=fine, in_specs=in_specs, out_specs=out_specs, check_vma=False)
```

time: 181 us -> 164 us (0.906)
  starting transfers between devices: 58.2 us -> 40.1 us
  Pallas kernels: 28.4 us -> 45.4 us
  waiting for transfers between devices: 18.1 us -> 8.72 us
  other arithmetic: 5.42 us -> 1.03 us
  local copies, waits for them, and re-layouts: 7.55 us -> 5.5 us
    pallas_call x3 -> x6, Pallas kernels: 28.4 us -> 45.4 us  [the longest x1 14 us: last_product(): pl.pallas_call(functools.partial(last_kernel, width, scale), grid=(lane_b...]
    all_to_all x5 -> x2, waiting for transfers between devices: 18.1 us -> 7.89 us  [exchange(): return lax.all_to_all(value, axes, 0, 0)]
    ppermute x1, starting transfers between devices: 11.9 us -> 3.95 us  [per_device(): feature_grad = column_part + lax.ppermute(column_part, 'core', swap_core)]
    all_to_all x5 -> x2, starting transfers between devices: 26.3 us -> 21.6 us  [exchange(): return lax.all_to_all(value, axes, 0, 0)]
    ppermute x1, starting transfers between devices: 12.6 us -> 8.28 us  [per_device(): other_terms = lax.ppermute(other_terms, 'core', swap_core)]
    all_gather x2, blocking collectives: 25.3 us -> 29.2 us  [the longest x1 19 us: per_device(): hidden_z = lax.all_gather(hidden, 'zh', axis=0, tiled=True)]
    all_to_all x3 -> x0, other arithmetic: 3.7 us -> none  [the longest x2 2.7 us: spread(): lax.all_to_all(jnp.broadcast_to(value[None], (n,) + value.shape), axes, 0...]
    all_to_all x2, blocking collectives: 35.6 us -> 32.1 us  [exchange(): return lax.all_to_all(value, axes, 0, 0)]
  transfers between devices with their start and end apart: 8 -> 5, of which waited for: 3 -> 2; matrix products, arithmetic and copies ran while one was open for 5% -> 1% of each run, Pallas kernels for 13% -> 16%
where the time goes in v3:
time: 164 us; the launch traced here: 163 us
  blocking collectives  61.3 us (37%)
  Pallas kernels  45.4 us (28%)
  starting transfers between devices  40.1 us (24%)
  waiting for transfers between devices  8.72 us (5%)
  local copies, waits for them, and re-layouts  5.5 us (3%)
    all_to_all x2, blocking collectives, exchange(): return lax.all_to_all(value, axes, 0, 0)  32.1 us
    all_to_all x2, starting transfers between devices, exchange(): return lax.all_to_all(value, axes, 0, 0)  21.6 us
    all_gather x1, blocking collectives, per_device(): hidden_z = lax.all_gather(hidden, 'zh', axis=0, tiled=True)  19 us
    pallas_call x1, Pallas kernels, last_product(): pl.pallas_call(functools.partial(last_kernel, width, scale), grid=(lane_b...  14 us
    pallas_call x1, Pallas kernels, all_edges(): pl.pallas_call(functools.partial(edges_kernel, lane_blocks, sub_blocks, s...  13.7 us
    pallas_call x1, Pallas kernels, first_product(): pl.pallas_call(functools.partial(first_kernel, lane_blocks, sub_blocks, s...  11.9 us
    all_gather x1, blocking collectives, per_device(): hidden_all = lax.all_gather(hidden_z, 'x', axis=0, tiled=True)  10.2 us
    ppermute x1, starting transfers between devices, per_device(): other_terms = lax.ppermute(other_terms, 'core', swap_core)  8.28 us
  transfers between devices with their start and end apart: 5, of which 2 were waited for; matrix products, arithmetic and copies ran while one was open for 1% of the time, Pallas kernels for 16%

profile of v3, /device:TPU:1, one launch (start us, length us, event | category | flops | bytes accessed | tf_op | source)
XLA Modules:
  0.0 163.4 jit_solution(6319558137341946062)
XLA Ops:
  0.6 1.5 copy.8.cotangent_ref
  2.1 1.6 shard_map.76
  3.7 15.6 %all-to-all-start = ((f32[4,80,128]{2,1,0:T(8,128)}), f32[4,80,128]{2,1,0:T(8,128)S(1)}, u32[]{:S(2)}, u32[]{:S(2)}) async-start(f32[4,80,128]{2,1,0:T(8,128)} %shard_map.76), calls=%async_computation | async-start | bytes 327680 | tf_op jit(solution)/shard_map/all_to_all | solution.py:313
  20.1 1.0 copy-done.1
  21.1 0.7 copy-done.2
  21.8 11.9 %shard_map.77 = f32[16,128,128]{2,1,0:T(8,128)} custom-call(s32[2]{0:T(128)S(1)} %pad_add_fusion.1.base_ref, s32[1]{0:T(128)} %bitcast.7.count_ref, s32[2,256]{1,0:T(2,128)S(1)} %bitcast.9, f32[64,2048]{1,0:T(8,128)S(1)} %copy-done.1), custom_call_target="tpu_custom_call" | custom-call | flops 8589934592 | bytes 2097152 | tf_op jit(solution)/shard_map/pallas_call | solution.py:125
  33.7 0.8 broadcast_dynamic-update-slice_fusion
  34.6 6.0 %all-to-all-start.1 = ((f32[16,128,128]{2,1,0:T(8,128)}), f32[16,128,128]{2,1,0:T(8,128)S(1)}, u32[]{:S(2)}, u32[]{:S(2)}) async-start(f32[16,128,128]{2,1,0:T(8,128)} %broadcast_dynamic-update-slice_fusion), calls=%async_computation.1 | async-start | bytes 2097152 | tf_op jit(solution)/shard_map/all_to_all | solution.py:313
  40.6 13.7 %shard_map.78.edges_ref = bf16[16,2048,256]{2,1,0:T(8,128)(2,1)} custom-call(s32[2]{0:T(128)S(1)} %rev.3.base_ref, s32[1]{0:T(128)} %bitcast.8.count_ref, s32[2,256]{1,0:T(2,128)S(1)} %bitcast.10), custom_call_target="tpu_custom_call" | custom-call | flops 8589934592 | bytes 16777216 | tf_op jit(solution)/shard_map/pallas_call | solution.py:157
  54.3 7.9 %all-to-all-done.1.own_ref = f32[16,128,128]{2,1,0:T(8,128)S(1)} async-done(((f32[16,128,128]{2,1,0:T(8,128)}), f32[16,128,128]{2,1,0:T(8,128)S(1)}, u32[]{:S(2)}, u32[]{:S(2)}) %all-to-all-start.1) | async-done | bytes 1048608 | tf_op jit(solution)/shard_map/all_to_all | solution.py:313
  62.2 6.2 %collective-permute-start = (f32[16,128,128]{2,1,0:T(8,128)S(1)}, f32[16,128,128]{2,1,0:T(8,128)S(1)}, u32[]{:S(2)}, u32[]{:S(2)}) collective-permute-start(f32[16,128,128]{2,1,0:T(8,128)S(1)} %all-to-all-done.1.own_ref), channel_id=1, source_target_pairs={{0,256},{256,0},{1,257},{257,1},{2,258},{258,2},{3,259},{259,3},{4... | collective-permute-start | bytes 3145736 | tf_op jit(solution)/shard_map/ppermute | solution.py:344
  68.6 19.0 %all_gather.6 = f32[256,128]{1,0:T(8,128)S(1)} all-gather(f32[64,128]{1,0:T(8,128)S(1)} %slice_reduce_fusion), channel_id=1, replica_groups=mesh['core'=2,'zl'=4,'y'=4,'x'=4,'zh'=4] {'zh'}, dimensions={0}, use_global_device_ids=true | all-gather | bytes 163840 | tf_op jit(solution)/shard_map/all_gather | solution.py:345
  87.5 10.2 %all_gather.7.hidden_ref = f32[1024,128]{1,0:T(8,128)S(1)} all-gather(f32[256,128]{1,0:T(8,128)S(1)} %all_gather.6), channel_id=1, replica_groups=mesh['core'=2,'zl'=4,'y'=4,'x'=4,'zh'=4] {'x'}, dimensions={0}, use_global_device_ids=true | all-gather | bytes 655360 | tf_op jit(solution)/shard_map/all_gather | solution.py:346
  97.8 2.2 %shard_map.79 = (f32[128,64]{1,0:T(8,128)S(1)}, f32[4,64,128]{2,1,0:T(8,128)S(1)}, f32[16,16,128]{2,1,0:T(8,128)S(1)}, f32[16,16,128]{2,1,0:T(8,128)S(1)}) custom-call(s32[2]{0:T(128)S(1)} %pad_add_fusion.at_ref, f32[1024,128]{1,0:T(8,128)S(1)} %all_gather.7.hidden_ref, f32[16,128,128]{2,1,0:T(8,128)S(1)} %all-to-all-done.1.own_ref, ...), custom_call_target="tpu_custom_call" | custom-call | flops 1073741824 | bytes 2097152 | tf_op jit(solution)/shard_map/pallas_call | solution.py:257
  100.0 8.3 %collective-permute-start.1 = (f32[16,16,128]{2,1,0:T(8,128)S(1)}, f32[16,16,128]{2,1,0:T(8,128)S(1)}, u32[]{:S(2)}, u32[]{:S(2)}) collective-permute-start(f32[16,16,128]{2,1,0:T(8,128)S(1)} %get-tuple-element.22), channel_id=1, source_target_pairs={{0,256},{256,0},{1,257},{257,1},{2,258},{258,2},{3,259},{259,3},{4... | collective-permute-start | bytes 393224 | tf_op jit(solution)/shard_map/ppermute | solution.py:352
  108.3 7.9 %all_to_all.20.grad_ref = f32[4,64,128]{2,1,0:T(8,128)} all-to-all(f32[4,64,128]{2,1,0:T(8,128)S(1)} %get-tuple-element.20), channel_id=1, replica_groups=mesh['core'=2,'zl'=4,'y'=4,'x'=4,'zh'=4] {'x'}, dimensions={0} | all-to-all | bytes 262144 | tf_op jit(solution)/shard_map/all_to_all | solution.py:313
  116.3 0.6 copy-done.4
  116.9 1.9 %shard_map.80 = f32[16,80,128]{2,1,0:T(8,128)} custom-call(f32[4,64,128]{2,1,0:T(8,128)} %all_to_all.20.grad_ref, f32[16,16,128]{2,1,0:T(8,128)} %copy-done, f32[16,16,128]{2,1,0:T(8,128)} %copy-done.4), custom_call_target="tpu_custom_call" | custom-call | flops 1048576 | bytes 1048576 | tf_op jit(solution)/shard_map/pallas_call | solution.py:282
  118.8 24.2 %all_to_all.21.source_ref = f32[16,80,128]{2,1,0:T(8,128)S(1)} all-to-all(f32[16,80,128]{2,1,0:T(8,128)} %shard_map.80), channel_id=1, replica_groups=mesh['core'=2,'zl'=4,'y'=4,'x'=4,'zh'=4] {'zl','y'}, dimensions={0} | all-to-all | bytes 1310720 | tf_op jit(solution)/shard_map/all_to_all | solution.py:313
  143.0 14.0 %shard_map.81 = (f32[64,2048]{1,0:T(8,128)S(1)}, f32[32,64]{1,0:T(8,128)}) custom-call(bf16[16,2048,256]{2,1,0:T(8,128)(2,1)} %shard_map.78.edges_ref, f32[16,80,128]{2,1,0:T(8,128)S(1)} %all_to_all.21.source_ref), custom_call_target="tpu_custom_call" | custom-call | flops 4294967296 | bytes 16777216 | tf_op jit(solution)/shard_map/pallas_call | solution.py:184
  157.0 3.9 %collective-permute-start.2 = (f32[64,2048]{1,0:T(8,128)S(1)}, f32[64,2048]{1,0:T(8,128)S(1)}, u32[]{:S(2)}, u32[]{:S(2)}) collective-permute-start(f32[64,2048]{1,0:T(8,128)S(1)} %get-tuple-element.23), channel_id=1, source_target_pairs={{0,256},{256,0},{1,257},{257,1},{2,258},{258,2},{3,259},{259,3},{4... | collective-permute-start | bytes 1572872 | tf_op jit(solution)/shard_map/ppermute | solution.py:356
  161.0 0.7 copy.9
  161.7 0.8 collective-permute-done.2
  162.5 0.8 add.7
  (15 shorter events, 0.3 us)
Async XLA Ops:
  3.7 30.0 %all-to-all-start = ((f32[4,80,128]{2,1,0:T(8,128)}), f32[4,80,128]{2,1,0:T(8,128)S(1)}, u32[]{:S(2)}, u32[]{:S(2)}) async-start(f32[4,80,128]{2,1,0:T(8,128)} %shard_map.76), calls=%async_computation | async-start | bytes 327680 | tf_op jit(solution)/shard_map/all_to_all | solution.py:313
  20.1 1.0 copy-start.1
  21.1 0.7 copy-start.2
  21.8 18.8 %copy-start.3 = (s32[1,1,2,256]{3,2,1,0:T(2,128)S(1)}, s32[1,1,2,256]{3,2,1,0:T(2,128)}, u32[]{:S(2)}) copy-start(s32[1,1,2,256]{3,2,1,0:T(2,128)} %param.6) | copy-start | bytes 6148
  34.6 27.6 %all-to-all-start.1 = ((f32[16,128,128]{2,1,0:T(8,128)}), f32[16,128,128]{2,1,0:T(8,128)S(1)}, u32[]{:S(2)}, u32[]{:S(2)}) async-start(f32[16,128,128]{2,1,0:T(8,128)} %broadcast_dynamic-update-slice_fusion), calls=%async_computation.1 | async-start | bytes 2097152 | tf_op jit(solution)/shard_map/all_to_all | solution.py:313
  62.2 35.6 %collective-permute-start = (f32[16,128,128]{2,1,0:T(8,128)S(1)}, f32[16,128,128]{2,1,0:T(8,128)S(1)}, u32[]{:S(2)}, u32[]{:S(2)}) collective-permute-start(f32[16,128,128]{2,1,0:T(8,128)S(1)} %all-to-all-done.1.own_ref), channel_id=1, source_target_pairs={{0,256},{256,0},{1,257},{257,1},{2,258},{258,2},{3,259},{259,3},{4... | collective-permute-start | bytes 3145736 | tf_op jit(solution)/shard_map/ppermute | solution.py:344
  100.0 16.2 %copy-start = (f32[16,16,128]{2,1,0:T(8,128)}, f32[16,16,128]{2,1,0:T(8,128)S(1)}, u32[]{:S(2)}) copy-start(f32[16,16,128]{2,1,0:T(8,128)S(1)} %get-tuple-element.21.own_ref) | copy-start | bytes 393220
  100.0 16.2 %collective-permute-start.1 = (f32[16,16,128]{2,1,0:T(8,128)S(1)}, f32[16,16,128]{2,1,0:T(8,128)S(1)}, u32[]{:S(2)}, u32[]{:S(2)}) collective-permute-start(f32[16,16,128]{2,1,0:T(8,128)S(1)} %get-tuple-element.22), channel_id=1, source_target_pairs={{0,256},{256,0},{1,257},{257,1},{2,258},{258,2},{3,259},{259,3},{4... | collective-permute-start | bytes 393224 | tf_op jit(solution)/shard_map/ppermute | solution.py:352
  116.2 0.7 copy-start.4
  157.0 5.5 %collective-permute-start.2 = (f32[64,2048]{1,0:T(8,128)S(1)}, f32[64,2048]{1,0:T(8,128)S(1)}, u32[]{:S(2)}, u32[]{:S(2)}) collective-permute-start(f32[64,2048]{1,0:T(8,128)S(1)} %get-tuple-element.23), channel_id=1, source_target_pairs={{0,256},{256,0},{1,257},{257,1},{2,258},{258,2},{3,259},{259,3},{4... | collective-permute-start | bytes 1572872 | tf_op jit(solution)/shard_map/ppermute | solution.py:356

commit v4 on v3

v4 whole, which is shorter than its diff:
```python
import functools

import jax
import jax.numpy as jnp
from jax import lax
from jax.experimental import pallas as pl
from jax.experimental.pallas import tpu as pltpu
from jax.sharding import Mesh
from jax.sharding import PartitionSpec as P

TILE = 128
MODULUS = 32749
INVERSE = 1.0 / MODULUS
WHOLE = 2**32 // MODULUS
PART = 2**32 / MODULUS - WHOLE
TURN = 2.0**32
OFFSET = 64 - 2**31
f32, bf16, i32 = jnp.float32, jnp.bfloat16, jnp.int32


def residue(value):
    quotient = (value.astype(f32) * INVERSE).astype(i32)
    rest = value - quotient * MODULUS
    rest = jnp.where(rest < 0, rest + MODULUS, rest)
    return jnp.where(rest >= MODULUS, rest - MODULUS, rest)


def turns(value):
    rest = residue(value)
    return rest * WHOLE + (rest.astype(f32) * PART + 0.5).astype(i32)


def split(value):
    high = value.astype(bf16)
    return high, (value - high.astype(f32)).astype(bf16)


def pack(value):
    n = value.shape[-2] // 2
    return jnp.concatenate([value[..., :n, :], value[..., n:, :]], axis=-1)


def unpack(value):
    width = value.shape[-1] // 2
    return jnp.concatenate([value[..., :width], value[..., width:]], axis=-2)


def listed_tiles(swap, sub_blocks, count_ref, pairs_ref, tiles):
    slots = pairs_ref.shape[1]
    major, minor = (pairs_ref[1:2, :], pairs_ref[0:1, :]) if swap else (pairs_ref[0:1, :], pairs_ref[1:2, :])
    code = major * sub_blocks + minor
    code = jnp.where(lax.broadcasted_iota(i32, (1, slots), 1) < count_ref[0], code, -1)
    listed = (lax.broadcasted_iota(i32, (tiles, slots), 0) == code).astype(f32)
    return jnp.broadcast_to(jnp.sum(listed, axis=1, keepdims=True), (tiles, TILE))


def sub_turns(sub_base, sub_blocks, sub_poly):
    shape = (TILE, TILE)
    sub = sub_base + TILE * lax.broadcasted_iota(i32, shape, 0) + lax.broadcasted_iota(i32, shape, 1)
    columns = turns(sub * residue(sub_poly[0] * sub + sub_poly[1])).T
    return [jnp.broadcast_to(columns[:, l:l + 1], shape) for l in range(sub_blocks)]


def lane_turns(j, sub_base, lane_base, sub_blocks, lane_poly):
    lane = lane_base + j * TILE + lax.broadcasted_iota(i32, (sub_blocks, TILE), 1)
    first = sub_base + TILE * lax.broadcasted_iota(i32, (sub_blocks, TILE), 0)
    inner = residue(lane_poly[0] * lane + lane_poly[1] + 7 * first)
    return turns(lane * inner) + OFFSET


def step_turns(lane_base):
    lane = lane_base + lax.broadcasted_iota(i32, (TILE, TILE), 1)
    k = lax.broadcasted_iota(i32, (TILE, TILE), 0)
    return turns(7 * k * lane), turns(7 * TILE * k)


def fold(total, scale):
    width = total.shape[0] // 2
    total = total[:, :TILE] + total[:, TILE:]
    return (total[:width] + total[width:]) * scale


def product_kernel(
    lane_blocks, sub_blocks, swap, sub_poly, lane_poly, scale, width,
    base_ref, count_ref, pairs_ref, source_ref, out_ref, *refs,
):
    sub_table, step_table, growth_table, lane_table, mask_table, source_parts = refs[-6:]
    sub_base, lane_base = base_ref[0], base_ref[1]
    mask_table[...] = listed_tiles(swap, sub_blocks, count_ref, pairs_ref, lane_blocks * sub_blocks)
    for l, table in enumerate(sub_turns(sub_base, sub_blocks, sub_poly)):
        columns = slice(l * TILE, (l + 1) * TILE)
        sub_table[columns, :] = table
        piece = source_ref[l, :width, :] if swap else source_ref[:, columns]
        source_parts[:width, columns], source_parts[width:, columns] = split(piece)
    if swap:
        refs[0][...] = unpack(jnp.sum(source_ref[:, width:, :], axis=0))

    step_table[...], growth_table[...] = step_turns(lane_base)

    def block(j, carry):
        lane_table[...] = lane_turns(j, sub_base, lane_base, sub_blocks, lane_poly)
        total = jnp.zeros((2 * width, 2 * TILE), f32)
        for l in range(0, sub_blocks, 2):
            lhs, rhs = [], []
            for at in (l, l + 1):
                columns = slice(at * TILE, (at + 1) * TILE)
                turn = sub_table[columns, :] + step_table[...] + lane_table[at:at + 1, :]
                rhs.append(jnp.concatenate(split(turn.astype(f32)), axis=1))
                listed = jnp.broadcast_to(mask_table[pl.ds(j * sub_blocks + at, 1), :], (2 * width, TILE)).astype(bf16)
                lhs.append(source_parts[:, columns] * listed)
            total += jnp.dot(
                jnp.concatenate(lhs, axis=1), jnp.concatenate(rhs, axis=0), preferred_element_type=f32
            )
        step_table[...] += growth_table[...]
        result = fold(total, scale / TURN)
        if swap:
            out_ref[:, pl.ds(pl.multiple_of(j * TILE, TILE), TILE)] = result
        else:
            out_ref[j] = result
        return carry

    lax.fori_loop(0, lane_blocks, block, 0, unroll=4)


SMEM, VMEM = pl.BlockSpec(memory_space=pltpu.SMEM), pl.BlockSpec(memory_space=pltpu.VMEM)


def cost(flops, traffic):
    return pl.CostEstimate(flops=flops, bytes_accessed=traffic, transcendentals=0)


def edge_product(base, count, pairs, source, lane_blocks, sub_blocks, swap, sub_poly, lane_poly, scale, width):
    out = jax.ShapeDtypeStruct((lane_blocks, width, TILE), f32)
    if swap:
        out = (
            jax.ShapeDtypeStruct((width, lane_blocks * TILE), f32),
            jax.ShapeDtypeStruct((2 * (source.shape[1] - width), TILE // 2), f32),
        )
    return pl.pallas_call(
        functools.partial(product_kernel, lane_blocks, sub_blocks, swap, sub_poly, lane_poly, scale, width),
        out_shape=out,
        in_specs=[SMEM, SMEM, VMEM, VMEM],
        out_specs=(VMEM, VMEM) if swap else VMEM,
        scratch_shapes=[
            pltpu.VMEM((sub_blocks * TILE, TILE), i32),
            pltpu.VMEM((TILE, TILE), i32),
            pltpu.VMEM((TILE, TILE), i32),
            pltpu.VMEM((sub_blocks, TILE), i32),
            pltpu.VMEM((lane_blocks * sub_blocks, TILE), f32),
            pltpu.VMEM((2 * width, sub_blocks * TILE), bf16),
        ],
        compiler_params=pltpu.CompilerParams(vmem_limit_bytes=24 << 20),
        cost_estimate=cost(8 << 30, 1 << 21),
    )(base, count, pairs, source)


def dot3(a, b):
    a_high, a_low = split(a)
    b_high, b_low = split(b)
    product = functools.partial(jnp.dot, preferred_element_type=f32)
    return product(a_high, b_high) + (product(a_high, b_low) + product(a_low, b_high))


def beside(values):
    return jnp.concatenate(values, axis=-1)


def layer_kernel(
    n_x, n_zh, at_ref, hidden_ref, own_ref, other_ref, both_ref,
    act_ref, grad_ref, own_terms_ref, other_terms_ref, weight,
):
    core, zh = at_ref[0], at_ref[1]
    half = own_ref.shape[0]
    packed, rows, width = own_terms_ref.shape[1], 2 * own_terms_ref.shape[1], own_ref.shape[2] // 2
    depth = hidden_ref.shape[0]
    for which, ref in ((core, own_ref), (1 - core, other_ref)):
        for z in range(0, n_zh, 2):
            pair = [ref[:, at * packed:(at + 1) * packed, :] for at in (z, z + 1)]
            wide = [beside([p[..., :width] for p in pair]), beside([p[..., width:] for p in pair])]
            wide = jnp.concatenate(wide, axis=1).reshape(half * rows, 2 * width)
            weight[pl.ds(pl.multiple_of(which * half * rows, 8), half * rows), z * width:(z + 2) * width] = wide
    pairs = []
    for z in range(0, n_zh, 2):
        pair = [both_ref[at, packed:, :] for at in (z, z + 1)]
        pairs.append(jnp.concatenate([beside([p[:, :width] for p in pair]), beside([p[:, width:] for p in pair])], axis=0))
    cotangent = beside(pairs)

    pre = dot3(hidden_ref[...].T, weight[...])
    squash = 1.0 / (1.0 + jnp.exp(-pre))
    activations = pre * squash
    grad_pre = cotangent * squash * (1.0 + pre * (1.0 - squash))
    n_rows = pre.shape[0]
    picked = [weight[pl.ds(pl.multiple_of((x * n_zh + zh) * width, 8), width), :] for x in range(n_x)]
    grad_ref[...] = dot3(jnp.concatenate(picked, axis=0), grad_pre.T).reshape(n_x, width, n_rows)

    for z in range(n_zh):
        columns = slice(z * width, (z + 1) * width)

        @pl.when(zh == z)
        def _():
            act_ref[...] = activations[:, columns]
            for which, ref in ((core, own_terms_ref), (1 - core, other_terms_ref)):
                part = hidden_ref[pl.ds(pl.multiple_of(which * (depth // 2), 8), depth // 2), :]
                ref[...] = pack(dot3(part, grad_pre[:, columns]).reshape(half, rows, width))


def layer(at, hidden_all, own, other, both, n_x, n_zh, rows):
    half = own.shape[0]
    width = own.shape[2] // 2
    n_rows = hidden_all.shape[1]
    terms = jax.ShapeDtypeStruct((half, rows // 2, 2 * width), f32)
    return pl.pallas_call(
        functools.partial(layer_kernel, n_x, n_zh),
        out_shape=(
            jax.ShapeDtypeStruct((n_rows, width), f32),
            jax.ShapeDtypeStruct((n_x, width, n_rows), f32),
            terms, terms,
        ),
        in_specs=[SMEM, VMEM, VMEM, VMEM, VMEM],
        out_specs=(VMEM, VMEM, VMEM, VMEM),
        scratch_shapes=[pltpu.VMEM((2 * half * rows, n_zh * width), f32)],
        compiler_params=pltpu.CompilerParams(vmem_limit_bytes=32 << 20),
        cost_estimate=cost(1 << 30, 1 << 21),
    )(at, hidden_all, own, other, both)


def join_kernel(grad_ref, own_ref, other_ref, out_ref):
    width = grad_ref.shape[1]
    grad = jnp.sum(grad_ref[...], axis=0)
    for n in range(out_ref.shape[0]):
        out_ref[n, :width, :] = grad
    out_ref[:, width:, :] = own_ref[...] + other_ref[...]


def join(grad_terms, own_terms, other_terms):
    n, packed, lanes = own_terms.shape
    return pl.pallas_call(
        join_kernel,
        out_shape=jax.ShapeDtypeStruct((n, grad_terms.shape[1] + packed, lanes), f32),
        in_specs=[VMEM] * 3,
        out_specs=VMEM,
        cost_estimate=cost(1 << 20, 1 << 20),
    )(grad_terms, own_terms, other_terms)


def start_kernel(weight_ref, cotangent_ref, out_ref):
    both = jnp.concatenate([pack(weight_ref[...]), pack(cotangent_ref[...])], axis=0)
    for n in range(out_ref.shape[0]):
        out_ref[n] = both


def start(weight, cotangent, n):
    rows = (weight.shape[0] + cotangent.shape[0]) // 2
    return pl.pallas_call(
        start_kernel,
        out_shape=jax.ShapeDtypeStruct((n, rows, 2 * weight.shape[1]), f32),
        in_specs=[VMEM] * 2,
        out_specs=VMEM,
        cost_estimate=cost(1 << 16, 1 << 18),
    )(weight, cotangent)


def copies(value, n):
    return jnp.broadcast_to(value[None], (n,) + value.shape)


def exchange(value, axes):
    return lax.all_to_all(value, axes, 0, 0)


def per_device(features, tile_list, tile_count, weight, cotangent):
    nbr, feat = ("zl", "y"), ("x", "zh")
    pairs, count = tile_list[0, 0], tile_count[0]
    n_nbr = lax.axis_size(nbr)
    n_x, n_zh = lax.axis_size("x"), lax.axis_size("zh")
    core, nbr_id = lax.axis_index("core"), lax.axis_index(nbr)
    width, c_dev = features.shape
    n_rows = cotangent.shape[0]
    r_dev = n_rows * n_nbr
    scale = (12.0 / (c_dev * n_nbr / 2)) ** 0.5
    row_blocks, col_blocks = r_dev // TILE, c_dev // TILE
    swap_core = [(0, 1), (1, 0)]

    rows_poly, cols_poly = (3, 11), (5, 13)
    packed = weight.shape[0] // 2
    both_z = exchange(start(weight, cotangent, n_zh), "zh")

    bases = jnp.stack([nbr_id * c_dev, core * r_dev]).astype(i32)
    partial = edge_product(
        bases, count, pairs, features, row_blocks, col_blocks, False, cols_poly, rows_poly, scale, width
    )
    both_z, partial = lax.optimization_barrier((both_z, partial))
    weight_z = both_z[:, :packed].reshape(-1, TILE)
    hidden = jnp.sum(exchange(partial, nbr), axis=0)
    hidden, weight_z = lax.optimization_barrier((hidden, copies(weight_z, n_nbr)))
    own = exchange(weight_z, nbr)
    hidden_z = lax.all_gather(hidden, "zh", axis=0, tiled=True)
    hidden_z, own = lax.optimization_barrier((hidden_z, own))
    other = lax.ppermute(own, "core", swap_core)
    hidden_all = lax.all_gather(hidden_z, "x", axis=0, tiled=True)

    at = jnp.stack([core, lax.axis_index("zh")]).astype(i32)
    activations, grad_terms, own_terms, other_terms = layer(
        at, hidden_all, own, other, both_z, n_x, n_zh, weight.shape[0]
    )
    other_terms = lax.ppermute(other_terms, "core", swap_core)
    grad_terms = exchange(grad_terms, "x")
    grad_block = exchange(join(grad_terms, own_terms, other_terms), nbr)
    column_part, weight_grad = edge_product(
        bases[::-1], count, pairs, grad_block, col_blocks, row_blocks, True, rows_poly, cols_poly, scale, width
    )
    feature_grad = column_part + lax.ppermute(column_part, "core", swap_core)
    return activations, feature_grad, weight_grad


def halves(n):
    minor = 1
    while minor * minor < n:
        minor *= 2
    return n // minor, minor


def solution(mesh):
    sizes = (mesh.shape["row"], *halves(mesh.shape["nbr"]), *halves(mesh.shape["feat"]))
    fine = Mesh(mesh.devices.reshape(sizes), ("core", "zl", "y", "x", "zh"))
    nbr, feat = ("zl", "y"), ("x", "zh")
    rows = ("core", *nbr)
    in_specs = (P(feat, nbr), P("core", nbr, None, None), P("core", nbr), P(rows, feat), P(rows, feat))
    out_specs = (P(rows, feat), P(feat, nbr), P(rows, feat))
    return jax.shard_map(per_device, mesh=fine, in_specs=in_specs, out_specs=out_specs, check_vma=False)
```

time: 164 us -> 154 us (0.939)
  Pallas kernels: 45.4 us -> 19.5 us
  waiting for transfers between devices: 8.72 us -> 31.6 us
  blocking collectives: 61.3 us -> 39 us
  starting transfers between devices: 40.1 us -> 56.2 us
    pallas_call x4 -> x3, Pallas kernels: 41.8 us -> 16 us  [the longest x2 13.8 us: edge_product(): pl.pallas_call(functools.partial(product_kernel, lane_blocks, sub_blocks,...]
    all_to_all x2 -> x1, blocking collectives: 32.1 us -> 8.57 us  [exchange(): return lax.all_to_all(value, axes, 0, 0)]
    all_to_all x2 -> x4, waiting for transfers between devices: 7.89 us -> 30.8 us  [exchange(): return lax.all_to_all(value, axes, 0, 0)]
    all_to_all x2 -> x4, starting transfers between devices: 21.6 us -> 39.6 us  [exchange(): return lax.all_to_all(value, axes, 0, 0)]
    ppermute x1, starting transfers between devices: 8.28 us -> 4.42 us  [per_device(): other_terms = lax.ppermute(other_terms, 'core', swap_core)]
    unnamed x12 -> x14, local copies, waits for them, and re-layouts: 4.56 us -> 3.59 us
  transfers between devices with their start and end apart: 5 -> 7, of which waited for: 2 -> 4; matrix products, arithmetic and copies ran while one was open for 1% -> 1% of each run, Pallas kernels for 16% -> 5%
where the time goes in v4:
time: 154 us; the launch traced here: 153 us
  starting transfers between devices  56.2 us (36%)
  blocking collectives  39 us (25%)
  waiting for transfers between devices  31.6 us (21%)
  Pallas kernels  19.5 us (13%)
  local copies, waits for them, and re-layouts  4.53 us (3%)
    all_to_all x4, starting transfers between devices, exchange(): return lax.all_to_all(value, axes, 0, 0)  39.6 us
    all_to_all x4, waiting for transfers between devices, exchange(): return lax.all_to_all(value, axes, 0, 0)  30.8 us
    all_gather x1, blocking collectives, per_device(): hidden_z = lax.all_gather(hidden, 'zh', axis=0, tiled=True)  19.4 us
    pallas_call x2, Pallas kernels, edge_product(): pl.pallas_call(functools.partial(product_kernel, lane_blocks, sub_blocks,...  13.8 us
    all_gather x1, blocking collectives, per_device(): hidden_all = lax.all_gather(hidden_z, 'x', axis=0, tiled=True)  11 us
    all_to_all x1, blocking collectives, exchange(): return lax.all_to_all(value, axes, 0, 0)  8.57 us
    ppermute x1, starting transfers between devices, per_device(): other = lax.ppermute(own, 'core', swap_core)  6.76 us
    ppermute x1, starting transfers between devices, per_device(): feature_grad = column_part + lax.ppermute(column_part, 'core', swap_core)  5.34 us
  transfers between devices with their start and end apart: 7, of which 4 were waited for; matrix products, arithmetic and copies ran while one was open for 1% of the time, Pallas kernels for 5%

profile of v4, /device:TPU:1, one launch (start us, length us, event | category | flops | bytes accessed | tf_op | source)
XLA Modules:
  0.0 153.3 jit_solution(124625326973510728)
XLA Ops:
  0.6 1.5 %copy.8.cotangent_ref = f32[128,64]{1,0:T(8,128)} copy(f32[128,64]{0,1:T(8,128)} %param.9) | data formatting | bytes 65536 | tf_op args[4]
  2.2 1.6 %shard_map.76 = f32[4,80,128]{2,1,0:T(8,128)} custom-call(f32[32,64]{1,0:T(8,128)} %weight_ref.1, f32[128,64]{1,0:T(8,128)} %copy.8.cotangent_ref), custom_call_target="tpu_custom_call" | custom-call | flops 65536 | bytes 262144 | tf_op jit(solution)/shard_map/pallas_call | solution.py:254
  3.8 15.6 %all-to-all-start = ((f32[4,80,128]{2,1,0:T(8,128)}), f32[4,80,128]{2,1,0:T(8,128)S(1)}, u32[]{:S(2)}, u32[]{:S(2)}) async-start(f32[4,80,128]{2,1,0:T(8,128)} %shard_map.76), calls=%async_computation | async-start | bytes 327680 | tf_op jit(solution)/shard_map/all_to_all | solution.py:268
  20.2 0.7 copy-done.4
  20.8 7.3 %shard_map.77 = f32[16,64,128]{2,1,0:T(8,128)} custom-call(s32[2]{0:T(128)S(1)} %pad_add_fusion.1.base_ref, s32[1]{0:T(128)} %bitcast.7.count_ref, s32[2,256]{1,0:T(2,128)S(1)} %bitcast.10, f32[64,2048]{1,0:T(8,128)S(1)} %copy-done.3), custom_call_target="tpu_custom_call" | custom-call | flops 8589934592 | bytes 2097152 | tf_op jit(solution)/shard_map/pallas_call | solution.py:139
  28.1 3.9 %all-to-all-done.both_ref = f32[4,80,128]{2,1,0:T(8,128)S(1)} async-done(((f32[4,80,128]{2,1,0:T(8,128)}), f32[4,80,128]{2,1,0:T(8,128)S(1)}, u32[]{:S(2)}, u32[]{:S(2)}) %all-to-all-start) | async-done | bytes 163872 | tf_op jit(solution)/shard_map/all_to_all | solution.py:268
  32.0 7.8 %all-to-all-start.1 = ((f32[16,64,128]{2,1,0:T(8,128)}), f32[16,64,128]{2,1,0:T(8,128)S(1)}, u32[]{:S(2)}, u32[]{:S(2)}) async-start(f32[16,64,128]{2,1,0:T(8,128)} %shard_map.77), calls=%async_computation.1 | async-start | bytes 1048576 | tf_op jit(solution)/shard_map/all_to_all | solution.py:268
  39.8 11.7 %all-to-all-done.1 = f32[16,64,128]{2,1,0:T(8,128)S(1)} async-done(((f32[16,64,128]{2,1,0:T(8,128)}), f32[16,64,128]{2,1,0:T(8,128)S(1)}, u32[]{:S(2)}, u32[]{:S(2)}) %all-to-all-start.1) | async-done | bytes 524320 | tf_op jit(solution)/shard_map/all_to_all | solution.py:268
  51.6 0.8 broadcast_in_dim.8
  52.4 6.8 %all-to-all-start.2 = ((f32[16,64,128]{2,1,0:T(8,128)}), f32[16,64,128]{2,1,0:T(8,128)S(1)}, u32[]{:S(2)}, u32[]{:S(2)}) async-start(f32[16,64,128]{2,1,0:T(8,128)} %broadcast_in_dim.8), calls=%async_computation.2 | async-start | bytes 1048576 | tf_op jit(solution)/shard_map/all_to_all | solution.py:268
  59.2 19.4 %all_gather.6 = f32[256,128]{1,0:T(8,128)S(1)} all-gather(f32[64,128]{1,0:T(8,128)S(1)} %reduce_sum.9), channel_id=1, replica_groups=mesh['core'=2,'zl'=4,'y'=4,'x'=4,'zh'=4] {'zh'}, dimensions={0}, use_global_device_ids=true | all-gather | bytes 163840 | tf_op jit(solution)/shard_map/all_gather | solution.py:297
  78.6 6.8 %collective-permute-start = (f32[16,64,128]{2,1,0:T(8,128)S(1)}, f32[16,64,128]{2,1,0:T(8,128)S(1)}, u32[]{:S(2)}, u32[]{:S(2)}) collective-permute-start(f32[16,64,128]{2,1,0:T(8,128)S(1)} %all-to-all-done.2.own_ref), channel_id=1, source_target_pairs={{0,256},{256,0},{1,257},{257,1},{2,258},{258,2},{3,259},{259,3},{4... | collective-permute-start | bytes 1572872 | tf_op jit(solution)/shard_map/ppermute | solution.py:299
  85.5 11.0 %all_gather.7.hidden_ref = f32[1024,128]{1,0:T(8,128)S(1)} all-gather(f32[256,128]{1,0:T(8,128)S(1)} %all_gather.6), channel_id=1, replica_groups=mesh['core'=2,'zl'=4,'y'=4,'x'=4,'zh'=4] {'x'}, dimensions={0}, use_global_device_ids=true | all-gather | bytes 655360 | tf_op jit(solution)/shard_map/all_gather | solution.py:300
  96.5 2.2 %shard_map.78 = (f32[128,64]{1,0:T(8,128)S(1)}, f32[4,64,128]{2,1,0:T(8,128)S(1)}, f32[16,16,128]{2,1,0:T(8,128)S(1)}, f32[16,16,128]{2,1,0:T(8,128)S(1)}) custom-call(s32[2]{0:T(128)S(1)} %pad_add_fusion.at_ref, f32[1024,128]{1,0:T(8,128)S(1)} %all_gather.7.hidden_ref, f32[16,64,128]{2,1,0:T(8,128)S(1)} %all-to-all-done.2.own_ref, ...), custom_call_target="tpu_custom_call" | custom-call | flops 1073741824 | bytes 2097152 | tf_op jit(solution)/shard_map/pallas_call | solution.py:212
  98.8 4.4 %collective-permute-start.1 = (f32[16,16,128]{2,1,0:T(8,128)S(1)}, f32[16,16,128]{2,1,0:T(8,128)S(1)}, u32[]{:S(2)}, u32[]{:S(2)}) collective-permute-start(f32[16,16,128]{2,1,0:T(8,128)S(1)} %get-tuple-element.24), channel_id=1, source_target_pairs={{0,256},{256,0},{1,257},{257,1},{2,258},{258,2},{3,259},{259,3},{4... | collective-permute-start | bytes 393224 | tf_op jit(solution)/shard_map/ppermute | solution.py:306
  103.2 8.6 %all_to_all.25.grad_ref = f32[4,64,128]{2,1,0:T(8,128)} all-to-all(f32[4,64,128]{2,1,0:T(8,128)S(1)} %get-tuple-element.22), channel_id=1, replica_groups=mesh['core'=2,'zl'=4,'y'=4,'x'=4,'zh'=4] {'x'}, dimensions={0} | all-to-all | bytes 262144 | tf_op jit(solution)/shard_map/all_to_all | solution.py:268
  112.4 1.9 %shard_map.79 = f32[16,80,128]{2,1,0:T(8,128)} custom-call(f32[4,64,128]{2,1,0:T(8,128)} %all_to_all.25.grad_ref, f32[16,16,128]{2,1,0:T(8,128)} %copy-done.2, f32[16,16,128]{2,1,0:T(8,128)} %copy-done.5), custom_call_target="tpu_custom_call" | custom-call | flops 1048576 | bytes 1048576 | tf_op jit(solution)/shard_map/pallas_call | solution.py:237
  114.3 9.5 %all-to-all-start.4 = ((f32[16,80,128]{2,1,0:T(8,128)}), f32[16,80,128]{2,1,0:T(8,128)S(1)}, u32[]{:S(2)}, u32[]{:S(2)}) async-start(f32[16,80,128]{2,1,0:T(8,128)} %shard_map.79), calls=%async_computation.4 | async-start | bytes 1310720 | tf_op jit(solution)/shard_map/all_to_all | solution.py:268
  123.9 15.2 %all-to-all-done.4.source_ref = f32[16,80,128]{2,1,0:T(8,128)S(1)} async-done(((f32[16,80,128]{2,1,0:T(8,128)}), f32[16,80,128]{2,1,0:T(8,128)S(1)}, u32[]{:S(2)}, u32[]{:S(2)}) %all-to-all-start.4) | async-done | bytes 655392 | tf_op jit(solution)/shard_map/all_to_all | solution.py:268
  139.1 6.5 %shard_map.80 = (f32[64,2048]{1,0:T(8,128)S(1)}, f32[32,64]{1,0:T(8,128)}) custom-call(s32[2]{0:T(128)S(1)} %rev.3.base_ref, s32[1]{0:T(128)} %bitcast.8.count_ref, s32[2,256]{1,0:T(2,128)S(1)} %bitcast.11, f32[16,80,128]{2,1,0:T(8,128)S(1)} %all-to-all-done.4.source_ref), custom_call_target="tpu_custom_call" | custom-call | flops 8589934592 | bytes 2097152 | tf_op jit(solution)/shard_map/pallas_call | solution.py:139
  145.6 5.3 %collective-permute-start.2 = (f32[64,2048]{1,0:T(8,128)S(1)}, f32[64,2048]{1,0:T(8,128)S(1)}, u32[]{:S(2)}, u32[]{:S(2)}) collective-permute-start(f32[64,2048]{1,0:T(8,128)S(1)} %get-tuple-element.25), channel_id=1, source_target_pairs={{0,256},{256,0},{1,257},{257,1},{2,258},{258,2},{3,259},{259,3},{4... | collective-permute-start | bytes 1572872 | tf_op jit(solution)/shard_map/ppermute | solution.py:312
  150.9 0.7 copy.9
  151.6 0.8 collective-permute-done.2
  152.4 0.8 add.7
  (20 shorter events, 1.0 us)
Async XLA Ops:
  0.6 19.5 %copy-start.3 = (f32[64,2048]{1,0:T(8,128)S(1)}, f32[64,2048]{1,0:T(8,128)}, u32[]{:S(2)}) copy-start(f32[64,2048]{1,0:T(8,128)} %source_ref.1) | copy-start | bytes 1572868
  3.8 28.2 %all-to-all-start = ((f32[4,80,128]{2,1,0:T(8,128)}), f32[4,80,128]{2,1,0:T(8,128)S(1)}, u32[]{:S(2)}, u32[]{:S(2)}) async-start(f32[4,80,128]{2,1,0:T(8,128)} %shard_map.76), calls=%async_computation | async-start | bytes 327680 | tf_op jit(solution)/shard_map/all_to_all | solution.py:268
  20.2 0.7 copy-start.4
  32.0 7.8 %copy-start = (f32[4,80,128]{2,1,0:T(8,128)}, f32[4,80,128]{2,1,0:T(8,128)S(1)}, u32[]{:S(2)}) copy-start(f32[4,80,128]{2,1,0:T(8,128)S(1)} %all-to-all-done.both_ref) | copy-start | bytes 491524
  32.0 19.5 %all-to-all-start.1 = ((f32[16,64,128]{2,1,0:T(8,128)}), f32[16,64,128]{2,1,0:T(8,128)S(1)}, u32[]{:S(2)}, u32[]{:S(2)}) async-start(f32[16,64,128]{2,1,0:T(8,128)} %shard_map.77), calls=%async_computation.1 | async-start | bytes 1048576 | tf_op jit(solution)/shard_map/all_to_all | solution.py:268
  39.8 11.8 %slice-start = ((f32[4,80,128]{2,1,0:T(8,128)}), f32[4,16,128]{2,1,0:T(8,128)S(1)}, s32[]{:S(2)}) async-start(f32[4,80,128]{2,1,0:T(8,128)} %copy-done), calls=%async_computation.5 | async-start | bytes 65536 | tf_op jit(solution)/shard_map/slice | solution.py:293
  52.4 26.2 %all-to-all-start.2 = ((f32[16,64,128]{2,1,0:T(8,128)}), f32[16,64,128]{2,1,0:T(8,128)S(1)}, u32[]{:S(2)}, u32[]{:S(2)}) async-start(f32[16,64,128]{2,1,0:T(8,128)} %broadcast_in_dim.8), calls=%async_computation.2 | async-start | bytes 1048576 | tf_op jit(solution)/shard_map/all_to_all | solution.py:268
  78.6 17.9 %collective-permute-start = (f32[16,64,128]{2,1,0:T(8,128)S(1)}, f32[16,64,128]{2,1,0:T(8,128)S(1)}, u32[]{:S(2)}, u32[]{:S(2)}) collective-permute-start(f32[16,64,128]{2,1,0:T(8,128)S(1)} %all-to-all-done.2.own_ref), channel_id=1, source_target_pairs={{0,256},{256,0},{1,257},{257,1},{2,258},{258,2},{3,259},{259,3},{4... | collective-permute-start | bytes 1572872 | tf_op jit(solution)/shard_map/ppermute | solution.py:299
  85.5 11.0 %copy-start.1 = (f32[4,80,128]{2,1,0:T(8,128)S(1)}, f32[4,80,128]{2,1,0:T(8,128)}, u32[]{:S(2)}) copy-start(f32[4,80,128]{2,1,0:T(8,128)} %copy-done) | copy-start | bytes 491524
  98.8 13.0 %copy-start.2 = (f32[16,16,128]{2,1,0:T(8,128)}, f32[16,16,128]{2,1,0:T(8,128)S(1)}, u32[]{:S(2)}) copy-start(f32[16,16,128]{2,1,0:T(8,128)S(1)} %get-tuple-element.23.own_ref) | copy-start | bytes 393220
  98.8 13.0 %collective-permute-start.1 = (f32[16,16,128]{2,1,0:T(8,128)S(1)}, f32[16,16,128]{2,1,0:T(8,128)S(1)}, u32[]{:S(2)}, u32[]{:S(2)}) collective-permute-start(f32[16,16,128]{2,1,0:T(8,128)S(1)} %get-tuple-element.24), channel_id=1, source_target_pairs={{0,256},{256,0},{1,257},{257,1},{2,258},{258,2},{3,259},{259,3},{4... | collective-permute-start | bytes 393224 | tf_op jit(solution)/shard_map/ppermute | solution.py:306
  111.8 0.7 copy-start.5
  114.3 24.7 %all-to-all-start.4 = ((f32[16,80,128]{2,1,0:T(8,128)}), f32[16,80,128]{2,1,0:T(8,128)S(1)}, u32[]{:S(2)}, u32[]{:S(2)}) async-start(f32[16,80,128]{2,1,0:T(8,128)} %shard_map.79), calls=%async_computation.4 | async-start | bytes 1310720 | tf_op jit(solution)/shard_map/all_to_all | solution.py:268
  145.6 6.9 %collective-permute-start.2 = (f32[64,2048]{1,0:T(8,128)S(1)}, f32[64,2048]{1,0:T(8,128)S(1)}, u32[]{:S(2)}, u32[]{:S(2)}) collective-permute-start(f32[64,2048]{1,0:T(8,128)S(1)} %get-tuple-element.25), channel_id=1, source_target_pairs={{0,256},{256,0},{1,257},{257,1},{2,258},{258,2},{3,259},{259,3},{4... | collective-permute-start | bytes 1572872 | tf_op jit(solution)/shard_map/ppermute | solution.py:312

commit v5 on v4

--- a/solution.py
+++ b/solution.py
@@ -82,18 +82,21 @@
 
 def product_kernel(
     lane_blocks, sub_blocks, swap, sub_poly, lane_poly, scale, width,
-    base_ref, count_ref, pairs_ref, source_ref, out_ref, *refs,
+    base_ref, count_ref, pairs_ref, source_ref, *refs,
 ):
     sub_table, step_table, growth_table, lane_table, mask_table, source_parts = refs[-6:]
+    if swap:
+        terms_ref, out_ref, sum_ref = refs[:3]
+        sum_ref[...] = unpack(jnp.sum(terms_ref[...], axis=0))
+    else:
+        out_ref = refs[0]
     sub_base, lane_base = base_ref[0], base_ref[1]
     mask_table[...] = listed_tiles(swap, sub_blocks, count_ref, pairs_ref, lane_blocks * sub_blocks)
     for l, table in enumerate(sub_turns(sub_base, sub_blocks, sub_poly)):
         columns = slice(l * TILE, (l + 1) * TILE)
         sub_table[columns, :] = table
-        piece = source_ref[l, :width, :] if swap else source_ref[:, columns]
+        piece = source_ref[l] if swap else source_ref[:, columns]
         source_parts[:width, columns], source_parts[width:, columns] = split(piece)
-    if swap:
-        refs[0][...] = unpack(jnp.sum(source_ref[:, width:, :], axis=0))
 
     step_table[...], growth_table[...] = step_turns(lane_base)
 
@@ -129,17 +132,17 @@
     return pl.CostEstimate(flops=flops, bytes_accessed=traffic, transcendentals=0)
 
 
-def edge_product(base, count, pairs, source, lane_blocks, sub_blocks, swap, sub_poly, lane_poly, scale, width):
+def edge_product(base, count, pairs, source, lane_blocks, sub_blocks, swap, sub_poly, lane_poly, scale, width, *terms):
     out = jax.ShapeDtypeStruct((lane_blocks, width, TILE), f32)
     if swap:
         out = (
             jax.ShapeDtypeStruct((width, lane_blocks * TILE), f32),
-            jax.ShapeDtypeStruct((2 * (source.shape[1] - width), TILE // 2), f32),
+            jax.ShapeDtypeStruct((2 * terms[0].shape[1], terms[0].shape[2] // 2), f32),
         )
     return pl.pallas_call(
         functools.partial(product_kernel, lane_blocks, sub_blocks, swap, sub_poly, lane_poly, scale, width),
         out_shape=out,
-        in_specs=[SMEM, SMEM, VMEM, VMEM],
+        in_specs=[SMEM, SMEM, VMEM, VMEM] + [VMEM] * len(terms),
         out_specs=(VMEM, VMEM) if swap else VMEM,
         scratch_shapes=[
             pltpu.VMEM((sub_blocks * TILE, TILE), i32),
@@ -151,7 +154,7 @@
         ],
         compiler_params=pltpu.CompilerParams(vmem_limit_bytes=24 << 20),
         cost_estimate=cost(8 << 30, 1 << 21),
-    )(base, count, pairs, source)
+    )(base, count, pairs, source, *terms)
 
 
 def dot3(a, b):
@@ -179,32 +182,30 @@
             wide = [beside([p[..., :width] for p in pair]), beside([p[..., width:] for p in pair])]
             wide = jnp.concatenate(wide, axis=1).reshape(half * rows, 2 * width)
             weight[pl.ds(pl.multiple_of(which * half * rows, 8), half * rows), z * width:(z + 2) * width] = wide
-    pairs = []
-    for z in range(0, n_zh, 2):
-        pair = [both_ref[at, packed:, :] for at in (z, z + 1)]
-        pairs.append(jnp.concatenate([beside([p[:, :width] for p in pair]), beside([p[:, width:] for p in pair])], axis=0))
-    cotangent = beside(pairs)
+    cotangent = jnp.concatenate([both_ref[z, packed:, :] for z in range(n_zh)], axis=0).T
 
     pre = dot3(hidden_ref[...].T, weight[...])
     squash = 1.0 / (1.0 + jnp.exp(-pre))
-    activations = pre * squash
+    activations = (pre * squash).T
     grad_pre = cotangent * squash * (1.0 + pre * (1.0 - squash))
     n_rows = pre.shape[0]
     picked = [weight[pl.ds(pl.multiple_of((x * n_zh + zh) * width, 8), width), :] for x in range(n_x)]
-    grad_ref[...] = dot3(jnp.concatenate(picked, axis=0), grad_pre.T).reshape(n_x, width, n_rows)
+    grad_terms = dot3(jnp.concatenate(picked, axis=0), grad_pre.T).reshape(n_x, width, n_rows)
+    for y in range(grad_ref.shape[0]):
+        grad_ref[y] = grad_terms
 
     for z in range(n_zh):
         columns = slice(z * width, (z + 1) * width)
 
         @pl.when(zh == z)
         def _():
-            act_ref[...] = activations[:, columns]
+            act_ref[...] = activations[columns, :]
             for which, ref in ((core, own_terms_ref), (1 - core, other_terms_ref)):
                 part = hidden_ref[pl.ds(pl.multiple_of(which * (depth // 2), 8), depth // 2), :]
                 ref[...] = pack(dot3(part, grad_pre[:, columns]).reshape(half, rows, width))
 
 
-def layer(at, hidden_all, own, other, both, n_x, n_zh, rows):
+def layer(at, hidden_all, own, other, both, n_y, n_x, n_zh, rows):
     half = own.shape[0]
     width = own.shape[2] // 2
     n_rows = hidden_all.shape[1]
@@ -212,8 +213,8 @@
     return pl.pallas_call(
         functools.partial(layer_kernel, n_x, n_zh),
         out_shape=(
-            jax.ShapeDtypeStruct((n_rows, width), f32),
-            jax.ShapeDtypeStruct((n_x, width, n_rows), f32),
+            jax.ShapeDtypeStruct((width, n_rows), f32),
+            jax.ShapeDtypeStruct((n_y, n_x, width, n_rows), f32),
             terms, terms,
         ),
         in_specs=[SMEM, VMEM, VMEM, VMEM, VMEM],
@@ -224,40 +225,43 @@
     )(at, hidden_all, own, other, both)
 
 
-def join_kernel(grad_ref, own_ref, other_ref, out_ref):
+def join_kernel(n_x, grad_ref, own_ref, other_ref, out_ref, terms_ref):
     width = grad_ref.shape[1]
-    grad = jnp.sum(grad_ref[...], axis=0)
-    for n in range(out_ref.shape[0]):
-        out_ref[n, :width, :] = grad
-    out_ref[:, width:, :] = own_ref[...] + other_ref[...]
-
-
-def join(grad_terms, own_terms, other_terms):
-    n, packed, lanes = own_terms.shape
+    for y in range(grad_ref.shape[0] // n_x):
+        out_ref[y * width:(y + 1) * width, :] = jnp.sum(grad_ref[y * n_x:(y + 1) * n_x], axis=0)
+    terms_ref[...] = own_ref[...] + other_ref[...]
+
+
+def join(grad_terms, own_terms, other_terms, n_x):
+    n, width, lanes = grad_terms.shape
     return pl.pallas_call(
-        join_kernel,
-        out_shape=jax.ShapeDtypeStruct((n, grad_terms.shape[1] + packed, lanes), f32),
+        functools.partial(join_kernel, n_x),
+        out_shape=(
+            jax.ShapeDtypeStruct((n // n_x * width, lanes), f32),
+            jax.ShapeDtypeStruct(own_terms.shape, f32),
+        ),
         in_specs=[VMEM] * 3,
-        out_specs=VMEM,
+        out_specs=(VMEM, VMEM),
         cost_estimate=cost(1 << 20, 1 << 20),
     )(grad_terms, own_terms, other_terms)
 
 
-def start_kernel(weight_ref, cotangent_ref, out_ref):
-    both = jnp.concatenate([pack(weight_ref[...]), pack(cotangent_ref[...])], axis=0)
+def start_kernel(weight_ref, turned_ref, out_ref):
+    packed = weight_ref.shape[0] // 2
+    weight = pack(weight_ref[...])
     for n in range(out_ref.shape[0]):
-        out_ref[n] = both
-
-
-def start(weight, cotangent, n):
-    rows = (weight.shape[0] + cotangent.shape[0]) // 2
+        out_ref[n, :packed, :] = weight
+        out_ref[n, packed:, :] = turned_ref[...]
+
+
+def start(weight, turned, n):
     return pl.pallas_call(
         start_kernel,
-        out_shape=jax.ShapeDtypeStruct((n, rows, 2 * weight.shape[1]), f32),
+        out_shape=jax.ShapeDtypeStruct((n, weight.shape[0] // 2 + turned.shape[0], turned.shape[1]), f32),
         in_specs=[VMEM] * 2,
         out_specs=VMEM,
         cost_estimate=cost(1 << 16, 1 << 18),
-    )(weight, cotangent)
+    )(weight, turned)
 
 
 def copies(value, n):
@@ -272,7 +276,7 @@
     nbr, feat = ("zl", "y"), ("x", "zh")
     pairs, count = tile_list[0, 0], tile_count[0]
     n_nbr = lax.axis_size(nbr)
-    n_x, n_zh = lax.axis_size("x"), lax.axis_size("zh")
+    n_y, n_x, n_zh = lax.axis_size("y"), lax.axis_size("x"), lax.axis_size("zh")
     core, nbr_id = lax.axis_index("core"), lax.axis_index(nbr)
     width, c_dev = features.shape
     n_rows = cotangent.shape[0]
@@ -283,7 +287,7 @@
 
     rows_poly, cols_poly = (3, 11), (5, 13)
     packed = weight.shape[0] // 2
-    both_z = exchange(start(weight, cotangent, n_zh), "zh")
+    both_z = exchange(start(weight, cotangent.T, n_zh), "zh")
 
     bases = jnp.stack([nbr_id * c_dev, core * r_dev]).astype(i32)
     partial = edge_product(
@@ -297,20 +301,22 @@
     hidden_z = lax.all_gather(hidden, "zh", axis=0, tiled=True)
     hidden_z, own = lax.optimization_barrier((hidden_z, own))
     other = lax.ppermute(own, "core", swap_core)
-    hidden_all = lax.all_gather(hidden_z, "x", axis=0, tiled=True)
+    hidden_all = exchange(copies(hidden_z, n_x), "x").reshape(-1, n_rows)
 
     at = jnp.stack([core, lax.axis_index("zh")]).astype(i32)
     activations, grad_terms, own_terms, other_terms = layer(
-        at, hidden_all, own, other, both_z, n_x, n_zh, weight.shape[0]
+        at, hidden_all, own, other, both_z, n_y, n_x, n_zh, weight.shape[0]
     )
     other_terms = lax.ppermute(other_terms, "core", swap_core)
-    grad_terms = exchange(grad_terms, "x")
-    grad_block = exchange(join(grad_terms, own_terms, other_terms), nbr)
+    grad_terms = exchange(grad_terms.reshape(-1, width, n_rows), ("y", "x"))
+    grad_hidden, terms = join(grad_terms, own_terms, other_terms, n_x)
+    terms = exchange(terms, nbr)
+    grad_block = lax.all_gather(grad_hidden, "zl", axis=0, tiled=True).reshape(n_nbr, width, n_rows)
     column_part, weight_grad = edge_product(
-        bases[::-1], count, pairs, grad_block, col_blocks, row_blocks, True, rows_poly, cols_poly, scale, width
+        bases[::-1], count, pairs, grad_block, col_blocks, row_blocks, True, rows_poly, cols_poly, scale, width, terms
     )
     feature_grad = column_part + lax.ppermute(column_part, "core", swap_core)
-    return activations, feature_grad, weight_grad
+    return activations.T, feature_grad, weight_grad
 
 
 def halves(n):

time: 154 us -> 157 us (1.019)
  starting transfers between devices: 56.2 us -> 64.3 us
  blocking collectives: 39 us -> 31.9 us
  waiting for transfers between devices: 31.6 us -> 33.3 us
    all_to_all x1 -> x0, blocking collectives: 8.57 us -> none  [exchange(): return lax.all_to_all(value, axes, 0, 0)]
    all_to_all x4 -> x6, starting transfers between devices: 39.6 us -> 46.8 us  [exchange(): return lax.all_to_all(value, axes, 0, 0)]
    ppermute x1, starting transfers between devices: 5.34 us -> 7.34 us  [per_device(): feature_grad = column_part + lax.ppermute(column_part, 'core', swap_core)]
    unnamed x14 -> x16, local copies, waits for them, and re-layouts: 3.59 us -> 2.13 us
    all_to_all x4 -> x6, waiting for transfers between devices: 30.8 us -> 30.8 us  [exchange(): return lax.all_to_all(value, axes, 0, 0)]
  transfers between devices with their start and end apart: 7 -> 9, of which waited for: 4 -> 6; matrix products, arithmetic and copies ran while one was open for 1% -> 1% of each run, Pallas kernels for 5% -> 5%
where the time goes in v5:
time: 157 us; the launch traced here: 156 us
  starting transfers between devices  64.3 us (41%)
  waiting for transfers between devices  33.3 us (21%)
  blocking collectives  31.9 us (20%)
  Pallas kernels  20.2 us (13%)
  local copies, waits for them, and re-layouts  3.9 us (2%)
    all_to_all x6, starting transfers between devices, exchange(): return lax.all_to_all(value, axes, 0, 0)  46.8 us
    all_to_all x6, waiting for transfers between devices, exchange(): return lax.all_to_all(value, axes, 0, 0)  30.8 us
    all_gather x1, blocking collectives, per_device(): hidden_z = lax.all_gather(hidden, 'zh', axis=0, tiled=True)  19.4 us
    pallas_call x2, Pallas kernels, edge_product(): pl.pallas_call(functools.partial(product_kernel, lane_blocks, sub_blocks,...  13.7 us
    all_gather x1, blocking collectives, per_device(): lax.all_gather(grad_hidden, 'zl', axis=0, tiled=True)  12.5 us
    ppermute x1, starting transfers between devices, per_device(): feature_grad = column_part + lax.ppermute(column_part, 'core', swap_core)  7.34 us
    ppermute x1, starting transfers between devices, per_device(): other = lax.ppermute(own, 'core', swap_core)  6.82 us
    ppermute x1, starting transfers between devices, per_device(): other_terms = lax.ppermute(other_terms, 'core', swap_core)  3.3 us
  transfers between devices with their start and end apart: 9, of which 6 were waited for; matrix products, arithmetic and copies ran while one was open for 1% of the time, Pallas kernels for 5%

profile of v5, /device:TPU:1, one launch (start us, length us, event | category | flops | bytes accessed | tf_op | source)
XLA Modules:
  0.0 156.0 jit_solution(5479591847323870943)
XLA Ops:
  0.6 1.6 %shard_map.76 = f32[4,80,128]{2,1,0:T(8,128)} custom-call(f32[32,64]{1,0:T(8,128)} %weight_ref.1, f32[64,128]{1,0:T(8,128)} %bitcast.19), custom_call_target="tpu_custom_call" | custom-call | flops 65536 | bytes 262144 | tf_op jit(solution)/shard_map/pallas_call | solution.py:258
  2.2 15.6 %all-to-all-start = ((f32[4,80,128]{2,1,0:T(8,128)}), f32[4,80,128]{2,1,0:T(8,128)S(1)}, u32[]{:S(2)}, u32[]{:S(2)}) async-start(f32[4,80,128]{2,1,0:T(8,128)} %shard_map.76), calls=%async_computation | async-start | bytes 327680 | tf_op jit(solution)/shard_map/all_to_all | solution.py:272
  19.2 7.3 %shard_map.77 = f32[16,64,128]{2,1,0:T(8,128)} custom-call(s32[2]{0:T(128)S(1)} %pad_add_fusion.1.base_ref, s32[1]{0:T(128)} %bitcast.12.count_ref, s32[2,256]{1,0:T(2,128)S(1)} %bitcast.17, f32[64,2048]{1,0:T(8,128)S(1)} %copy-done.3), custom_call_target="tpu_custom_call" | custom-call | flops 8589934592 | bytes 2097152 | tf_op jit(solution)/shard_map/pallas_call | solution.py:142
  26.5 3.9 %all-to-all-done.both_ref = f32[4,80,128]{2,1,0:T(8,128)S(1)} async-done(((f32[4,80,128]{2,1,0:T(8,128)}), f32[4,80,128]{2,1,0:T(8,128)S(1)}, u32[]{:S(2)}, u32[]{:S(2)}) %all-to-all-start) | async-done | bytes 163872 | tf_op jit(solution)/shard_map/all_to_all | solution.py:272
  30.4 7.8 %all-to-all-start.1 = ((f32[16,64,128]{2,1,0:T(8,128)}), f32[16,64,128]{2,1,0:T(8,128)S(1)}, u32[]{:S(2)}, u32[]{:S(2)}) async-start(f32[16,64,128]{2,1,0:T(8,128)} %shard_map.77), calls=%async_computation.1 | async-start | bytes 1048576 | tf_op jit(solution)/shard_map/all_to_all | solution.py:272
  38.2 11.7 %all-to-all-done.1 = f32[16,64,128]{2,1,0:T(8,128)S(1)} async-done(((f32[16,64,128]{2,1,0:T(8,128)}), f32[16,64,128]{2,1,0:T(8,128)S(1)}, u32[]{:S(2)}, u32[]{:S(2)}) %all-to-all-start.1) | async-done | bytes 524320 | tf_op jit(solution)/shard_map/all_to_all | solution.py:272
  50.0 0.8 broadcast_in_dim.14
  50.8 6.8 %all-to-all-start.2 = ((f32[16,64,128]{2,1,0:T(8,128)}), f32[16,64,128]{2,1,0:T(8,128)S(1)}, u32[]{:S(2)}, u32[]{:S(2)}) async-start(f32[16,64,128]{2,1,0:T(8,128)} %broadcast_in_dim.14), calls=%async_computation.2 | async-start | bytes 1048576 | tf_op jit(solution)/shard_map/all_to_all | solution.py:272
  57.6 19.4 %all_gather.6 = f32[256,128]{1,0:T(8,128)S(1)} all-gather(f32[64,128]{1,0:T(8,128)S(1)} %reduce_sum.9), channel_id=1, replica_groups=mesh['core'=2,'zl'=4,'y'=4,'x'=4,'zh'=4] {'zh'}, dimensions={0}, use_global_device_ids=true | all-gather | bytes 163840 | tf_op jit(solution)/shard_map/all_gather | solution.py:301
  77.0 6.8 %collective-permute-start = (f32[16,64,128]{2,1,0:T(8,128)S(1)}, f32[16,64,128]{2,1,0:T(8,128)S(1)}, u32[]{:S(2)}, u32[]{:S(2)}) collective-permute-start(f32[16,64,128]{2,1,0:T(8,128)S(1)} %all-to-all-done.2.own_ref), channel_id=1, source_target_pairs={{0,256},{256,0},{1,257},{257,1},{2,258},{258,2},{3,259},{259,3},{4... | collective-permute-start | bytes 1572872 | tf_op jit(solution)/shard_map/ppermute | solution.py:303
  84.7 4.1 %all-to-all-start.3 = ((f32[4,256,128]{2,1,0:T(8,128)}), f32[4,256,128]{2,1,0:T(8,128)S(1)}, u32[]{:S(2)}, u32[]{:S(2)}) async-start(f32[4,256,128]{2,1,0:T(8,128)} %broadcast_in_dim.15), calls=%async_computation.3 | async-start | bytes 1048576 | tf_op jit(solution)/shard_map/all_to_all | solution.py:272
  88.8 9.2 %all-to-all-done.3 = f32[4,256,128]{2,1,0:T(8,128)S(1)} async-done(((f32[4,256,128]{2,1,0:T(8,128)}), f32[4,256,128]{2,1,0:T(8,128)S(1)}, u32[]{:S(2)}, u32[]{:S(2)}) %all-to-all-start.3) | async-done | bytes 524320 | tf_op jit(solution)/shard_map/all_to_all | solution.py:272
  98.1 3.0 %shard_map.78 = (f32[64,128]{1,0:T(8,128)}, f32[4,4,64,128]{3,2,1,0:T(8,128)}, f32[16,16,128]{2,1,0:T(8,128)S(1)}, f32[16,16,128]{2,1,0:T(8,128)S(1)}) custom-call(s32[2]{0:T(128)S(1)} %pad_add_fusion.at_ref, f32[1024,128]{1,0:T(8,128)S(1)} %bitcast.15, f32[16,64,128]{2,1,0:T(8,128)S(1)} %all-to-all-done.2.own_ref, ...), custom_call_target="tpu_custom_call" | custom-call | flops 1073741824 | bytes 2097152 | tf_op jit(solution)/shard_map/pallas_call | solution.py:213
  101.7 4.9 %all-to-all-start.4 = ((f32[16,64,128]{2,1,0:T(8,128)}), f32[16,64,128]{2,1,0:T(8,128)S(1)}, u32[]{:S(2)}, u32[]{:S(2)}) async-start(f32[16,64,128]{2,1,0:T(8,128)} %bitcast.10), calls=%async_computation.4 | async-start | bytes 1048576 | tf_op jit(solution)/shard_map/all_to_all | solution.py:272
  106.7 3.3 %collective-permute-start.1 = (f32[16,16,128]{2,1,0:T(8,128)S(1)}, f32[16,16,128]{2,1,0:T(8,128)S(1)}, u32[]{:S(2)}, u32[]{:S(2)}) collective-permute-start(f32[16,16,128]{2,1,0:T(8,128)S(1)} %get-tuple-element.26), channel_id=1, source_target_pairs={{0,256},{256,0},{1,257},{257,1},{2,258},{258,2},{3,259},{259,3},{4... | collective-permute-start | bytes 393224 | tf_op jit(solution)/shard_map/ppermute | solution.py:310
  110.0 1.0 collective-permute-done.1.other_ref
  110.9 5.9 %all-to-all-done.4.grad_ref = f32[16,64,128]{2,1,0:T(8,128)S(1)} async-done(((f32[16,64,128]{2,1,0:T(8,128)}), f32[16,64,128]{2,1,0:T(8,128)S(1)}, u32[]{:S(2)}, u32[]{:S(2)}) %all-to-all-start.4) | async-done | bytes 524320 | tf_op jit(solution)/shard_map/all_to_all | solution.py:272
  117.7 1.9 %shard_map.79 = (f32[256,128]{1,0:T(8,128)}, f32[16,16,128]{2,1,0:T(8,128)}) custom-call(f32[16,64,128]{2,1,0:T(8,128)} %copy-done.5, f32[16,16,128]{2,1,0:T(8,128)} %copy-done.2, f32[16,16,128]{2,1,0:T(8,128)} %copy-done.7), custom_call_target="tpu_custom_call" | custom-call | flops 1048576 | bytes 1048576 | tf_op jit(solution)/shard_map/pallas_call | solution.py:237
  119.5 7.6 %all-to-all-start.5 = ((f32[16,16,128]{2,1,0:T(8,128)}), f32[16,16,128]{2,1,0:T(8,128)S(1)}, u32[]{:S(2)}, u32[]{:S(2)}) async-start(f32[16,16,128]{2,1,0:T(8,128)} %get-tuple-element.28), calls=%async_computation.5 | async-start | bytes 262144 | tf_op jit(solution)/shard_map/all_to_all | solution.py:272
  127.3 12.5 %all_gather.7 = f32[1024,128]{1,0:T(8,128)S(1)} all-gather(f32[256,128]{1,0:T(8,128)S(1)} %copy-done.6), channel_id=1, replica_groups=mesh['core'=2,'zl'=4,'y'=4,'x'=4,'zh'=4] {'zl'}, dimensions={0}, use_global_device_ids=true | all-gather | bytes 655360 | tf_op jit(solution)/shard_map/all_gather | solution.py:314
  139.8 6.5 %shard_map.80 = (f32[64,2048]{1,0:T(8,128)S(1)}, f32[32,64]{1,0:T(8,128)}) custom-call(s32[2]{0:T(128)S(1)} %rev.3.base_ref, s32[1]{0:T(128)} %bitcast.13.count_ref, s32[2,256]{1,0:T(2,128)S(1)} %bitcast.18, f32[16,64,128]{2,1,0:T(8,128)S(1)} %bitcast.14, f32[16,16,128]{2,1,0:T(8,128)S(1)} %all-to-all-done.5.refs_0_), custom_call_target="tpu_custom_call" | custom-call | flops 8589934592 | bytes 2097152 | tf_op jit(solution)/shard_map/pallas_call | solution.py:142
  146.3 7.3 %collective-permute-start.2 = (f32[64,2048]{1,0:T(8,128)S(1)}, f32[64,2048]{1,0:T(8,128)S(1)}, u32[]{:S(2)}, u32[]{:S(2)}) collective-permute-start(f32[64,2048]{1,0:T(8,128)S(1)} %get-tuple-element.29), channel_id=1, source_target_pairs={{0,256},{256,0},{1,257},{257,1},{2,258},{258,2},{3,259},{259,3},{4... | collective-permute-start | bytes 1572872 | tf_op jit(solution)/shard_map/ppermute | solution.py:318
  153.6 1.5 collective-permute-done.2
  155.1 0.9 add.7
  (26 shorter events, 3.2 us)
Async XLA Ops:
  0.6 17.9 %copy-start.3 = (f32[64,2048]{1,0:T(8,128)S(1)}, f32[64,2048]{1,0:T(8,128)}, u32[]{:S(2)}) copy-start(f32[64,2048]{1,0:T(8,128)} %source_ref.1) | copy-start | bytes 1572868
  2.2 28.2 %all-to-all-start = ((f32[4,80,128]{2,1,0:T(8,128)}), f32[4,80,128]{2,1,0:T(8,128)S(1)}, u32[]{:S(2)}, u32[]{:S(2)}) async-start(f32[4,80,128]{2,1,0:T(8,128)} %shard_map.76), calls=%async_computation | async-start | bytes 327680 | tf_op jit(solution)/shard_map/all_to_all | solution.py:272
  18.6 0.7 copy-start.4
  30.4 7.8 %copy-start = (f32[4,80,128]{2,1,0:T(8,128)}, f32[4,80,128]{2,1,0:T(8,128)S(1)}, u32[]{:S(2)}) copy-start(f32[4,80,128]{2,1,0:T(8,128)S(1)} %all-to-all-done.both_ref) | copy-start | bytes 491524
  30.4 19.5 %all-to-all-start.1 = ((f32[16,64,128]{2,1,0:T(8,128)}), f32[16,64,128]{2,1,0:T(8,128)S(1)}, u32[]{:S(2)}, u32[]{:S(2)}) async-start(f32[16,64,128]{2,1,0:T(8,128)} %shard_map.77), calls=%async_computation.1 | async-start | bytes 1048576 | tf_op jit(solution)/shard_map/all_to_all | solution.py:272
  38.2 11.8 %slice-start = ((f32[4,80,128]{2,1,0:T(8,128)}), f32[4,16,128]{2,1,0:T(8,128)S(1)}, s32[]{:S(2)}) async-start(f32[4,80,128]{2,1,0:T(8,128)} %copy-done), calls=%async_computation.6 | async-start | bytes 65536 | tf_op jit(solution)/shard_map/slice | solution.py:297
  50.8 26.2 %all-to-all-start.2 = ((f32[16,64,128]{2,1,0:T(8,128)}), f32[16,64,128]{2,1,0:T(8,128)S(1)}, u32[]{:S(2)}, u32[]{:S(2)}) async-start(f32[16,64,128]{2,1,0:T(8,128)} %broadcast_in_dim.14), calls=%async_computation.2 | async-start | bytes 1048576 | tf_op jit(solution)/shard_map/all_to_all | solution.py:272
  77.0 21.1 %collective-permute-start = (f32[16,64,128]{2,1,0:T(8,128)S(1)}, f32[16,64,128]{2,1,0:T(8,128)S(1)}, u32[]{:S(2)}, u32[]{:S(2)}) collective-permute-start(f32[16,64,128]{2,1,0:T(8,128)S(1)} %all-to-all-done.2.own_ref), channel_id=1, source_target_pairs={{0,256},{256,0},{1,257},{257,1},{2,258},{258,2},{3,259},{259,3},{4... | collective-permute-start | bytes 1572872 | tf_op jit(solution)/shard_map/ppermute | solution.py:303
  84.7 13.4 %copy-start.1 = (f32[4,80,128]{2,1,0:T(8,128)S(1)}, f32[4,80,128]{2,1,0:T(8,128)}, u32[]{:S(2)}) copy-start(f32[4,80,128]{2,1,0:T(8,128)} %copy-done) | copy-start | bytes 491524
  84.7 13.4 %all-to-all-start.3 = ((f32[4,256,128]{2,1,0:T(8,128)}), f32[4,256,128]{2,1,0:T(8,128)S(1)}, u32[]{:S(2)}, u32[]{:S(2)}) async-start(f32[4,256,128]{2,1,0:T(8,128)} %broadcast_in_dim.15), calls=%async_computation.3 | async-start | bytes 1048576 | tf_op jit(solution)/shard_map/all_to_all | solution.py:272
  101.1 0.6 copy-start.2
  101.7 15.1 %all-to-all-start.4 = ((f32[16,64,128]{2,1,0:T(8,128)}), f32[16,64,128]{2,1,0:T(8,128)S(1)}, u32[]{:S(2)}, u32[]{:S(2)}) async-start(f32[16,64,128]{2,1,0:T(8,128)} %bitcast.10), calls=%async_computation.4 | async-start | bytes 1048576 | tf_op jit(solution)/shard_map/all_to_all | solution.py:272
  106.7 4.3 %collective-permute-start.1 = (f32[16,16,128]{2,1,0:T(8,128)S(1)}, f32[16,16,128]{2,1,0:T(8,128)S(1)}, u32[]{:S(2)}, u32[]{:S(2)}) collective-permute-start(f32[16,16,128]{2,1,0:T(8,128)S(1)} %get-tuple-element.26), channel_id=1, source_target_pairs={{0,256},{256,0},{1,257},{257,1},{2,258},{258,2},{3,259},{259,3},{4... | collective-permute-start | bytes 393224 | tf_op jit(solution)/shard_map/ppermute | solution.py:310
  110.9 6.0 %copy-start.7 = (f32[16,16,128]{2,1,0:T(8,128)}, f32[16,16,128]{2,1,0:T(8,128)S(1)}, u32[]{:S(2)}) copy-start(f32[16,16,128]{2,1,0:T(8,128)S(1)} %collective-permute-done.1.other_ref) | copy-start | bytes 393220
  116.9 0.8 copy-start.5
  119.5 7.7 %copy-start.6 = (f32[256,128]{1,0:T(8,128)S(1)}, f32[256,128]{1,0:T(8,128)}, u32[]{:S(2)}) copy-start(f32[256,128]{1,0:T(8,128)} %get-tuple-element.27) | copy-start | bytes 393220
  119.5 20.3 %all-to-all-start.5 = ((f32[16,16,128]{2,1,0:T(8,128)}), f32[16,16,128]{2,1,0:T(8,128)S(1)}, u32[]{:S(2)}, u32[]{:S(2)}) async-start(f32[16,16,128]{2,1,0:T(8,128)} %get-tuple-element.28), calls=%async_computation.5 | async-start | bytes 262144 | tf_op jit(solution)/shard_map/all_to_all | solution.py:272
  146.3 8.9 %collective-permute-start.2 = (f32[64,2048]{1,0:T(8,128)S(1)}, f32[64,2048]{1,0:T(8,128)S(1)}, u32[]{:S(2)}, u32[]{:S(2)}) collective-permute-start(f32[64,2048]{1,0:T(8,128)S(1)} %get-tuple-element.29), channel_id=1, source_target_pairs={{0,256},{256,0},{1,257},{257,1},{2,258},{258,2},{3,259},{259,3},{4... | collective-permute-start | bytes 1572872 | tf_op jit(solution)/shard_map/ppermute | solution.py:318

commit v6 on v4

--- a/solution.py
+++ b/solution.py
@@ -179,15 +179,11 @@
             wide = [beside([p[..., :width] for p in pair]), beside([p[..., width:] for p in pair])]
             wide = jnp.concatenate(wide, axis=1).reshape(half * rows, 2 * width)
             weight[pl.ds(pl.multiple_of(which * half * rows, 8), half * rows), z * width:(z + 2) * width] = wide
-    pairs = []
-    for z in range(0, n_zh, 2):
-        pair = [both_ref[at, packed:, :] for at in (z, z + 1)]
-        pairs.append(jnp.concatenate([beside([p[:, :width] for p in pair]), beside([p[:, width:] for p in pair])], axis=0))
-    cotangent = beside(pairs)
+    cotangent = jnp.concatenate([both_ref[z, packed:, :] for z in range(n_zh)], axis=0).T
 
     pre = dot3(hidden_ref[...].T, weight[...])
     squash = 1.0 / (1.0 + jnp.exp(-pre))
-    activations = pre * squash
+    activations = (pre * squash).T
     grad_pre = cotangent * squash * (1.0 + pre * (1.0 - squash))
     n_rows = pre.shape[0]
     picked = [weight[pl.ds(pl.multiple_of((x * n_zh + zh) * width, 8), width), :] for x in range(n_x)]
@@ -198,7 +194,7 @@
 
         @pl.when(zh == z)
         def _():
-            act_ref[...] = activations[:, columns]
+            act_ref[...] = activations[columns, :]
             for which, ref in ((core, own_terms_ref), (1 - core, other_terms_ref)):
                 part = hidden_ref[pl.ds(pl.multiple_of(which * (depth // 2), 8), depth // 2), :]
                 ref[...] = pack(dot3(part, grad_pre[:, columns]).reshape(half, rows, width))
@@ -212,7 +208,7 @@
     return pl.pallas_call(
         functools.partial(layer_kernel, n_x, n_zh),
         out_shape=(
-            jax.ShapeDtypeStruct((n_rows, width), f32),
+            jax.ShapeDtypeStruct((width, n_rows), f32),
             jax.ShapeDtypeStruct((n_x, width, n_rows), f32),
             terms, terms,
         ),
@@ -241,23 +237,6 @@
         out_specs=VMEM,
         cost_estimate=cost(1 << 20, 1 << 20),
     )(grad_terms, own_terms, other_terms)
-
-
-def start_kernel(weight_ref, cotangent_ref, out_ref):
-    both = jnp.concatenate([pack(weight_ref[...]), pack(cotangent_ref[...])], axis=0)
-    for n in range(out_ref.shape[0]):
-        out_ref[n] = both
-
-
-def start(weight, cotangent, n):
-    rows = (weight.shape[0] + cotangent.shape[0]) // 2
-    return pl.pallas_call(
-        start_kernel,
-        out_shape=jax.ShapeDtypeStruct((n, rows, 2 * weight.shape[1]), f32),
-        in_specs=[VMEM] * 2,
-        out_specs=VMEM,
-        cost_estimate=cost(1 << 16, 1 << 18),
-    )(weight, cotangent)
 
 
 def copies(value, n):
@@ -283,15 +262,17 @@
 
     rows_poly, cols_poly = (3, 11), (5, 13)
     packed = weight.shape[0] // 2
-    both_z = exchange(start(weight, cotangent, n_zh), "zh")
+    both = jnp.concatenate([pack(weight), cotangent.T], axis=0)
 
     bases = jnp.stack([nbr_id * c_dev, core * r_dev]).astype(i32)
     partial = edge_product(
         bases, count, pairs, features, row_blocks, col_blocks, False, cols_poly, rows_poly, scale, width
     )
-    both_z, partial = lax.optimization_barrier((both_z, partial))
+    both, partial = lax.optimization_barrier((both, partial))
+    both_z = lax.all_gather(both, "zh")
+    partial, both_z = lax.optimization_barrier((exchange(partial, nbr), both_z))
+    hidden = jnp.sum(partial, axis=0)
     weight_z = both_z[:, :packed].reshape(-1, TILE)
-    hidden = jnp.sum(exchange(partial, nbr), axis=0)
     hidden, weight_z = lax.optimization_barrier((hidden, copies(weight_z, n_nbr)))
     own = exchange(weight_z, nbr)
     hidden_z = lax.all_gather(hidden, "zh", axis=0, tiled=True)
@@ -310,7 +291,7 @@
         bases[::-1], count, pairs, grad_block, col_blocks, row_blocks, True, rows_poly, cols_poly, scale, width
     )
     feature_grad = column_part + lax.ppermute(column_part, "core", swap_core)
-    return activations, feature_grad, weight_grad
+    return activations.T, feature_grad, weight_grad
 
 
 def halves(n):

time: 154 us -> 150 us (0.974)
  blocking collectives: 39 us -> 60.9 us
  waiting for transfers between devices: 31.6 us -> 16.7 us
  starting transfers between devices: 56.2 us -> 47.5 us
    all_gather x0 -> x1, blocking collectives: none -> 24.9 us  [per_device(): both_z = lax.all_gather(both, 'zh')]
    all_to_all x4 -> x3, waiting for transfers between devices: 30.8 us -> 15.2 us  [exchange(): return lax.all_to_all(value, axes, 0, 0)]
    all_to_all x4 -> x3, starting transfers between devices: 39.6 us -> 29.3 us  [exchange(): return lax.all_to_all(value, axes, 0, 0)]
    all_gather x1, blocking collectives: 19.4 us -> 16.5 us  [per_device(): hidden_z = lax.all_gather(hidden, 'zh', axis=0, tiled=True)]
    ppermute x1, starting transfers between devices: 6.76 us -> 8.47 us  [per_device(): other = lax.ppermute(own, 'core', swap_core)]
    pallas_call x1 -> x0, Pallas kernels: 1.61 us -> none  [start(): pl.pallas_call(start_kernel, out_shape=jax.ShapeDtypeStruct((n, rows, 2 *...]
    unnamed x14 -> x12, local copies, waits for them, and re-layouts: 3.59 us -> 2.41 us
  transfers between devices with their start and end apart: 7 -> 6, of which waited for: 4 -> 2; matrix products, arithmetic and copies ran while one was open for 1% -> 0% of each run, Pallas kernels for 5% -> 0%
where the time goes in v6:
time: 150 us; the launch traced here: 149 us
  blocking collectives  60.9 us (41%)
  starting transfers between devices  47.5 us (32%)
  Pallas kernels  18.5 us (12%)
  waiting for transfers between devices  16.7 us (11%)
  local copies, waits for them, and re-layouts  3.36 us (2%)
    all_to_all x3, starting transfers between devices, exchange(): return lax.all_to_all(value, axes, 0, 0)  29.3 us
    all_gather x1, blocking collectives, per_device(): both_z = lax.all_gather(both, 'zh')  24.9 us
    all_gather x1, blocking collectives, per_device(): hidden_z = lax.all_gather(hidden, 'zh', axis=0, tiled=True)  16.5 us
    all_to_all x3, waiting for transfers between devices, exchange(): return lax.all_to_all(value, axes, 0, 0)  15.2 us
    pallas_call x2, Pallas kernels, edge_product(): pl.pallas_call(functools.partial(product_kernel, lane_blocks, sub_blocks,...  13.7 us
    all_gather x1, blocking collectives, per_device(): hidden_all = lax.all_gather(hidden_z, 'x', axis=0, tiled=True)  10.9 us
    all_to_all x1, blocking collectives, exchange(): return lax.all_to_all(value, axes, 0, 0)  8.58 us
    ppermute x1, starting transfers between devices, per_device(): other = lax.ppermute(own, 'core', swap_core)  8.47 us
  transfers between devices with their start and end apart: 6, of which 2 were waited for; matrix products, arithmetic and copies ran while one was open for 0% of the time, Pallas kernels for 0%

profile of v6, /device:TPU:1, one launch (start us, length us, event | category | flops | bytes accessed | tf_op | source)
XLA Modules:
  0.0 149.4 jit_solution(9128450177130569120)
XLA Ops:
  1.4 0.1 pad_add_fusion.1.base_ref
  1.5 0.7 copy-done.2
  2.2 1.0 copy-done.1
  3.2 7.2 %shard_map.76 = f32[16,64,128]{2,1,0:T(8,128)} custom-call(s32[2]{0:T(128)S(1)} %pad_add_fusion.1.base_ref, s32[1]{0:T(128)} %bitcast.10.count_ref, s32[2,256]{1,0:T(2,128)S(1)} %bitcast.14, f32[64,2048]{1,0:T(8,128)S(1)} %copy-done.1), custom_call_target="tpu_custom_call" | custom-call | flops 8589934592 | bytes 2097152 | tf_op jit(solution)/shard_map/pallas_call | solution.py:139
  10.5 9.2 %all-to-all-start = ((f32[16,64,128]{2,1,0:T(8,128)}), f32[16,64,128]{2,1,0:T(8,128)S(1)}, u32[]{:S(2)}, u32[]{:S(2)}) async-start(f32[16,64,128]{2,1,0:T(8,128)} %shard_map.76), calls=%async_computation | async-start | bytes 1048576 | tf_op jit(solution)/shard_map/all_to_all | solution.py:247
  19.7 24.9 %all-gather = f32[320,128]{1,0:T(8,128)S(1)} all-gather(f32[80,128]{1,0:T(8,128)S(1)} %pad_maximum_fusion), channel_id=2, replica_groups=mesh['core'=2,'zl'=4,'y'=4,'x'=4,'zh'=4] {'zh'}, dimensions={0}, use_global_device_ids=true | all-gather | bytes 204800 | tf_op jit(solution)/shard_map/all_gather | solution.py:272
  44.6 0.8 broadcast_in_dim.8
  45.5 10.2 %all-to-all-start.1 = ((f32[16,64,128]{2,1,0:T(8,128)}), f32[16,64,128]{2,1,0:T(8,128)S(1)}, u32[]{:S(2)}, u32[]{:S(2)}) async-start(f32[16,64,128]{2,1,0:T(8,128)} %broadcast_in_dim.8), calls=%async_computation.1 | async-start | bytes 1048576 | tf_op jit(solution)/shard_map/all_to_all | solution.py:247
  55.7 16.5 %all_gather.14 = f32[256,128]{1,0:T(8,128)S(1)} all-gather(f32[64,128]{1,0:T(8,128)S(1)} %reduce_sum.9), channel_id=1, replica_groups=mesh['core'=2,'zl'=4,'y'=4,'x'=4,'zh'=4] {'zh'}, dimensions={0}, use_global_device_ids=true | all-gather | bytes 163840 | tf_op jit(solution)/shard_map/all_gather | solution.py:278
  72.2 8.5 %collective-permute-start = (f32[16,64,128]{2,1,0:T(8,128)S(1)}, f32[16,64,128]{2,1,0:T(8,128)S(1)}, u32[]{:S(2)}, u32[]{:S(2)}) collective-permute-start(f32[16,64,128]{2,1,0:T(8,128)S(1)} %all-to-all-done.1.own_ref), channel_id=1, source_target_pairs={{0,256},{256,0},{1,257},{257,1},{2,258},{258,2},{3,259},{259,3},{4... | collective-permute-start | bytes 1572872 | tf_op jit(solution)/shard_map/ppermute | solution.py:280
  80.7 0.1 pad_add_fusion.at_ref
  80.8 10.9 %all_gather.15.hidden_ref = f32[1024,128]{1,0:T(8,128)S(1)} all-gather(f32[256,128]{1,0:T(8,128)S(1)} %all_gather.14), channel_id=1, replica_groups=mesh['core'=2,'zl'=4,'y'=4,'x'=4,'zh'=4] {'x'}, dimensions={0}, use_global_device_ids=true | all-gather | bytes 655360 | tf_op jit(solution)/shard_map/all_gather | solution.py:281
  91.6 2.9 %shard_map.77 = (f32[64,128]{1,0:T(8,128)}, f32[4,64,128]{2,1,0:T(8,128)S(1)}, f32[16,16,128]{2,1,0:T(8,128)S(1)}, f32[16,16,128]{2,1,0:T(8,128)S(1)}) custom-call(s32[2]{0:T(128)S(1)} %pad_add_fusion.at_ref, f32[1024,128]{1,0:T(8,128)S(1)} %all_gather.15.hidden_ref, f32[16,64,128]{2,1,0:T(8,128)S(1)} %all-to-all-done.1.own_ref, ...), custom_call_target="tpu_custom_call" | custom-call | flops 1073741824 | bytes 2097152 | tf_op jit(solution)/shard_map/pallas_call | solution.py:208
  94.5 4.4 %collective-permute-start.1 = (f32[16,16,128]{2,1,0:T(8,128)S(1)}, f32[16,16,128]{2,1,0:T(8,128)S(1)}, u32[]{:S(2)}, u32[]{:S(2)}) collective-permute-start(f32[16,16,128]{2,1,0:T(8,128)S(1)} %get-tuple-element.28), channel_id=1, source_target_pairs={{0,256},{256,0},{1,257},{257,1},{2,258},{258,2},{3,259},{259,3},{4... | collective-permute-start | bytes 393224 | tf_op jit(solution)/shard_map/ppermute | solution.py:287
  98.9 8.6 %all_to_all.20.grad_ref = f32[4,64,128]{2,1,0:T(8,128)} all-to-all(f32[4,64,128]{2,1,0:T(8,128)S(1)} %get-tuple-element.26), channel_id=1, replica_groups=mesh['core'=2,'zl'=4,'y'=4,'x'=4,'zh'=4] {'x'}, dimensions={0} | all-to-all | bytes 262144 | tf_op jit(solution)/shard_map/all_to_all | solution.py:247
  107.5 0.6 copy-done.3
  108.1 1.9 %shard_map.78 = f32[16,80,128]{2,1,0:T(8,128)} custom-call(f32[4,64,128]{2,1,0:T(8,128)} %all_to_all.20.grad_ref, f32[16,16,128]{2,1,0:T(8,128)} %copy-done, f32[16,16,128]{2,1,0:T(8,128)} %copy-done.3), custom_call_target="tpu_custom_call" | custom-call | flops 1048576 | bytes 1048576 | tf_op jit(solution)/shard_map/pallas_call | solution.py:233
  110.0 9.9 %all-to-all-start.3 = ((f32[16,80,128]{2,1,0:T(8,128)}), f32[16,80,128]{2,1,0:T(8,128)S(1)}, u32[]{:S(2)}, u32[]{:S(2)}) async-start(f32[16,80,128]{2,1,0:T(8,128)} %shard_map.78), calls=%async_computation.3 | async-start | bytes 1310720 | tf_op jit(solution)/shard_map/all_to_all | solution.py:247
  120.0 0.1 rev.3.base_ref
  120.0 15.2 %all-to-all-done.3.source_ref = f32[16,80,128]{2,1,0:T(8,128)S(1)} async-done(((f32[16,80,128]{2,1,0:T(8,128)}), f32[16,80,128]{2,1,0:T(8,128)S(1)}, u32[]{:S(2)}, u32[]{:S(2)}) %all-to-all-start.3) | async-done | bytes 655392 | tf_op jit(solution)/shard_map/all_to_all | solution.py:247
  135.2 6.5 %shard_map.79 = (f32[64,2048]{1,0:T(8,128)S(1)}, f32[32,64]{1,0:T(8,128)}) custom-call(s32[2]{0:T(128)S(1)} %rev.3.base_ref, s32[1]{0:T(128)} %bitcast.11.count_ref, s32[2,256]{1,0:T(2,128)S(1)} %bitcast.15, f32[16,80,128]{2,1,0:T(8,128)S(1)} %all-to-all-done.3.source_ref), custom_call_target="tpu_custom_call" | custom-call | flops 8589934592 | bytes 2097152 | tf_op jit(solution)/shard_map/pallas_call | solution.py:139
  141.7 5.3 %collective-permute-start.2 = (f32[64,2048]{1,0:T(8,128)S(1)}, f32[64,2048]{1,0:T(8,128)S(1)}, u32[]{:S(2)}, u32[]{:S(2)}) collective-permute-start(f32[64,2048]{1,0:T(8,128)S(1)} %get-tuple-element.29), channel_id=1, source_target_pairs={{0,256},{256,0},{1,257},{257,1},{2,258},{258,2},{3,259},{259,3},{4... | collective-permute-start | bytes 1572872 | tf_op jit(solution)/shard_map/ppermute | solution.py:293
  147.0 1.5 %collective-permute-done.2 = f32[64,2048]{1,0:T(8,128)S(1)} collective-permute-done((f32[64,2048]{1,0:T(8,128)S(1)}, f32[64,2048]{1,0:T(8,128)S(1)}, u32[]{:S(2)}, u32[]{:S(2)}) %collective-permute-start.2) | collective-permute-done | bytes 524320 | tf_op jit(solution)/shard_map/ppermute | solution.py:293
  148.6 0.9 add.7
  (17 shorter events, 0.2 us)
Async XLA Ops:
  0.6 0.7 copy-start.5
  0.6 0.8 copy-start.4
  1.5 0.7 copy-start.2
  2.2 1.0 copy-start.1
  10.5 34.1 %all-to-all-start = ((f32[16,64,128]{2,1,0:T(8,128)}), f32[16,64,128]{2,1,0:T(8,128)S(1)}, u32[]{:S(2)}, u32[]{:S(2)}) async-start(f32[16,64,128]{2,1,0:T(8,128)} %shard_map.76), calls=%async_computation | async-start | bytes 1048576 | tf_op jit(solution)/shard_map/all_to_all | solution.py:247
  45.5 26.7 %all-to-all-start.1 = ((f32[16,64,128]{2,1,0:T(8,128)}), f32[16,64,128]{2,1,0:T(8,128)S(1)}, u32[]{:S(2)}, u32[]{:S(2)}) async-start(f32[16,64,128]{2,1,0:T(8,128)} %broadcast_in_dim.8), calls=%async_computation.1 | async-start | bytes 1048576 | tf_op jit(solution)/shard_map/all_to_all | solution.py:247
  72.2 19.4 %collective-permute-start = (f32[16,64,128]{2,1,0:T(8,128)S(1)}, f32[16,64,128]{2,1,0:T(8,128)S(1)}, u32[]{:S(2)}, u32[]{:S(2)}) collective-permute-start(f32[16,64,128]{2,1,0:T(8,128)S(1)} %all-to-all-done.1.own_ref), channel_id=1, source_target_pairs={{0,256},{256,0},{1,257},{257,1},{2,258},{258,2},{3,259},{259,3},{4... | collective-permute-start | bytes 1572872 | tf_op jit(solution)/shard_map/ppermute | solution.py:280
  94.5 13.0 %copy-start = (f32[16,16,128]{2,1,0:T(8,128)}, f32[16,16,128]{2,1,0:T(8,128)S(1)}, u32[]{:S(2)}) copy-start(f32[16,16,128]{2,1,0:T(8,128)S(1)} %get-tuple-element.27.own_ref) | copy-start | bytes 393220
  94.5 13.0 %collective-permute-start.1 = (f32[16,16,128]{2,1,0:T(8,128)S(1)}, f32[16,16,128]{2,1,0:T(8,128)S(1)}, u32[]{:S(2)}, u32[]{:S(2)}) collective-permute-start(f32[16,16,128]{2,1,0:T(8,128)S(1)} %get-tuple-element.28), channel_id=1, source_target_pairs={{0,256},{256,0},{1,257},{257,1},{2,258},{258,2},{3,259},{259,3},{4... | collective-permute-start | bytes 393224 | tf_op jit(solution)/shard_map/ppermute | solution.py:287
  107.5 0.6 copy-start.3
  110.0 25.2 %all-to-all-start.3 = ((f32[16,80,128]{2,1,0:T(8,128)}), f32[16,80,128]{2,1,0:T(8,128)S(1)}, u32[]{:S(2)}, u32[]{:S(2)}) async-start(f32[16,80,128]{2,1,0:T(8,128)} %shard_map.78), calls=%async_computation.3 | async-start | bytes 1310720 | tf_op jit(solution)/shard_map/all_to_all | solution.py:247
  141.7 6.9 %collective-permute-start.2 = (f32[64,2048]{1,0:T(8,128)S(1)}, f32[64,2048]{1,0:T(8,128)S(1)}, u32[]{:S(2)}, u32[]{:S(2)}) collective-permute-start(f32[64,2048]{1,0:T(8,128)S(1)} %get-tuple-element.29), channel_id=1, source_target_pairs={{0,256},{256,0},{1,257},{257,1},{2,258},{258,2},{3,259},{259,3},{4... | collective-permute-start | bytes 1572872 | tf_op jit(solution)/shard_map/ppermute | solution.py:293

commit v7 on v6

--- a/solution.py
+++ b/solution.py
@@ -179,7 +179,7 @@
             wide = [beside([p[..., :width] for p in pair]), beside([p[..., width:] for p in pair])]
             wide = jnp.concatenate(wide, axis=1).reshape(half * rows, 2 * width)
             weight[pl.ds(pl.multiple_of(which * half * rows, 8), half * rows), z * width:(z + 2) * width] = wide
-    cotangent = jnp.concatenate([both_ref[z, packed:, :] for z in range(n_zh)], axis=0).T
+    cotangent = jnp.concatenate([both_ref[z, width + packed:, :] for z in range(n_zh)], axis=0).T
 
     pre = dot3(hidden_ref[...].T, weight[...])
     squash = 1.0 / (1.0 + jnp.exp(-pre))
@@ -239,8 +239,46 @@
     )(grad_terms, own_terms, other_terms)
 
 
-def copies(value, n):
-    return jnp.broadcast_to(value[None], (n,) + value.shape)
+def sum_kernel(parts_ref, weight_ref, turned_ref, out_ref):
+    width, packed = parts_ref.shape[1], weight_ref.shape[0] // 2
+    out_ref[:width, :] = jnp.sum(parts_ref[...], axis=0)
+    out_ref[width:width + packed, :] = pack(weight_ref[...])
+    out_ref[width + packed:, :] = turned_ref[...]
+
+
+def sum_parts(parts, weight, turned):
+    rows = parts.shape[1] + weight.shape[0] // 2 + turned.shape[0]
+    return pl.pallas_call(
+        sum_kernel,
+        out_shape=jax.ShapeDtypeStruct((rows, parts.shape[2]), f32),
+        in_specs=[VMEM] * 3,
+        out_specs=VMEM,
+        cost_estimate=cost(1 << 20, 1 << 20),
+    )(parts, weight, turned)
+
+
+def deal_kernel(gathered_ref, hidden_ref, weight_ref):
+    n_zh = gathered_ref.shape[0]
+    width, packed = hidden_ref.shape[0] // n_zh, weight_ref.shape[1] // n_zh
+    for z in range(n_zh):
+        hidden_ref[z * width:(z + 1) * width, :] = gathered_ref[z, :width, :]
+        weight = gathered_ref[z, width:width + packed, :]
+        for n in range(weight_ref.shape[0]):
+            weight_ref[n, z * packed:(z + 1) * packed, :] = weight
+
+
+def deal(gathered, width, packed, n):
+    n_zh, _, lanes = gathered.shape
+    return pl.pallas_call(
+        deal_kernel,
+        out_shape=(
+            jax.ShapeDtypeStruct((n_zh * width, lanes), f32),
+            jax.ShapeDtypeStruct((n, n_zh * packed, lanes), f32),
+        ),
+        in_specs=[VMEM],
+        out_specs=(VMEM, VMEM),
+        cost_estimate=cost(1 << 20, 1 << 20),
+    )(gathered)
 
 
 def exchange(value, axes):
@@ -262,27 +300,20 @@
 
     rows_poly, cols_poly = (3, 11), (5, 13)
     packed = weight.shape[0] // 2
-    both = jnp.concatenate([pack(weight), cotangent.T], axis=0)
-
     bases = jnp.stack([nbr_id * c_dev, core * r_dev]).astype(i32)
     partial = edge_product(
         bases, count, pairs, features, row_blocks, col_blocks, False, cols_poly, rows_poly, scale, width
     )
-    both, partial = lax.optimization_barrier((both, partial))
-    both_z = lax.all_gather(both, "zh")
-    partial, both_z = lax.optimization_barrier((exchange(partial, nbr), both_z))
-    hidden = jnp.sum(partial, axis=0)
-    weight_z = both_z[:, :packed].reshape(-1, TILE)
-    hidden, weight_z = lax.optimization_barrier((hidden, copies(weight_z, n_nbr)))
+    gathered = lax.all_gather(sum_parts(exchange(partial, nbr), weight, cotangent.T), "zh")
+    hidden_z, weight_z = deal(gathered, width, packed, n_nbr)
     own = exchange(weight_z, nbr)
-    hidden_z = lax.all_gather(hidden, "zh", axis=0, tiled=True)
-    hidden_z, own = lax.optimization_barrier((hidden_z, own))
+    hidden_all = lax.all_gather(hidden_z, "x", axis=0, tiled=True)
+    hidden_all, own = lax.optimization_barrier((hidden_all, own))
     other = lax.ppermute(own, "core", swap_core)
-    hidden_all = lax.all_gather(hidden_z, "x", axis=0, tiled=True)
 
     at = jnp.stack([core, lax.axis_index("zh")]).astype(i32)
     activations, grad_terms, own_terms, other_terms = layer(
-        at, hidden_all, own, other, both_z, n_x, n_zh, weight.shape[0]
+        at, hidden_all, own, other, gathered, n_x, n_zh, weight.shape[0]
     )
     other_terms = lax.ppermute(other_terms, "core", swap_core)
     grad_terms = exchange(grad_terms, "x")

time: 150 us -> 140 us (0.933)
  starting transfers between devices: 47.5 us -> 30.2 us
  blocking collectives: 60.9 us -> 64.6 us
  Pallas kernels: 18.5 us -> 21.3 us
  waiting for transfers between devices: 16.7 us -> 18.3 us
    all_to_all x1 -> x2, blocking collectives: 8.58 us -> 30.9 us  [exchange(): return lax.all_to_all(value, axes, 0, 0)]
    all_gather x2 -> x1, blocking collectives: 41.4 us -> 22.8 us  [per_device(): lax.all_gather(sum_parts(exchange(partial, nbr), weight, cotangent.T), 'zh')]
    all_to_all x3 -> x2, starting transfers between devices: 29.3 us -> 13.3 us  [exchange(): return lax.all_to_all(value, axes, 0, 0)]
    pallas_call x0 -> x2, Pallas kernels: none -> 3.61 us  [the longest x1 1.85 us: deal(): pl.pallas_call(deal_kernel, out_shape=(jax.ShapeDtypeStruct((n_zh * width...]
    ppermute x1, starting transfers between devices: 4.41 us -> 2.27 us  [per_device(): other_terms = lax.ppermute(other_terms, 'core', swap_core)]
    all_to_all x3 -> x2, waiting for transfers between devices: 15.2 us -> 15.3 us  [exchange(): return lax.all_to_all(value, axes, 0, 0)]
  transfers between devices with their start and end apart: 6 -> 5, of which waited for: 2 -> 4; matrix products, arithmetic and copies ran while one was open for 0% -> 0% of each run, Pallas kernels for 0% -> 0%
where the time goes in v7:
time: 140 us; the launch traced here: 139 us
  blocking collectives  64.6 us (46%)
  starting transfers between devices  30.2 us (22%)
  Pallas kernels  21.3 us (15%)
  waiting for transfers between devices  18.3 us (13%)
  local copies, waits for them, and re-layouts  2.48 us (2%)
    all_to_all x2, blocking collectives, exchange(): return lax.all_to_all(value, axes, 0, 0)  30.9 us
    all_gather x1, blocking collectives, per_device(): lax.all_gather(sum_parts(exchange(partial, nbr), weight, cotangent.T), 'zh')  22.8 us
    all_to_all x2, waiting for transfers between devices, exchange(): return lax.all_to_all(value, axes, 0, 0)  15.3 us
    all_to_all x2, starting transfers between devices, exchange(): return lax.all_to_all(value, axes, 0, 0)  13.3 us
    pallas_call x2, Pallas kernels, edge_product(): pl.pallas_call(functools.partial(product_kernel, lane_blocks, sub_blocks,...  12.9 us
    all_gather x1, blocking collectives, per_device(): hidden_all = lax.all_gather(hidden_z, 'x', axis=0, tiled=True)  10.9 us
    ppermute x1, starting transfers between devices, per_device(): other = lax.ppermute(own, 'core', swap_core)  9.14 us
    ppermute x1, starting transfers between devices, per_device(): feature_grad = column_part + lax.ppermute(column_part, 'core', swap_core)  5.49 us
  transfers between devices with their start and end apart: 5, of which 4 were waited for; matrix products, arithmetic and copies ran while one was open for 0% of the time, Pallas kernels for 0%

profile of v7, /device:TPU:1, one launch (start us, length us, event | category | flops | bytes accessed | tf_op | source)
XLA Modules:
  0.0 139.2 jit_solution(121854766794202666)
XLA Ops:
  1.4 0.7 copy-done.3
  2.0 1.0 copy-done.2
  3.1 6.4 %shard_map.76 = f32[16,64,128]{2,1,0:T(8,128)S(1)} custom-call(s32[2]{0:T(128)S(1)} %pad_add_fusion.1.base_ref, s32[1]{0:T(128)} %bitcast.9.count_ref, s32[2,256]{1,0:T(2,128)S(1)} %bitcast.13, f32[64,2048]{1,0:T(8,128)S(1)} %copy-done.2), custom_call_target="tpu_custom_call" | custom-call | flops 8589934592 | bytes 2097152 | tf_op jit(solution)/shard_map/pallas_call | solution.py:139
  9.5 22.8 %all_to_all.20.parts_ref = f32[16,64,128]{2,1,0:T(8,128)} all-to-all(f32[16,64,128]{2,1,0:T(8,128)S(1)} %shard_map.76), channel_id=1, replica_groups=mesh['core'=2,'zl'=4,'y'=4,'x'=4,'zh'=4] {'zl','y'}, dimensions={0} | all-to-all | bytes 1048576 | tf_op jit(solution)/shard_map/all_to_all | solution.py:285
  32.3 1.8 %shard_map.77 = f32[144,128]{1,0:T(8,128)} custom-call(f32[16,64,128]{2,1,0:T(8,128)} %all_to_all.20.parts_ref, f32[32,64]{1,0:T(8,128)} %weight_ref.1, f32[64,128]{1,0:T(8,128)} %bitcast.15), custom_call_target="tpu_custom_call" | custom-call | flops 1048576 | bytes 1048576 | tf_op jit(solution)/shard_map/pallas_call | solution.py:251
  34.1 22.8 %all-gather = f32[576,128]{1,0:T(8,128)} all-gather(f32[144,128]{1,0:T(8,128)} %shard_map.77), channel_id=2, replica_groups=mesh['core'=2,'zl'=4,'y'=4,'x'=4,'zh'=4] {'zh'}, dimensions={0}, use_global_device_ids=true | all-gather | bytes 368640 | tf_op jit(solution)/shard_map/all_gather | solution.py:307
  56.9 1.8 %shard_map.78 = (f32[256,128]{1,0:T(8,128)}, f32[16,64,128]{2,1,0:T(8,128)}) custom-call(f32[4,144,128]{2,1,0:T(8,128)} %bitcast.11), custom_call_target="tpu_custom_call" | custom-call | flops 1048576 | bytes 1048576 | tf_op jit(solution)/shard_map/pallas_call | solution.py:272
  58.7 6.0 %all-to-all-start.1 = ((f32[16,64,128]{2,1,0:T(8,128)}), f32[16,64,128]{2,1,0:T(8,128)S(1)}, u32[]{:S(2)}, u32[]{:S(2)}) async-start(f32[16,64,128]{2,1,0:T(8,128)} %get-tuple-element.14), calls=%async_computation.1 | async-start | bytes 1048576 | tf_op jit(solution)/shard_map/all_to_all | solution.py:285
  64.7 10.9 %all_gather.11.hidden_ref = f32[1024,128]{1,0:T(8,128)S(1)} all-gather(f32[256,128]{1,0:T(8,128)S(1)} %copy-done.4), channel_id=1, replica_groups=mesh['core'=2,'zl'=4,'y'=4,'x'=4,'zh'=4] {'x'}, dimensions={0}, use_global_device_ids=true | all-gather | bytes 655360 | tf_op jit(solution)/shard_map/all_gather | solution.py:310
  75.6 0.3 all-to-all-done.1.own_ref
  75.9 9.1 %collective-permute-start = (f32[16,64,128]{2,1,0:T(8,128)S(1)}, f32[16,64,128]{2,1,0:T(8,128)S(1)}, u32[]{:S(2)}, u32[]{:S(2)}) collective-permute-start(f32[16,64,128]{2,1,0:T(8,128)S(1)} %all-to-all-done.1.own_ref), channel_id=1, source_target_pairs={{0,256},{256,0},{1,257},{257,1},{2,258},{258,2},{3,259},{259,3},{4... | collective-permute-start | bytes 1572872 | tf_op jit(solution)/shard_map/ppermute | solution.py:312
  85.2 1.4 %collective-permute-done.other_ref = f32[16,64,128]{2,1,0:T(8,128)S(1)} collective-permute-done((f32[16,64,128]{2,1,0:T(8,128)S(1)}, f32[16,64,128]{2,1,0:T(8,128)S(1)}, u32[]{:S(2)}, u32[]{:S(2)}) %collective-permute-start) | collective-permute-done | bytes 524320 | tf_op jit(solution)/shard_map/ppermute | solution.py:312
  86.6 2.8 %shard_map.79 = (f32[64,128]{1,0:T(8,128)}, f32[4,64,128]{2,1,0:T(8,128)S(1)}, f32[16,16,128]{2,1,0:T(8,128)S(1)}, f32[16,16,128]{2,1,0:T(8,128)S(1)}) custom-call(s32[2]{0:T(128)S(1)} %pad_add_fusion.at_ref, f32[1024,128]{1,0:T(8,128)S(1)} %all_gather.11.hidden_ref, f32[16,64,128]{2,1,0:T(8,128)S(1)} %all-to-all-done.1.own_ref, ...), custom_call_target="tpu_custom_call" | custom-call | flops 1073741824 | bytes 2097152 | tf_op jit(solution)/shard_map/pallas_call | solution.py:208
  89.5 2.3 %collective-permute-start.1 = (f32[16,16,128]{2,1,0:T(8,128)S(1)}, f32[16,16,128]{2,1,0:T(8,128)S(1)}, u32[]{:S(2)}, u32[]{:S(2)}) collective-permute-start(f32[16,16,128]{2,1,0:T(8,128)S(1)} %get-tuple-element.20), channel_id=1, source_target_pairs={{0,256},{256,0},{1,257},{257,1},{2,258},{258,2},{3,259},{259,3},{4... | collective-permute-start | bytes 393224 | tf_op jit(solution)/shard_map/ppermute | solution.py:318
  91.7 8.1 %all_to_all.21.grad_ref = f32[4,64,128]{2,1,0:T(8,128)} all-to-all(f32[4,64,128]{2,1,0:T(8,128)S(1)} %get-tuple-element.18), channel_id=1, replica_groups=mesh['core'=2,'zl'=4,'y'=4,'x'=4,'zh'=4] {'x'}, dimensions={0} | all-to-all | bytes 262144 | tf_op jit(solution)/shard_map/all_to_all | solution.py:285
  99.9 0.6 copy-done.5
  100.5 1.9 %shard_map.80 = f32[16,80,128]{2,1,0:T(8,128)} custom-call(f32[4,64,128]{2,1,0:T(8,128)} %all_to_all.21.grad_ref, f32[16,16,128]{2,1,0:T(8,128)} %copy-done.1, f32[16,16,128]{2,1,0:T(8,128)} %copy-done.5), custom_call_target="tpu_custom_call" | custom-call | flops 1048576 | bytes 1048576 | tf_op jit(solution)/shard_map/pallas_call | solution.py:233
  102.4 7.2 %all-to-all-start.3 = ((f32[16,80,128]{2,1,0:T(8,128)}), f32[16,80,128]{2,1,0:T(8,128)S(1)}, u32[]{:S(2)}, u32[]{:S(2)}) async-start(f32[16,80,128]{2,1,0:T(8,128)} %shard_map.80), calls=%async_computation.3 | async-start | bytes 1310720 | tf_op jit(solution)/shard_map/all_to_all | solution.py:285
  109.7 0.1 rev.3.base_ref
  109.8 15.0 %all-to-all-done.3.source_ref = f32[16,80,128]{2,1,0:T(8,128)S(1)} async-done(((f32[16,80,128]{2,1,0:T(8,128)}), f32[16,80,128]{2,1,0:T(8,128)S(1)}, u32[]{:S(2)}, u32[]{:S(2)}) %all-to-all-start.3) | async-done | bytes 655392 | tf_op jit(solution)/shard_map/all_to_all | solution.py:285
  124.8 6.5 %shard_map.81 = (f32[64,2048]{1,0:T(8,128)S(1)}, f32[32,64]{1,0:T(8,128)}) custom-call(s32[2]{0:T(128)S(1)} %rev.3.base_ref, s32[1]{0:T(128)} %bitcast.10.count_ref, s32[2,256]{1,0:T(2,128)S(1)} %bitcast.14, f32[16,80,128]{2,1,0:T(8,128)S(1)} %all-to-all-done.3.source_ref), custom_call_target="tpu_custom_call" | custom-call | flops 8589934592 | bytes 2097152 | tf_op jit(solution)/shard_map/pallas_call | solution.py:139
  131.3 5.5 %collective-permute-start.2 = (f32[64,2048]{1,0:T(8,128)S(1)}, f32[64,2048]{1,0:T(8,128)S(1)}, u32[]{:S(2)}, u32[]{:S(2)}) collective-permute-start(f32[64,2048]{1,0:T(8,128)S(1)} %get-tuple-element.21), channel_id=1, source_target_pairs={{0,256},{256,0},{1,257},{257,1},{2,258},{258,2},{3,259},{259,3},{4... | collective-permute-start | bytes 1572872 | tf_op jit(solution)/shard_map/ppermute | solution.py:324
  136.8 1.5 %collective-permute-done.2 = f32[64,2048]{1,0:T(8,128)S(1)} collective-permute-done((f32[64,2048]{1,0:T(8,128)S(1)}, f32[64,2048]{1,0:T(8,128)S(1)}, u32[]{:S(2)}, u32[]{:S(2)}) %collective-permute-start.2) | collective-permute-done | bytes 524320 | tf_op jit(solution)/shard_map/ppermute | solution.py:324
  138.3 0.9 add.7
  (12 shorter events, 0.2 us)
Async XLA Ops:
  1.4 0.7 copy-start.3
  2.0 1.0 copy-start.2
  58.7 6.0 %copy-start.4 = (f32[256,128]{1,0:T(8,128)S(1)}, f32[256,128]{1,0:T(8,128)}, u32[]{:S(2)}) copy-start(f32[256,128]{1,0:T(8,128)} %get-tuple-element.13) | copy-start | bytes 393220
  58.7 17.2 %all-to-all-start.1 = ((f32[16,64,128]{2,1,0:T(8,128)}), f32[16,64,128]{2,1,0:T(8,128)S(1)}, u32[]{:S(2)}, u32[]{:S(2)}) async-start(f32[16,64,128]{2,1,0:T(8,128)} %get-tuple-element.14), calls=%async_computation.1 | async-start | bytes 1048576 | tf_op jit(solution)/shard_map/all_to_all | solution.py:285
  64.7 21.9 %copy-start = (f32[576,128]{1,0:T(8,128)S(1)}, f32[576,128]{1,0:T(8,128)}, u32[]{:S(2)}) copy-start(f32[576,128]{1,0:T(8,128)} %all-gather) | copy-start | bytes 884740
  75.9 10.7 %collective-permute-start = (f32[16,64,128]{2,1,0:T(8,128)S(1)}, f32[16,64,128]{2,1,0:T(8,128)S(1)}, u32[]{:S(2)}, u32[]{:S(2)}) collective-permute-start(f32[16,64,128]{2,1,0:T(8,128)S(1)} %all-to-all-done.1.own_ref), channel_id=1, source_target_pairs={{0,256},{256,0},{1,257},{257,1},{2,258},{258,2},{3,259},{259,3},{4... | collective-permute-start | bytes 1572872 | tf_op jit(solution)/shard_map/ppermute | solution.py:312
  89.5 10.4 %copy-start.1 = (f32[16,16,128]{2,1,0:T(8,128)}, f32[16,16,128]{2,1,0:T(8,128)S(1)}, u32[]{:S(2)}) copy-start(f32[16,16,128]{2,1,0:T(8,128)S(1)} %get-tuple-element.19.own_ref) | copy-start | bytes 393220
  89.5 10.4 %collective-permute-start.1 = (f32[16,16,128]{2,1,0:T(8,128)S(1)}, f32[16,16,128]{2,1,0:T(8,128)S(1)}, u32[]{:S(2)}, u32[]{:S(2)}) collective-permute-start(f32[16,16,128]{2,1,0:T(8,128)S(1)} %get-tuple-element.20), channel_id=1, source_target_pairs={{0,256},{256,0},{1,257},{257,1},{2,258},{258,2},{3,259},{259,3},{4... | collective-permute-start | bytes 393224 | tf_op jit(solution)/shard_map/ppermute | solution.py:318
  99.9 0.6 copy-start.5
  102.4 22.4 %all-to-all-start.3 = ((f32[16,80,128]{2,1,0:T(8,128)}), f32[16,80,128]{2,1,0:T(8,128)S(1)}, u32[]{:S(2)}, u32[]{:S(2)}) async-start(f32[16,80,128]{2,1,0:T(8,128)} %shard_map.80), calls=%async_computation.3 | async-start | bytes 1310720 | tf_op jit(solution)/shard_map/all_to_all | solution.py:285
  131.3 7.0 %collective-permute-start.2 = (f32[64,2048]{1,0:T(8,128)S(1)}, f32[64,2048]{1,0:T(8,128)S(1)}, u32[]{:S(2)}, u32[]{:S(2)}) collective-permute-start(f32[64,2048]{1,0:T(8,128)S(1)} %get-tuple-element.21), channel_id=1, source_target_pairs={{0,256},{256,0},{1,257},{257,1},{2,258},{258,2},{3,259},{259,3},{4... | collective-permute-start | bytes 1572872 | tf_op jit(solution)/shard_map/ppermute | solution.py:324

commit v8 on v7

--- a/solution.py
+++ b/solution.py
@@ -241,16 +241,19 @@
 
 def sum_kernel(parts_ref, weight_ref, turned_ref, out_ref):
     width, packed = parts_ref.shape[1], weight_ref.shape[0] // 2
-    out_ref[:width, :] = jnp.sum(parts_ref[...], axis=0)
-    out_ref[width:width + packed, :] = pack(weight_ref[...])
-    out_ref[width + packed:, :] = turned_ref[...]
-
-
-def sum_parts(parts, weight, turned):
+    total = jnp.sum(parts_ref[...], axis=0)
+    weight = pack(weight_ref[...])
+    for n in range(out_ref.shape[0]):
+        out_ref[n, :width, :] = total
+        out_ref[n, width:width + packed, :] = weight
+        out_ref[n, width + packed:, :] = turned_ref[...]
+
+
+def sum_parts(parts, weight, turned, n):
     rows = parts.shape[1] + weight.shape[0] // 2 + turned.shape[0]
     return pl.pallas_call(
         sum_kernel,
-        out_shape=jax.ShapeDtypeStruct((rows, parts.shape[2]), f32),
+        out_shape=jax.ShapeDtypeStruct((n, rows, parts.shape[2]), f32),
         in_specs=[VMEM] * 3,
         out_specs=VMEM,
         cost_estimate=cost(1 << 20, 1 << 20),
@@ -304,7 +307,7 @@
     partial = edge_product(
         bases, count, pairs, features, row_blocks, col_blocks, False, cols_poly, rows_poly, scale, width
     )
-    gathered = lax.all_gather(sum_parts(exchange(partial, nbr), weight, cotangent.T), "zh")
+    gathered = exchange(sum_parts(exchange(partial, nbr), weight, cotangent.T, n_zh), "zh")
     hidden_z, weight_z = deal(gathered, width, packed, n_nbr)
     own = exchange(weight_z, nbr)
     hidden_all = lax.all_gather(hidden_z, "x", axis=0, tiled=True)

time: 140 us -> 146 us (1.043)
  blocking collectives: 64.6 us -> 70 us
  waiting for transfers between devices: 18.3 us -> 20 us
    all_to_all x2 -> x3, blocking collectives: 30.9 us -> 58.8 us  [exchange(): return lax.all_to_all(value, axes, 0, 0)]
    all_gather x1 -> x0, blocking collectives: 22.8 us -> none  [per_device(): lax.all_gather(sum_parts(exchange(partial, nbr), weight, cotangent.T), 'zh')]
    ppermute x1, starting transfers between devices: 9.14 us -> 5.18 us  [per_device(): other = lax.ppermute(own, 'core', swap_core)]
    all_to_all x2, starting transfers between devices: 13.3 us -> 16.5 us  [exchange(): return lax.all_to_all(value, axes, 0, 0)]
    all_to_all x2, waiting for transfers between devices: 15.3 us -> 17 us  [exchange(): return lax.all_to_all(value, axes, 0, 0)]
where the time goes in v8:
time: 146 us
  blocking collectives  70 us (48%)
  starting transfers between devices  29.4 us (20%)
  Pallas kernels  21.4 us (15%)
  waiting for transfers between devices  20 us (14%)
  local copies, waits for them, and re-layouts  2.48 us (2%)
    all_to_all x3, blocking collectives, exchange(): return lax.all_to_all(value, axes, 0, 0)  58.8 us
    all_to_all x2, waiting for transfers between devices, exchange(): return lax.all_to_all(value, axes, 0, 0)  17 us
    all_to_all x2, starting transfers between devices, exchange(): return lax.all_to_all(value, axes, 0, 0)  16.5 us
    pallas_call x2, Pallas kernels, edge_product(): pl.pallas_call(functools.partial(product_kernel, lane_blocks, sub_blocks,...  12.9 us
    all_gather x1, blocking collectives, per_device(): hidden_all = lax.all_gather(hidden_z, 'x', axis=0, tiled=True)  11.2 us
    ppermute x1, starting transfers between devices, per_device(): feature_grad = column_part + lax.ppermute(column_part, 'core', swap_core)  5.49 us
    ppermute x1, starting transfers between devices, per_device(): other = lax.ppermute(own, 'core', swap_core)  5.18 us
  transfers between devices with their start and end apart: 5, of which 4 were waited for; matrix products, arithmetic and copies ran while one was open for 0% of the time, Pallas kernels for 0%

profile of v8, /device:TPU:1, one launch (start us, length us, event | category | flops | bytes accessed | tf_op | source)
XLA Modules:
  0.0 145.6 jit_solution(8403521201082495300)
XLA Ops:
  1.4 0.7 copy-done.3
  2.0 1.0 copy-done.2
  3.1 6.4 %shard_map.76 = f32[16,64,128]{2,1,0:T(8,128)S(1)} custom-call(s32[2]{0:T(128)S(1)} %pad_add_fusion.1.base_ref, s32[1]{0:T(128)} %bitcast.8.count_ref, s32[2,256]{1,0:T(2,128)S(1)} %bitcast.10, f32[64,2048]{1,0:T(8,128)S(1)} %copy-done.2), custom_call_target="tpu_custom_call" | custom-call | flops 8589934592 | bytes 2097152 | tf_op jit(solution)/shard_map/pallas_call | solution.py:139
  9.5 22.8 %all_to_all.25.parts_ref = f32[16,64,128]{2,1,0:T(8,128)} all-to-all(f32[16,64,128]{2,1,0:T(8,128)S(1)} %shard_map.76), channel_id=1, replica_groups=mesh['core'=2,'zl'=4,'y'=4,'x'=4,'zh'=4] {'zl','y'}, dimensions={0} | all-to-all | bytes 1048576 | tf_op jit(solution)/shard_map/all_to_all | solution.py:288
  32.3 1.8 %shard_map.77 = f32[4,144,128]{2,1,0:T(8,128)} custom-call(f32[16,64,128]{2,1,0:T(8,128)} %all_to_all.25.parts_ref, f32[32,64]{1,0:T(8,128)} %weight_ref.1, f32[64,128]{1,0:T(8,128)} %bitcast.12), custom_call_target="tpu_custom_call" | custom-call | flops 1048576 | bytes 1048576 | tf_op jit(solution)/shard_map/pallas_call | solution.py:254
  34.1 27.3 %all_to_all.26.gathered_ref.both_ref = f32[4,144,128]{2,1,0:T(8,128)} all-to-all(f32[4,144,128]{2,1,0:T(8,128)} %shard_map.77), channel_id=1, replica_groups=mesh['core'=2,'zl'=4,'y'=4,'x'=4,'zh'=4] {'zh'}, dimensions={0} | all-to-all | bytes 589824 | tf_op jit(solution)/shard_map/all_to_all | solution.py:288
  61.5 1.8 %shard_map.78 = (f32[256,128]{1,0:T(8,128)}, f32[16,64,128]{2,1,0:T(8,128)}) custom-call(f32[4,144,128]{2,1,0:T(8,128)} %all_to_all.26.gathered_ref.both_ref), custom_call_target="tpu_custom_call" | custom-call | flops 1048576 | bytes 1048576 | tf_op jit(solution)/shard_map/pallas_call | solution.py:275
  63.3 11.1 %all-to-all-start.2 = ((f32[16,64,128]{2,1,0:T(8,128)}), f32[16,64,128]{2,1,0:T(8,128)S(1)}, u32[]{:S(2)}, u32[]{:S(2)}) async-start(f32[16,64,128]{2,1,0:T(8,128)} %get-tuple-element.14), calls=%async_computation.2 | async-start | bytes 1048576 | tf_op jit(solution)/shard_map/all_to_all | solution.py:288
  74.5 11.2 %all_gather.3.hidden_ref = f32[1024,128]{1,0:T(8,128)S(1)} all-gather(f32[256,128]{1,0:T(8,128)S(1)} %copy-done.4), channel_id=1, replica_groups=mesh['core'=2,'zl'=4,'y'=4,'x'=4,'zh'=4] {'x'}, dimensions={0}, use_global_device_ids=true | all-gather | bytes 655360 | tf_op jit(solution)/shard_map/all_gather | solution.py:313
  85.6 2.0 %all-to-all-done.2.own_ref = f32[16,64,128]{2,1,0:T(8,128)S(1)} async-done(((f32[16,64,128]{2,1,0:T(8,128)}), f32[16,64,128]{2,1,0:T(8,128)S(1)}, u32[]{:S(2)}, u32[]{:S(2)}) %all-to-all-start.2) | async-done | bytes 524320 | tf_op jit(solution)/shard_map/all_to_all | solution.py:288
  87.6 5.2 %collective-permute-start = (f32[16,64,128]{2,1,0:T(8,128)S(1)}, f32[16,64,128]{2,1,0:T(8,128)S(1)}, u32[]{:S(2)}, u32[]{:S(2)}) collective-permute-start(f32[16,64,128]{2,1,0:T(8,128)S(1)} %all-to-all-done.2.own_ref), channel_id=1, source_target_pairs={{0,256},{256,0},{1,257},{257,1},{2,258},{258,2},{3,259},{259,3},{4... | collective-permute-start | bytes 1572872 | tf_op jit(solution)/shard_map/ppermute | solution.py:315
  92.9 1.4 collective-permute-done.other_ref
  94.3 2.8 %shard_map.79 = (f32[64,128]{1,0:T(8,128)}, f32[4,64,128]{2,1,0:T(8,128)S(1)}, f32[16,16,128]{2,1,0:T(8,128)S(1)}, f32[16,16,128]{2,1,0:T(8,128)S(1)}) custom-call(s32[2]{0:T(128)S(1)} %pad_add_fusion.at_ref, f32[1024,128]{1,0:T(8,128)S(1)} %all_gather.3.hidden_ref, f32[16,64,128]{2,1,0:T(8,128)S(1)} %all-to-all-done.2.own_ref, ...), custom_call_target="tpu_custom_call" | custom-call | flops 1073741824 | bytes 2097152 | tf_op jit(solution)/shard_map/pallas_call | solution.py:208
  97.2 2.3 %collective-permute-start.1 = (f32[16,16,128]{2,1,0:T(8,128)S(1)}, f32[16,16,128]{2,1,0:T(8,128)S(1)}, u32[]{:S(2)}, u32[]{:S(2)}) collective-permute-start(f32[16,16,128]{2,1,0:T(8,128)S(1)} %get-tuple-element.20), channel_id=1, source_target_pairs={{0,256},{256,0},{1,257},{257,1},{2,258},{258,2},{3,259},{259,3},{4... | collective-permute-start | bytes 393224 | tf_op jit(solution)/shard_map/ppermute | solution.py:321
  99.5 8.7 %all_to_all.27.grad_ref = f32[4,64,128]{2,1,0:T(8,128)} all-to-all(f32[4,64,128]{2,1,0:T(8,128)S(1)} %get-tuple-element.18), channel_id=1, replica_groups=mesh['core'=2,'zl'=4,'y'=4,'x'=4,'zh'=4] {'x'}, dimensions={0} | all-to-all | bytes 262144 | tf_op jit(solution)/shard_map/all_to_all | solution.py:288
  108.2 0.6 copy-done.5
  108.9 1.9 %shard_map.80 = f32[16,80,128]{2,1,0:T(8,128)} custom-call(f32[4,64,128]{2,1,0:T(8,128)} %all_to_all.27.grad_ref, f32[16,16,128]{2,1,0:T(8,128)} %copy-done.1, f32[16,16,128]{2,1,0:T(8,128)} %copy-done.5), custom_call_target="tpu_custom_call" | custom-call | flops 1048576 | bytes 1048576 | tf_op jit(solution)/shard_map/pallas_call | solution.py:233
  110.8 5.3 %all-to-all-start.4 = ((f32[16,80,128]{2,1,0:T(8,128)}), f32[16,80,128]{2,1,0:T(8,128)S(1)}, u32[]{:S(2)}, u32[]{:S(2)}) async-start(f32[16,80,128]{2,1,0:T(8,128)} %shard_map.80), calls=%async_computation.4 | async-start | bytes 1310720 | tf_op jit(solution)/shard_map/all_to_all | solution.py:288
  116.1 0.1 rev.3.base_ref
  116.2 15.0 %all-to-all-done.4.source_ref = f32[16,80,128]{2,1,0:T(8,128)S(1)} async-done(((f32[16,80,128]{2,1,0:T(8,128)}), f32[16,80,128]{2,1,0:T(8,128)S(1)}, u32[]{:S(2)}, u32[]{:S(2)}) %all-to-all-start.4) | async-done | bytes 655392 | tf_op jit(solution)/shard_map/all_to_all | solution.py:288
  131.2 6.5 %shard_map.81 = (f32[64,2048]{1,0:T(8,128)S(1)}, f32[32,64]{1,0:T(8,128)}) custom-call(s32[2]{0:T(128)S(1)} %rev.3.base_ref, s32[1]{0:T(128)} %bitcast.9.count_ref, s32[2,256]{1,0:T(2,128)S(1)} %bitcast.11, f32[16,80,128]{2,1,0:T(8,128)S(1)} %all-to-all-done.4.source_ref), custom_call_target="tpu_custom_call" | custom-call | flops 8589934592 | bytes 2097152 | tf_op jit(solution)/shard_map/pallas_call | solution.py:139
  137.7 5.5 %collective-permute-start.2 = (f32[64,2048]{1,0:T(8,128)S(1)}, f32[64,2048]{1,0:T(8,128)S(1)}, u32[]{:S(2)}, u32[]{:S(2)}) collective-permute-start(f32[64,2048]{1,0:T(8,128)S(1)} %get-tuple-element.21), channel_id=1, source_target_pairs={{0,256},{256,0},{1,257},{257,1},{2,258},{258,2},{3,259},{259,3},{4... | collective-permute-start | bytes 1572872 | tf_op jit(solution)/shard_map/ppermute | solution.py:327
  143.2 1.5 %collective-permute-done.2 = f32[64,2048]{1,0:T(8,128)S(1)} collective-permute-done((f32[64,2048]{1,0:T(8,128)S(1)}, f32[64,2048]{1,0:T(8,128)S(1)}, u32[]{:S(2)}, u32[]{:S(2)}) %collective-permute-start.2) | collective-permute-done | bytes 524320 | tf_op jit(solution)/shard_map/ppermute | solution.py:327
  144.7 0.9 add.7
  (12 shorter events, 0.2 us)
Async XLA Ops:
  1.4 0.7 copy-start.3
  2.0 1.0 copy-start.2
  63.3 11.2 %copy-start.4 = (f32[256,128]{1,0:T(8,128)S(1)}, f32[256,128]{1,0:T(8,128)}, u32[]{:S(2)}) copy-start(f32[256,128]{1,0:T(8,128)} %get-tuple-element.13) | copy-start | bytes 393220
  63.3 24.3 %all-to-all-start.2 = ((f32[16,64,128]{2,1,0:T(8,128)}), f32[16,64,128]{2,1,0:T(8,128)S(1)}, u32[]{:S(2)}, u32[]{:S(2)}) async-start(f32[16,64,128]{2,1,0:T(8,128)} %get-tuple-element.14), calls=%async_computation.2 | async-start | bytes 1048576 | tf_op jit(solution)/shard_map/all_to_all | solution.py:288
  74.5 19.9 %copy-start = (f32[4,144,128]{2,1,0:T(8,128)S(1)}, f32[4,144,128]{2,1,0:T(8,128)}, u32[]{:S(2)}) copy-start(f32[4,144,128]{2,1,0:T(8,128)} %all_to_all.26.gathered_ref.both_ref) | copy-start | bytes 884740
  87.6 6.7 %collective-permute-start = (f32[16,64,128]{2,1,0:T(8,128)S(1)}, f32[16,64,128]{2,1,0:T(8,128)S(1)}, u32[]{:S(2)}, u32[]{:S(2)}) collective-permute-start(f32[16,64,128]{2,1,0:T(8,128)S(1)} %all-to-all-done.2.own_ref), channel_id=1, source_target_pairs={{0,256},{256,0},{1,257},{257,1},{2,258},{258,2},{3,259},{259,3},{4... | collective-permute-start | bytes 1572872 | tf_op jit(solution)/shard_map/ppermute | solution.py:315
  97.2 11.0 %copy-start.1 = (f32[16,16,128]{2,1,0:T(8,128)}, f32[16,16,128]{2,1,0:T(8,128)S(1)}, u32[]{:S(2)}) copy-start(f32[16,16,128]{2,1,0:T(8,128)S(1)} %get-tuple-element.19.own_ref) | copy-start | bytes 393220
  97.2 11.0 %collective-permute-start.1 = (f32[16,16,128]{2,1,0:T(8,128)S(1)}, f32[16,16,128]{2,1,0:T(8,128)S(1)}, u32[]{:S(2)}, u32[]{:S(2)}) collective-permute-start(f32[16,16,128]{2,1,0:T(8,128)S(1)} %get-tuple-element.20), channel_id=1, source_target_pairs={{0,256},{256,0},{1,257},{257,1},{2,258},{258,2},{3,259},{259,3},{4... | collective-permute-start | bytes 393224 | tf_op jit(solution)/shard_map/ppermute | solution.py:321
  108.2 0.6 copy-start.5
  110.8 20.4 %all-to-all-start.4 = ((f32[16,80,128]{2,1,0:T(8,128)}), f32[16,80,128]{2,1,0:T(8,128)S(1)}, u32[]{:S(2)}, u32[]{:S(2)}) async-start(f32[16,80,128]{2,1,0:T(8,128)} %shard_map.80), calls=%async_computation.4 | async-start | bytes 1310720 | tf_op jit(solution)/shard_map/all_to_all | solution.py:288
  137.7 7.0 %collective-permute-start.2 = (f32[64,2048]{1,0:T(8,128)S(1)}, f32[64,2048]{1,0:T(8,128)S(1)}, u32[]{:S(2)}, u32[]{:S(2)}) collective-permute-start(f32[64,2048]{1,0:T(8,128)S(1)} %get-tuple-element.21), channel_id=1, source_target_pairs={{0,256},{256,0},{1,257},{257,1},{2,258},{258,2},{3,259},{259,3},{4... | collective-permute-start | bytes 1572872 | tf_op jit(solution)/shard_map/ppermute | solution.py:327

commit v9 on v6

--- a/solution.py
+++ b/solution.py
@@ -179,7 +179,7 @@
             wide = [beside([p[..., :width] for p in pair]), beside([p[..., width:] for p in pair])]
             wide = jnp.concatenate(wide, axis=1).reshape(half * rows, 2 * width)
             weight[pl.ds(pl.multiple_of(which * half * rows, 8), half * rows), z * width:(z + 2) * width] = wide
-    cotangent = jnp.concatenate([both_ref[z, packed:, :] for z in range(n_zh)], axis=0).T
+    cotangent = jnp.concatenate([both_ref[z, width + packed:, :] for z in range(n_zh)], axis=0).T
 
     pre = dot3(hidden_ref[...].T, weight[...])
     squash = 1.0 / (1.0 + jnp.exp(-pre))
@@ -220,25 +220,6 @@
     )(at, hidden_all, own, other, both)
 
 
-def join_kernel(grad_ref, own_ref, other_ref, out_ref):
-    width = grad_ref.shape[1]
-    grad = jnp.sum(grad_ref[...], axis=0)
-    for n in range(out_ref.shape[0]):
-        out_ref[n, :width, :] = grad
-    out_ref[:, width:, :] = own_ref[...] + other_ref[...]
-
-
-def join(grad_terms, own_terms, other_terms):
-    n, packed, lanes = own_terms.shape
-    return pl.pallas_call(
-        join_kernel,
-        out_shape=jax.ShapeDtypeStruct((n, grad_terms.shape[1] + packed, lanes), f32),
-        in_specs=[VMEM] * 3,
-        out_specs=VMEM,
-        cost_estimate=cost(1 << 20, 1 << 20),
-    )(grad_terms, own_terms, other_terms)
-
-
 def copies(value, n):
     return jnp.broadcast_to(value[None], (n,) + value.shape)
 
@@ -262,31 +243,27 @@
 
     rows_poly, cols_poly = (3, 11), (5, 13)
     packed = weight.shape[0] // 2
-    both = jnp.concatenate([pack(weight), cotangent.T], axis=0)
-
     bases = jnp.stack([nbr_id * c_dev, core * r_dev]).astype(i32)
     partial = edge_product(
         bases, count, pairs, features, row_blocks, col_blocks, False, cols_poly, rows_poly, scale, width
     )
-    both, partial = lax.optimization_barrier((both, partial))
-    both_z = lax.all_gather(both, "zh")
-    partial, both_z = lax.optimization_barrier((exchange(partial, nbr), both_z))
-    hidden = jnp.sum(partial, axis=0)
-    weight_z = both_z[:, :packed].reshape(-1, TILE)
-    hidden, weight_z = lax.optimization_barrier((hidden, copies(weight_z, n_nbr)))
-    own = exchange(weight_z, nbr)
-    hidden_z = lax.all_gather(hidden, "zh", axis=0, tiled=True)
-    hidden_z, own = lax.optimization_barrier((hidden_z, own))
+    hidden = jnp.sum(exchange(partial, nbr), axis=0)
+    gathered = lax.all_gather(jnp.concatenate([hidden, pack(weight), cotangent.T], axis=0), "zh")
+    weight_z = gathered[:, width:width + packed].reshape(-1, TILE)
+    hidden_z = gathered[:, :width].reshape(-1, n_rows)
+    own = exchange(copies(weight_z, n_nbr), nbr)
+    hidden_all = lax.all_gather(hidden_z, "x", axis=0, tiled=True)
+    hidden_all, own = lax.optimization_barrier((hidden_all, own))
     other = lax.ppermute(own, "core", swap_core)
-    hidden_all = lax.all_gather(hidden_z, "x", axis=0, tiled=True)
 
     at = jnp.stack([core, lax.axis_index("zh")]).astype(i32)
     activations, grad_terms, own_terms, other_terms = layer(
-        at, hidden_all, own, other, both_z, n_x, n_zh, weight.shape[0]
+        at, hidden_all, own, other, gathered, n_x, n_zh, weight.shape[0]
     )
     other_terms = lax.ppermute(other_terms, "core", swap_core)
     grad_terms = exchange(grad_terms, "x")
-    grad_block = exchange(join(grad_terms, own_terms, other_terms), nbr)
+    grad_hidden = copies(jnp.sum(grad_terms, axis=0), n_nbr)
+    grad_block = exchange(jnp.concatenate([grad_hidden, own_terms + other_terms], axis=1), nbr)
     column_part, weight_grad = edge_product(
         bases[::-1], count, pairs, grad_block, col_blocks, row_blocks, True, rows_poly, cols_poly, scale, width
     )

time: 150 us -> 136 us (0.907)
  blocking collectives: 60.9 us -> 41.3 us
  waiting for transfers between devices: 16.7 us -> 31.8 us
  starting transfers between devices: 47.5 us -> 39 us
  Pallas kernels: 18.5 us -> 16.6 us
    all_gather x2 -> x1, blocking collectives: 41.4 us -> 22.2 us  [per_device(): lax.all_gather(jnp.concatenate([hidden, pack(weight), cotangent.T], axis=...]
    all_to_all x3, waiting for transfers between devices: 15.2 us -> 28.9 us  [exchange(): return lax.all_to_all(value, axes, 0, 0)]
    all_to_all x3, starting transfers between devices: 29.3 us -> 22.9 us  [exchange(): return lax.all_to_all(value, axes, 0, 0)]
    ppermute x1, starting transfers between devices: 4.41 us -> 2.27 us  [per_device(): other_terms = lax.ppermute(other_terms, 'core', swap_core)]
    pallas_call x1 -> x0, Pallas kernels: 1.92 us -> none  [join(): pl.pallas_call(join_kernel, out_shape=jax.ShapeDtypeStruct((n, grad_terms...]
  transfers between devices with their start and end apart: 6 -> 6, of which waited for: 2 -> 5; matrix products, arithmetic and copies ran while one was open for 0% -> 0% of each run, Pallas kernels for 0% -> 0%
where the time goes in v9:
time: 136 us; the launch traced here: 135 us
  blocking collectives  41.3 us (30%)
  starting transfers between devices  39 us (29%)
  waiting for transfers between devices  31.8 us (23%)
  Pallas kernels  16.6 us (12%)
  local copies, waits for them, and re-layouts  2.74 us (2%)
  other arithmetic  2.05 us (2%)
  between operations  1.42 us (1%)
    all_to_all x3, waiting for transfers between devices, exchange(): return lax.all_to_all(value, axes, 0, 0)  28.9 us
    all_to_all x3, starting transfers between devices, exchange(): return lax.all_to_all(value, axes, 0, 0)  22.9 us
    all_gather x1, blocking collectives, per_device(): lax.all_gather(jnp.concatenate([hidden, pack(weight), cotangent.T], axis=...  22.2 us
    pallas_call x2, Pallas kernels, edge_product(): pl.pallas_call(functools.partial(product_kernel, lane_blocks, sub_blocks,...  13.8 us
    all_gather x1, blocking collectives, per_device(): hidden_all = lax.all_gather(hidden_z, 'x', axis=0, tiled=True)  11 us
    ppermute x1, starting transfers between devices, per_device(): other = lax.ppermute(own, 'core', swap_core)  8.41 us
    all_to_all x1, blocking collectives, exchange(): return lax.all_to_all(value, axes, 0, 0)  8.12 us
    ppermute x1, starting transfers between devices, per_device(): feature_grad = column_part + lax.ppermute(column_part, 'core', swap_core)  5.49 us
  transfers between devices with their start and end apart: 6, of which 5 were waited for; matrix products, arithmetic and copies ran while one was open for 0% of the time, Pallas kernels for 0%

profile of v9, /device:TPU:1, one launch (start us, length us, event | category | flops | bytes accessed | tf_op | source)
XLA Modules:
  0.0 135.0 jit_solution(10530504064836629821)
XLA Ops:
  1.4 0.7 copy-done.1
  2.0 1.0 copy-done
  3.1 7.3 %shard_map.76 = f32[16,64,128]{2,1,0:T(8,128)} custom-call(s32[2]{0:T(128)S(1)} %pad_add_fusion.1.base_ref, s32[1]{0:T(128)} %bitcast.11.count_ref, s32[2,256]{1,0:T(2,128)S(1)} %bitcast.16, f32[64,2048]{1,0:T(8,128)S(1)} %copy-done), custom_call_target="tpu_custom_call" | custom-call | flops 8589934592 | bytes 2097152 | tf_op jit(solution)/shard_map/pallas_call | solution.py:139
  10.4 9.3 %all-to-all-start = ((f32[16,64,128]{2,1,0:T(8,128)}), f32[16,64,128]{2,1,0:T(8,128)S(1)}, u32[]{:S(2)}, u32[]{:S(2)}) async-start(f32[16,64,128]{2,1,0:T(8,128)} %shard_map.76), calls=%async_computation | async-start | bytes 1048576 | tf_op jit(solution)/shard_map/all_to_all | solution.py:228
  19.7 13.6 %all-to-all-done = f32[16,64,128]{2,1,0:T(8,128)S(1)} async-done(((f32[16,64,128]{2,1,0:T(8,128)}), f32[16,64,128]{2,1,0:T(8,128)S(1)}, u32[]{:S(2)}, u32[]{:S(2)}) %all-to-all-start) | async-done | bytes 524320 | tf_op jit(solution)/shard_map/all_to_all | solution.py:228
  33.4 0.1 pad_maximum_fusion.1
  33.5 22.2 %all-gather = f32[576,128]{1,0:T(8,128)S(1)} all-gather(f32[144,128]{1,0:T(8,128)S(1)} %pad_maximum_fusion.1), channel_id=2, replica_groups=mesh['core'=2,'zl'=4,'y'=4,'x'=4,'zh'=4] {'zh'}, dimensions={0}, use_global_device_ids=true | all-gather | bytes 368640 | tf_op jit(solution)/shard_map/all_gather | solution.py:251
  55.7 0.8 broadcast_in_dim.14
  56.5 6.2 %all-to-all-start.1 = ((f32[16,64,128]{2,1,0:T(8,128)}), f32[16,64,128]{2,1,0:T(8,128)S(1)}, u32[]{:S(2)}, u32[]{:S(2)}) async-start(f32[16,64,128]{2,1,0:T(8,128)} %broadcast_in_dim.14), calls=%async_computation.1 | async-start | bytes 1048576 | tf_op jit(solution)/shard_map/all_to_all | solution.py:228
  62.8 11.0 %all_gather.11.hidden_ref = f32[1024,128]{1,0:T(8,128)S(1)} all-gather(f32[256,128]{1,0:T(8,128)S(1)} %bitcast.18), channel_id=1, replica_groups=mesh['core'=2,'zl'=4,'y'=4,'x'=4,'zh'=4] {'x'}, dimensions={0}, use_global_device_ids=true | all-gather | bytes 655360 | tf_op jit(solution)/shard_map/all_gather | solution.py:255
  73.7 0.3 all-to-all-done.1.own_ref
  74.0 8.4 %collective-permute-start = (f32[16,64,128]{2,1,0:T(8,128)S(1)}, f32[16,64,128]{2,1,0:T(8,128)S(1)}, u32[]{:S(2)}, u32[]{:S(2)}) collective-permute-start(f32[16,64,128]{2,1,0:T(8,128)S(1)} %all-to-all-done.1.own_ref), channel_id=1, source_target_pairs={{0,256},{256,0},{1,257},{257,1},{2,258},{258,2},{3,259},{259,3},{4... | collective-permute-start | bytes 1572872 | tf_op jit(solution)/shard_map/ppermute | solution.py:257
  82.5 1.4 %collective-permute-done.other_ref = f32[16,64,128]{2,1,0:T(8,128)S(1)} collective-permute-done((f32[16,64,128]{2,1,0:T(8,128)S(1)}, f32[16,64,128]{2,1,0:T(8,128)S(1)}, u32[]{:S(2)}, u32[]{:S(2)}) %collective-permute-start) | collective-permute-done | bytes 524320 | tf_op jit(solution)/shard_map/ppermute | solution.py:257
  83.9 2.8 %shard_map.77 = (f32[64,128]{1,0:T(8,128)}, f32[4,64,128]{2,1,0:T(8,128)S(1)}, f32[16,16,128]{2,1,0:T(8,128)S(1)}, f32[16,16,128]{2,1,0:T(8,128)S(1)}) custom-call(s32[2]{0:T(128)S(1)} %pad_add_fusion.at_ref, f32[1024,128]{1,0:T(8,128)S(1)} %all_gather.11.hidden_ref, f32[16,64,128]{2,1,0:T(8,128)S(1)} %all-to-all-done.1.own_ref, ...), custom_call_target="tpu_custom_call" | custom-call | flops 1073741824 | bytes 2097152 | tf_op jit(solution)/shard_map/pallas_call | solution.py:208
  86.8 2.3 %collective-permute-start.1 = (f32[16,16,128]{2,1,0:T(8,128)S(1)}, f32[16,16,128]{2,1,0:T(8,128)S(1)}, u32[]{:S(2)}, u32[]{:S(2)}) collective-permute-start(f32[16,16,128]{2,1,0:T(8,128)S(1)} %get-tuple-element.16), channel_id=1, source_target_pairs={{0,256},{256,0},{1,257},{257,1},{2,258},{258,2},{3,259},{259,3},{4... | collective-permute-start | bytes 393224 | tf_op jit(solution)/shard_map/ppermute | solution.py:263
  89.1 8.1 %all_to_all.20 = f32[4,64,128]{2,1,0:T(8,128)S(1)} all-to-all(f32[4,64,128]{2,1,0:T(8,128)S(1)} %get-tuple-element.14), channel_id=1, replica_groups=mesh['core'=2,'zl'=4,'y'=4,'x'=4,'zh'=4] {'x'}, dimensions={0} | all-to-all | bytes 262144 | tf_op jit(solution)/shard_map/all_to_all | solution.py:228
  97.3 0.9 pad_maximum_fusion
  98.2 7.4 %all-to-all-start.3 = ((f32[16,80,128]{2,1,0:T(8,128)}), f32[16,80,128]{2,1,0:T(8,128)S(1)}, u32[]{:S(2)}, u32[]{:S(2)}) async-start(f32[16,80,128]{2,1,0:T(8,128)} %pad_maximum_fusion), calls=%async_computation.3 | async-start | bytes 1310720 | tf_op jit(solution)/shard_map/all_to_all | solution.py:228
  105.5 0.1 rev.3.base_ref
  105.6 15.0 %all-to-all-done.3.source_ref = f32[16,80,128]{2,1,0:T(8,128)S(1)} async-done(((f32[16,80,128]{2,1,0:T(8,128)}), f32[16,80,128]{2,1,0:T(8,128)S(1)}, u32[]{:S(2)}, u32[]{:S(2)}) %all-to-all-start.3) | async-done | bytes 655392 | tf_op jit(solution)/shard_map/all_to_all | solution.py:228
  120.7 6.5 %shard_map.78 = (f32[64,2048]{1,0:T(8,128)S(1)}, f32[32,64]{1,0:T(8,128)}) custom-call(s32[2]{0:T(128)S(1)} %rev.3.base_ref, s32[1]{0:T(128)} %bitcast.12.count_ref, s32[2,256]{1,0:T(2,128)S(1)} %bitcast.17, f32[16,80,128]{2,1,0:T(8,128)S(1)} %all-to-all-done.3.source_ref), custom_call_target="tpu_custom_call" | custom-call | flops 8589934592 | bytes 2097152 | tf_op jit(solution)/shard_map/pallas_call | solution.py:139
  127.2 5.5 %collective-permute-start.2 = (f32[64,2048]{1,0:T(8,128)S(1)}, f32[64,2048]{1,0:T(8,128)S(1)}, u32[]{:S(2)}, u32[]{:S(2)}) collective-permute-start(f32[64,2048]{1,0:T(8,128)S(1)} %get-tuple-element.17), channel_id=1, source_target_pairs={{0,256},{256,0},{1,257},{257,1},{2,258},{258,2},{3,259},{259,3},{4... | collective-permute-start | bytes 1572872 | tf_op jit(solution)/shard_map/ppermute | solution.py:270
  132.7 1.5 %collective-permute-done.2 = f32[64,2048]{1,0:T(8,128)S(1)} collective-permute-done((f32[64,2048]{1,0:T(8,128)S(1)}, f32[64,2048]{1,0:T(8,128)S(1)}, u32[]{:S(2)}, u32[]{:S(2)}) %collective-permute-start.2) | collective-permute-done | bytes 524320 | tf_op jit(solution)/shard_map/ppermute | solution.py:270
  134.2 0.9 add.11
  (16 shorter events, 0.3 us)
Async XLA Ops:
  1.4 0.7 copy-start.1
  2.0 1.0 copy-start
  10.4 9.3 %copy-start.3 = (f32[32,64]{1,0:T(8,128)S(1)}, f32[32,64]{1,0:T(8,128)}, u32[]{:S(2)}) copy-start(f32[32,64]{1,0:T(8,128)} %param.8) | copy-start | bytes 24580
  10.4 23.0 %all-to-all-start = ((f32[16,64,128]{2,1,0:T(8,128)}), f32[16,64,128]{2,1,0:T(8,128)S(1)}, u32[]{:S(2)}, u32[]{:S(2)}) async-start(f32[16,64,128]{2,1,0:T(8,128)} %shard_map.76), calls=%async_computation | async-start | bytes 1048576 | tf_op jit(solution)/shard_map/all_to_all | solution.py:228
  19.7 13.7 %copy-start.2 = (f32[128,64]{0,1:T(8,128)S(1)}, f32[128,64]{0,1:T(8,128)}, u32[]{:S(2)}) copy-start(f32[128,64]{0,1:T(8,128)} %param.9) | copy-start | bytes 98308
  56.5 17.5 %all-to-all-start.1 = ((f32[16,64,128]{2,1,0:T(8,128)}), f32[16,64,128]{2,1,0:T(8,128)S(1)}, u32[]{:S(2)}, u32[]{:S(2)}) async-start(f32[16,64,128]{2,1,0:T(8,128)} %broadcast_in_dim.14), calls=%async_computation.1 | async-start | bytes 1048576 | tf_op jit(solution)/shard_map/all_to_all | solution.py:228
  74.0 9.9 %collective-permute-start = (f32[16,64,128]{2,1,0:T(8,128)S(1)}, f32[16,64,128]{2,1,0:T(8,128)S(1)}, u32[]{:S(2)}, u32[]{:S(2)}) collective-permute-start(f32[16,64,128]{2,1,0:T(8,128)S(1)} %all-to-all-done.1.own_ref), channel_id=1, source_target_pairs={{0,256},{256,0},{1,257},{257,1},{2,258},{258,2},{3,259},{259,3},{4... | collective-permute-start | bytes 1572872 | tf_op jit(solution)/shard_map/ppermute | solution.py:257
  86.8 10.4 %collective-permute-start.1 = (f32[16,16,128]{2,1,0:T(8,128)S(1)}, f32[16,16,128]{2,1,0:T(8,128)S(1)}, u32[]{:S(2)}, u32[]{:S(2)}) collective-permute-start(f32[16,16,128]{2,1,0:T(8,128)S(1)} %get-tuple-element.16), channel_id=1, source_target_pairs={{0,256},{256,0},{1,257},{257,1},{2,258},{258,2},{3,259},{259,3},{4... | collective-permute-start | bytes 393224 | tf_op jit(solution)/shard_map/ppermute | solution.py:263
  98.2 22.5 %all-to-all-start.3 = ((f32[16,80,128]{2,1,0:T(8,128)}), f32[16,80,128]{2,1,0:T(8,128)S(1)}, u32[]{:S(2)}, u32[]{:S(2)}) async-start(f32[16,80,128]{2,1,0:T(8,128)} %pad_maximum_fusion), calls=%async_computation.3 | async-start | bytes 1310720 | tf_op jit(solution)/shard_map/all_to_all | solution.py:228
  127.2 7.0 %collective-permute-start.2 = (f32[64,2048]{1,0:T(8,128)S(1)}, f32[64,2048]{1,0:T(8,128)S(1)}, u32[]{:S(2)}, u32[]{:S(2)}) collective-permute-start(f32[64,2048]{1,0:T(8,128)S(1)} %get-tuple-element.17), channel_id=1, source_target_pairs={{0,256},{256,0},{1,257},{257,1},{2,258},{258,2},{3,259},{259,3},{4... | collective-permute-start | bytes 1572872 | tf_op jit(solution)/shard_map/ppermute | solution.py:270

commit v10 on v9

--- a/solution.py
+++ b/solution.py
@@ -82,20 +82,28 @@
 
 def product_kernel(
     lane_blocks, sub_blocks, swap, sub_poly, lane_poly, scale, width,
-    base_ref, count_ref, pairs_ref, source_ref, out_ref, *refs,
+    base_ref, count_ref, pairs_ref, source_ref, *refs,
 ):
     sub_table, step_table, growth_table, lane_table, mask_table, source_parts = refs[-6:]
+    if not swap:
+        out_ref, fetched, arrived = refs[:3]
+        fetch = pltpu.make_async_copy(source_ref, fetched, arrived)
+        fetch.start()
     sub_base, lane_base = base_ref[0], base_ref[1]
     mask_table[...] = listed_tiles(swap, sub_blocks, count_ref, pairs_ref, lane_blocks * sub_blocks)
     for l, table in enumerate(sub_turns(sub_base, sub_blocks, sub_poly)):
+        sub_table[l * TILE:(l + 1) * TILE, :] = table
+
+    step_table[...], growth_table[...] = step_turns(lane_base)
+    if swap:
+        out_ref = refs[0]
+        refs[1][...] = unpack(jnp.sum(source_ref[:, width:, :], axis=0))
+    else:
+        fetch.wait()
+    for l in range(sub_blocks):
         columns = slice(l * TILE, (l + 1) * TILE)
-        sub_table[columns, :] = table
-        piece = source_ref[l, :width, :] if swap else source_ref[:, columns]
+        piece = source_ref[l, :width, :] if swap else fetched[:, columns]
         source_parts[:width, columns], source_parts[width:, columns] = split(piece)
-    if swap:
-        refs[0][...] = unpack(jnp.sum(source_ref[:, width:, :], axis=0))
-
-    step_table[...], growth_table[...] = step_turns(lane_base)
 
     def block(j, carry):
         lane_table[...] = lane_turns(j, sub_base, lane_base, sub_blocks, lane_poly)
@@ -119,7 +127,7 @@
             out_ref[j] = result
         return carry
 
-    lax.fori_loop(0, lane_blocks, block, 0, unroll=4)
+    lax.fori_loop(0, lane_blocks, block, 0, unroll=16)
 
 
 SMEM, VMEM = pl.BlockSpec(memory_space=pltpu.SMEM), pl.BlockSpec(memory_space=pltpu.VMEM)
@@ -136,12 +144,13 @@
             jax.ShapeDtypeStruct((width, lane_blocks * TILE), f32),
             jax.ShapeDtypeStruct((2 * (source.shape[1] - width), TILE // 2), f32),
         )
+    fetching = [] if swap else [pltpu.VMEM(source.shape, f32), pltpu.SemaphoreType.DMA]
     return pl.pallas_call(
         functools.partial(product_kernel, lane_blocks, sub_blocks, swap, sub_poly, lane_poly, scale, width),
         out_shape=out,
-        in_specs=[SMEM, SMEM, VMEM, VMEM],
+        in_specs=[SMEM, SMEM, VMEM, VMEM if swap else pl.BlockSpec(memory_space=pltpu.HBM)],
         out_specs=(VMEM, VMEM) if swap else VMEM,
-        scratch_shapes=[
+        scratch_shapes=fetching + [
             pltpu.VMEM((sub_blocks * TILE, TILE), i32),
             pltpu.VMEM((TILE, TILE), i32),
             pltpu.VMEM((TILE, TILE), i32),
@@ -149,7 +158,7 @@
             pltpu.VMEM((lane_blocks * sub_blocks, TILE), f32),
             pltpu.VMEM((2 * width, sub_blocks * TILE), bf16),
         ],
-        compiler_params=pltpu.CompilerParams(vmem_limit_bytes=24 << 20),
+        compiler_params=pltpu.CompilerParams(vmem_limit_bytes=(24 if swap else 60) << 20),
         cost_estimate=cost(8 << 30, 1 << 21),
     )(base, count, pairs, source)
 

time: 136 us -> 135 us (level)
  local copies, waits for them, and re-layouts: 2.74 us -> 1.03 us
    unnamed x8, local copies, waits for them, and re-layouts: 1.73 us -> 0.02 us
where the time goes in v10:
time: 135 us; the launch traced here: 134 us
  blocking collectives  41.3 us (31%)
  starting transfers between devices  39.1 us (29%)
  waiting for transfers between devices  31.8 us (24%)
  Pallas kernels  16.8 us (12%)
  other arithmetic  2.59 us (2%)
  between operations  1.44 us (1%)
    all_to_all x3, waiting for transfers between devices, exchange(): return lax.all_to_all(value, axes, 0, 0)  28.8 us
    all_to_all x3, starting transfers between devices, exchange(): return lax.all_to_all(value, axes, 0, 0)  22.9 us
    all_gather x1, blocking collectives, per_device(): lax.all_gather(jnp.concatenate([hidden, pack(weight), cotangent.T], axis=...  22.2 us
    pallas_call x2, Pallas kernels, edge_product(): pl.pallas_call(functools.partial(product_kernel, lane_blocks, sub_blocks,...  13.9 us
    all_gather x1, blocking collectives, per_device(): hidden_all = lax.all_gather(hidden_z, 'x', axis=0, tiled=True)  11 us
    ppermute x1, starting transfers between devices, per_device(): other = lax.ppermute(own, 'core', swap_core)  8.49 us
    all_to_all x1, blocking collectives, exchange(): return lax.all_to_all(value, axes, 0, 0)  8.03 us
    ppermute x1, starting transfers between devices, per_device(): feature_grad = column_part + lax.ppermute(column_part, 'core', swap_core)  5.48 us
  transfers between devices with their start and end apart: 6, of which 5 were waited for; matrix products, arithmetic and copies ran while one was open for 0% of the time, Pallas kernels for 0%

profile of v10, /device:TPU:1, one launch (start us, length us, event | category | flops | bytes accessed | tf_op | source)
XLA Modules:
  0.0 134.0 jit_solution(8473693679885945272)
XLA Ops:
  1.3 0.6 pad_add_fusion.1.base_ref
  1.9 7.5 %shard_map.76 = f32[16,64,128]{2,1,0:T(8,128)} custom-call(s32[2]{0:T(128)} %pad_add_fusion.1.base_ref, s32[1]{0:T(128)} %bitcast.11.count_ref, s32[2,256]{1,0:T(2,128)} %bitcast.16, f32[64,2048]{1,0:T(8,128)} %source_ref.1), custom_call_target="tpu_custom_call" | custom-call | flops 8589934592 | bytes 2097152 | tf_op jit(solution)/shard_map/pallas_call | solution.py:148
  9.4 9.2 %all-to-all-start = ((f32[16,64,128]{2,1,0:T(8,128)}), f32[16,64,128]{2,1,0:T(8,128)S(1)}, u32[]{:S(2)}, u32[]{:S(2)}) async-start(f32[16,64,128]{2,1,0:T(8,128)} %shard_map.76), calls=%async_computation | async-start | bytes 1048576 | tf_op jit(solution)/shard_map/all_to_all | solution.py:237
  18.7 13.6 %all-to-all-done = f32[16,64,128]{2,1,0:T(8,128)S(1)} async-done(((f32[16,64,128]{2,1,0:T(8,128)}), f32[16,64,128]{2,1,0:T(8,128)S(1)}, u32[]{:S(2)}, u32[]{:S(2)}) %all-to-all-start) | async-done | bytes 524320 | tf_op jit(solution)/shard_map/all_to_all | solution.py:237
  32.3 0.1 pad_maximum_fusion.1
  32.4 22.2 %all-gather = f32[576,128]{1,0:T(8,128)S(1)} all-gather(f32[144,128]{1,0:T(8,128)S(1)} %pad_maximum_fusion.1), channel_id=2, replica_groups=mesh['core'=2,'zl'=4,'y'=4,'x'=4,'zh'=4] {'zh'}, dimensions={0}, use_global_device_ids=true | all-gather | bytes 368640 | tf_op jit(solution)/shard_map/all_gather | solution.py:260
  54.6 0.8 broadcast_in_dim.14
  55.5 6.2 %all-to-all-start.1 = ((f32[16,64,128]{2,1,0:T(8,128)}), f32[16,64,128]{2,1,0:T(8,128)S(1)}, u32[]{:S(2)}, u32[]{:S(2)}) async-start(f32[16,64,128]{2,1,0:T(8,128)} %broadcast_in_dim.14), calls=%async_computation.1 | async-start | bytes 1048576 | tf_op jit(solution)/shard_map/all_to_all | solution.py:237
  61.7 11.0 %all_gather.11.hidden_ref = f32[1024,128]{1,0:T(8,128)S(1)} all-gather(f32[256,128]{1,0:T(8,128)S(1)} %bitcast.18), channel_id=1, replica_groups=mesh['core'=2,'zl'=4,'y'=4,'x'=4,'zh'=4] {'x'}, dimensions={0}, use_global_device_ids=true | all-gather | bytes 655360 | tf_op jit(solution)/shard_map/all_gather | solution.py:264
  72.7 0.2 all-to-all-done.1.own_ref
  73.0 8.5 %collective-permute-start = (f32[16,64,128]{2,1,0:T(8,128)S(1)}, f32[16,64,128]{2,1,0:T(8,128)S(1)}, u32[]{:S(2)}, u32[]{:S(2)}) collective-permute-start(f32[16,64,128]{2,1,0:T(8,128)S(1)} %all-to-all-done.1.own_ref), channel_id=1, source_target_pairs={{0,256},{256,0},{1,257},{257,1},{2,258},{258,2},{3,259},{259,3},{4... | collective-permute-start | bytes 1572872 | tf_op jit(solution)/shard_map/ppermute | solution.py:266
  81.5 0.1 pad_add_fusion.at_ref
  81.5 1.4 %collective-permute-done.other_ref = f32[16,64,128]{2,1,0:T(8,128)S(1)} collective-permute-done((f32[16,64,128]{2,1,0:T(8,128)S(1)}, f32[16,64,128]{2,1,0:T(8,128)S(1)}, u32[]{:S(2)}, u32[]{:S(2)}) %collective-permute-start) | collective-permute-done | bytes 524320 | tf_op jit(solution)/shard_map/ppermute | solution.py:266
  83.0 2.8 %shard_map.77 = (f32[64,128]{1,0:T(8,128)}, f32[4,64,128]{2,1,0:T(8,128)S(1)}, f32[16,16,128]{2,1,0:T(8,128)S(1)}, f32[16,16,128]{2,1,0:T(8,128)S(1)}) custom-call(s32[2]{0:T(128)S(1)} %pad_add_fusion.at_ref, f32[1024,128]{1,0:T(8,128)S(1)} %all_gather.11.hidden_ref, f32[16,64,128]{2,1,0:T(8,128)S(1)} %all-to-all-done.1.own_ref, ...), custom_call_target="tpu_custom_call" | custom-call | flops 1073741824 | bytes 2097152 | tf_op jit(solution)/shard_map/pallas_call | solution.py:217
  85.8 2.3 %collective-permute-start.1 = (f32[16,16,128]{2,1,0:T(8,128)S(1)}, f32[16,16,128]{2,1,0:T(8,128)S(1)}, u32[]{:S(2)}, u32[]{:S(2)}) collective-permute-start(f32[16,16,128]{2,1,0:T(8,128)S(1)} %get-tuple-element.16), channel_id=1, source_target_pairs={{0,256},{256,0},{1,257},{257,1},{2,258},{258,2},{3,259},{259,3},{4... | collective-permute-start | bytes 393224 | tf_op jit(solution)/shard_map/ppermute | solution.py:272
  88.1 8.0 %all_to_all.20 = f32[4,64,128]{2,1,0:T(8,128)S(1)} all-to-all(f32[4,64,128]{2,1,0:T(8,128)S(1)} %get-tuple-element.14), channel_id=1, replica_groups=mesh['core'=2,'zl'=4,'y'=4,'x'=4,'zh'=4] {'x'}, dimensions={0} | all-to-all | bytes 262144 | tf_op jit(solution)/shard_map/all_to_all | solution.py:237
  96.2 0.9 pad_maximum_fusion
  97.1 7.5 %all-to-all-start.3 = ((f32[16,80,128]{2,1,0:T(8,128)}), f32[16,80,128]{2,1,0:T(8,128)S(1)}, u32[]{:S(2)}, u32[]{:S(2)}) async-start(f32[16,80,128]{2,1,0:T(8,128)} %pad_maximum_fusion), calls=%async_computation.3 | async-start | bytes 1310720 | tf_op jit(solution)/shard_map/all_to_all | solution.py:237
  104.6 0.1 rev.3.base_ref
  104.7 15.0 %all-to-all-done.3.source_ref = f32[16,80,128]{2,1,0:T(8,128)S(1)} async-done(((f32[16,80,128]{2,1,0:T(8,128)}), f32[16,80,128]{2,1,0:T(8,128)S(1)}, u32[]{:S(2)}, u32[]{:S(2)}) %all-to-all-start.3) | async-done | bytes 655392 | tf_op jit(solution)/shard_map/all_to_all | solution.py:237
  119.7 6.4 %shard_map.78 = (f32[64,2048]{1,0:T(8,128)S(1)}, f32[32,64]{1,0:T(8,128)}) custom-call(s32[2]{0:T(128)S(1)} %rev.3.base_ref, s32[1]{0:T(128)} %bitcast.12.count_ref, s32[2,256]{1,0:T(2,128)S(1)} %bitcast.17, f32[16,80,128]{2,1,0:T(8,128)S(1)} %all-to-all-done.3.source_ref), custom_call_target="tpu_custom_call" | custom-call | flops 8589934592 | bytes 2097152 | tf_op jit(solution)/shard_map/pallas_call | solution.py:148
  126.1 5.5 %collective-permute-start.2 = (f32[64,2048]{1,0:T(8,128)S(1)}, f32[64,2048]{1,0:T(8,128)S(1)}, u32[]{:S(2)}, u32[]{:S(2)}) collective-permute-start(f32[64,2048]{1,0:T(8,128)S(1)} %get-tuple-element.17), channel_id=1, source_target_pairs={{0,256},{256,0},{1,257},{257,1},{2,258},{258,2},{3,259},{259,3},{4... | collective-permute-start | bytes 1572872 | tf_op jit(solution)/shard_map/ppermute | solution.py:279
  131.6 1.5 %collective-permute-done.2 = f32[64,2048]{1,0:T(8,128)S(1)} collective-permute-done((f32[64,2048]{1,0:T(8,128)S(1)}, f32[64,2048]{1,0:T(8,128)S(1)}, u32[]{:S(2)}, u32[]{:S(2)}) %collective-permute-start.2) | collective-permute-done | bytes 524320 | tf_op jit(solution)/shard_map/ppermute | solution.py:279
  133.1 0.9 add.11
  (16 shorter events, 0.1 us)
Async XLA Ops:
  9.4 9.2 %copy-start.2 = (f32[32,64]{1,0:T(8,128)S(1)}, f32[32,64]{1,0:T(8,128)}, u32[]{:S(2)}) copy-start(f32[32,64]{1,0:T(8,128)} %param.8) | copy-start | bytes 24580
  9.4 22.8 %all-to-all-start = ((f32[16,64,128]{2,1,0:T(8,128)}), f32[16,64,128]{2,1,0:T(8,128)S(1)}, u32[]{:S(2)}, u32[]{:S(2)}) async-start(f32[16,64,128]{2,1,0:T(8,128)} %shard_map.76), calls=%async_computation | async-start | bytes 1048576 | tf_op jit(solution)/shard_map/all_to_all | solution.py:237
  18.7 13.6 %copy-start.1 = (f32[128,64]{0,1:T(8,128)S(1)}, f32[128,64]{0,1:T(8,128)}, u32[]{:S(2)}) copy-start(f32[128,64]{0,1:T(8,128)} %param.9) | copy-start | bytes 98308
  55.5 17.5 %all-to-all-start.1 = ((f32[16,64,128]{2,1,0:T(8,128)}), f32[16,64,128]{2,1,0:T(8,128)S(1)}, u32[]{:S(2)}, u32[]{:S(2)}) async-start(f32[16,64,128]{2,1,0:T(8,128)} %broadcast_in_dim.14), calls=%async_computation.1 | async-start | bytes 1048576 | tf_op jit(solution)/shard_map/all_to_all | solution.py:237
  73.0 10.0 %collective-permute-start = (f32[16,64,128]{2,1,0:T(8,128)S(1)}, f32[16,64,128]{2,1,0:T(8,128)S(1)}, u32[]{:S(2)}, u32[]{:S(2)}) collective-permute-start(f32[16,64,128]{2,1,0:T(8,128)S(1)} %all-to-all-done.1.own_ref), channel_id=1, source_target_pairs={{0,256},{256,0},{1,257},{257,1},{2,258},{258,2},{3,259},{259,3},{4... | collective-permute-start | bytes 1572872 | tf_op jit(solution)/shard_map/ppermute | solution.py:266
  85.8 10.3 %collective-permute-start.1 = (f32[16,16,128]{2,1,0:T(8,128)S(1)}, f32[16,16,128]{2,1,0:T(8,128)S(1)}, u32[]{:S(2)}, u32[]{:S(2)}) collective-permute-start(f32[16,16,128]{2,1,0:T(8,128)S(1)} %get-tuple-element.16), channel_id=1, source_target_pairs={{0,256},{256,0},{1,257},{257,1},{2,258},{258,2},{3,259},{259,3},{4... | collective-permute-start | bytes 393224 | tf_op jit(solution)/shard_map/ppermute | solution.py:272
  97.1 7.5 %copy-start.3 = (s32[2]{0:T(128)S(1)}, s32[2]{0:T(128)}, u32[]{:S(2)}) copy-start(s32[2]{0:T(128)} %pad_add_fusion.1.base_ref) | copy-start | bytes 28
  97.1 22.6 %all-to-all-start.3 = ((f32[16,80,128]{2,1,0:T(8,128)}), f32[16,80,128]{2,1,0:T(8,128)S(1)}, u32[]{:S(2)}, u32[]{:S(2)}) async-start(f32[16,80,128]{2,1,0:T(8,128)} %pad_maximum_fusion), calls=%async_computation.3 | async-start | bytes 1310720 | tf_op jit(solution)/shard_map/all_to_all | solution.py:237
  104.6 15.1 %copy-start = (s32[1,1,2,256]{3,2,1,0:T(2,128)S(1)}, s32[1,1,2,256]{3,2,1,0:T(2,128)}, u32[]{:S(2)}) copy-start(s32[1,1,2,256]{3,2,1,0:T(2,128)} %param.6) | copy-start | bytes 6148
  126.1 7.0 %collective-permute-start.2 = (f32[64,2048]{1,0:T(8,128)S(1)}, f32[64,2048]{1,0:T(8,128)S(1)}, u32[]{:S(2)}, u32[]{:S(2)}) collective-permute-start(f32[64,2048]{1,0:T(8,128)S(1)} %get-tuple-element.17), channel_id=1, source_target_pairs={{0,256},{256,0},{1,257},{257,1},{2,258},{258,2},{3,259},{259,3},{4... | collective-permute-start | bytes 1572872 | tf_op jit(solution)/shard_map/ppermute | solution.py:279
